TPU v7x, 512 devices: a whole 4x4x16 slice. The times are simulated.
512 devices in a mesh: ctx: 32 (over y, x, core), head: 16 (over z).
Axes of the slice: x: 4, y: 4, z: 16, core: 2. Of those that a mesh axis runs over, the one named last changes fastest.
Arguments:
- query: bfloat16 [4096, 12288], P('ctx', 'head'), may hold values from -128 to 128
- kv_row: bfloat16 [4096, 576], P('ctx'), may hold values from -64 to 64
- w_uk: bfloat16 [512, 8192], P(None, 'head'), may hold values from -0.25 to 0.25
- w_uv: bfloat16 [512, 8192], P(None, 'head'), may hold values from -0.25 to 0.25
- grad_out: bfloat16 [4096, 8192], P('ctx', 'head'), may hold values from -6 to 6
- block_start: int32 [64], replicated, may hold values from 0 to 4032, as said below
Outputs:
- grad_query: bfloat16 [4096, 12288], P('ctx', 'head')
- grad_kv_row: float32 [4096, 576], P('ctx')
- grad_w_uk: float32 [512, 8192], P('ctx', 'head')
- grad_w_uv: float32 [512, 8192], P('ctx', 'head')
Inputs may be any that keep to these rules, and one draw needn't show every extreme that they name: block_start is a permutation of the multiples of 64 below 4096, so every position occurs once.
All inputs are finite; a program needn't handle non-finite values.
Results may differ from a plain program's by a relative error of at most 0.02.
Values may be sent and summed in bfloat16 or wider, within the bound.
No kernel may reach another device: no remote copies, remote signals or barrier semaphores. Data moves between devices by JAX's collectives and lax.ppermute only.
A program may use at most 128 MiB of HBM per device.

v0:
```python
import math

import jax
import jax.numpy as jnp
from jax import lax
from jax.sharding import PartitionSpec as P

LATENT = 512
ROPE = 64
NOPE = 128
VDIM = 128


eps = 1e-06
masked_low = -1e30


def rms_rows(latent):
    values = latent.astype(jnp.float32)
    inverse = lax.rsqrt(jnp.mean(values * values, axis=-1, keepdims=True) + eps)
    return (values * inverse, inverse)


def norm_back(x_hat, inverse, gradient):
    return inverse * (gradient - x_hat * jnp.mean(gradient * x_hat, axis=-1, keepdims=True))


def score_rows(q_nope, q_rope, k_nope, k_rope, scale):
    first = jnp.einsum("thd,khd->htk", q_nope, k_nope, preferred_element_type=jnp.float32)
    second = jnp.einsum("thr,kr->htk", q_rope, k_rope, preferred_element_type=jnp.float32)
    return (first + second) * scale


def local(query, kv_row, w_uk, w_uv, grad_out, block_start):
    tok_rows = query.shape[0]
    total = tok_rows * lax.axis_size("ctx")
    half_rows = tok_rows // 2
    heads_here = w_uk.shape[1] // NOPE
    width_q = NOPE + ROPE
    scale = 1.0 / math.sqrt(width_q)
    block = min(512, total)
    key_width = heads_here * NOPE
    offsets = jnp.arange(half_rows, dtype=jnp.int32)
    all_pos = (block_start[:, None] + offsets[None, :]).reshape(-1)
    my_pos = lax.dynamic_slice_in_dim(all_pos, lax.axis_index("ctx") * tok_rows, tok_rows)
    order = jnp.argsort(all_pos)
    query3 = query.reshape(tok_rows, heads_here, width_q)
    q_nope = query3[:, :, :NOPE]
    q_rope = query3[:, :, NOPE:]
    grad3 = grad_out.reshape(tok_rows, heads_here, VDIM)
    latent_all = lax.all_gather(kv_row, "ctx", axis=0, tiled=True)
    steps_keys = jnp.max(my_pos) // block + 1

    def expand(index, buffers):
        key_buf, value_buf = buffers
        picks = lax.dynamic_slice_in_dim(order, index * block, block)
        rows = jnp.take(latent_all, picks, axis=0)
        normed = rms_rows(rows[:, :LATENT])[0].astype(jnp.bfloat16)
        keys = jnp.dot(normed, w_uk, preferred_element_type=jnp.float32).astype(jnp.bfloat16)
        values = jnp.dot(normed, w_uv, preferred_element_type=jnp.float32).astype(jnp.bfloat16)
        key_buf = lax.dynamic_update_slice_in_dim(
            key_buf, jnp.concatenate([keys, rows[:, LATENT:]], axis=1), index * block, 0
        )
        value_buf = lax.dynamic_update_slice_in_dim(value_buf, values, index * block, 0)
        return (key_buf, value_buf)

    key_buf = jnp.zeros((total, key_width + ROPE), jnp.bfloat16)
    value_buf = jnp.zeros((total, heads_here * VDIM), jnp.bfloat16)
    key_buf, value_buf = lax.fori_loop(0, steps_keys, expand, (key_buf, value_buf))

    def key_block(index):
        both = lax.dynamic_slice_in_dim(key_buf, index * block, block)
        k_nope = both[:, :key_width].reshape(block, heads_here, NOPE)
        k_rope = both[:, key_width:]
        values = lax.dynamic_slice_in_dim(value_buf, index * block, block).reshape(
            block, heads_here, VDIM
        )
        key_pos = index * block + jnp.arange(block, dtype=jnp.int32)
        visible = key_pos[None, None, :] <= my_pos[None, :, None]
        return (k_nope, k_rope, values, visible)

    def gather_stats(index, carry):
        top, weight_sum, weighted = carry
        k_nope, k_rope, values, visible = key_block(index)
        scores = score_rows(q_nope, q_rope, k_nope, k_rope, scale)
        slopes = jnp.einsum("thd,khd->htk", grad3, values, preferred_element_type=jnp.float32)
        fresh = jnp.maximum(top, jnp.max(jnp.where(visible, scores, masked_low), axis=-1))
        fade = jnp.exp(top - fresh)
        weights = jnp.where(visible, jnp.exp(scores - fresh[..., None]), 0.0)
        weight_sum = weight_sum * fade + jnp.sum(weights, axis=-1)
        weighted = weighted * fade + jnp.sum(weights * slopes, axis=-1)
        return (fresh, weight_sum, weighted)

    zero_rows = jnp.zeros((heads_here, tok_rows), jnp.float32)
    start_stats = (jnp.full((heads_here, tok_rows), masked_low, jnp.float32), zero_rows, zero_rows)
    top, weight_sum, weighted = lax.fori_loop(0, steps_keys, gather_stats, start_stats)
    log_total = top + jnp.log(weight_sum)
    average = weighted / weight_sum

    def query_grads(index, carry):
        grad_nope, grad_rope = carry
        k_nope, k_rope, values, visible = key_block(index)
        scores = score_rows(q_nope, q_rope, k_nope, k_rope, scale)
        slopes = jnp.einsum("thd,khd->htk", grad3, values, preferred_element_type=jnp.float32)
        probs = jnp.where(visible, jnp.exp(scores - log_total[..., None]), 0.0)
        score_grad = (probs * (slopes - average[..., None]) * scale).astype(jnp.bfloat16)
        grad_nope = grad_nope + jnp.einsum(
            "htk,khd->thd", score_grad, k_nope, preferred_element_type=jnp.float32
        )
        grad_rope = grad_rope + jnp.einsum(
            "htk,kr->thr", score_grad, k_rope, preferred_element_type=jnp.float32
        )
        return (grad_nope, grad_rope)

    start_grads = (
        jnp.zeros((tok_rows, heads_here, NOPE), jnp.float32),
        jnp.zeros((tok_rows, heads_here, ROPE), jnp.float32),
    )
    grad_nope, grad_rope = lax.fori_loop(0, steps_keys, query_grads, start_grads)
    grad_query = (
        jnp.concatenate([grad_nope, grad_rope], axis=-1)
        .astype(jnp.bfloat16)
        .reshape(tok_rows, heads_here * width_q)
    )
    stats = jnp.concatenate([log_total.T, average.T], axis=1)
    all_stats = lax.all_gather(stats, "ctx", axis=0, tiled=True)
    x_hat, inverse = rms_rows(kv_row[:, :LATENT])
    normed_own = x_hat.astype(jnp.bfloat16)
    own_nope = (
        jnp.dot(normed_own, w_uk, preferred_element_type=jnp.float32)
        .astype(jnp.bfloat16)
        .reshape(tok_rows, heads_here, NOPE)
    )
    own_values = (
        jnp.dot(normed_own, w_uv, preferred_element_type=jnp.float32)
        .astype(jnp.bfloat16)
        .reshape(tok_rows, heads_here, VDIM)
    )
    own_rope = kv_row[:, LATENT:]
    first_key = jnp.min(my_pos)

    def piece_terms(carry, q_piece, g_piece, piece_pos, piece_stats):
        key_grad, rope_grad, value_grad = carry
        rows = q_piece.shape[0]
        q_three = q_piece.reshape(rows, heads_here, width_q)
        g_three = g_piece.reshape(rows, heads_here, VDIM)
        scores = score_rows(q_three[:, :, :NOPE], q_three[:, :, NOPE:], own_nope, own_rope, scale)
        slopes = jnp.einsum("thd,khd->htk", g_three, own_values, preferred_element_type=jnp.float32)
        visible = my_pos[None, None, :] <= piece_pos[None, :, None]
        piece_total = piece_stats[:, :heads_here].T
        piece_average = piece_stats[:, heads_here:].T
        probs = jnp.where(visible, jnp.exp(scores - piece_total[..., None]), 0.0)
        score_grad = (probs * (slopes - piece_average[..., None]) * scale).astype(jnp.bfloat16)
        key_grad = key_grad + jnp.einsum(
            "htk,thd->khd", score_grad, q_three[:, :, :NOPE], preferred_element_type=jnp.float32
        )
        rope_grad = rope_grad + jnp.einsum(
            "htk,thr->kr", score_grad, q_three[:, :, NOPE:], preferred_element_type=jnp.float32
        )
        value_grad = value_grad + jnp.einsum(
            "htk,thd->khd", probs.astype(jnp.bfloat16), g_three, preferred_element_type=jnp.float32
        )
        return (key_grad, rope_grad, value_grad)

    def keep_carry(carry, q_piece, g_piece, piece_pos, piece_stats):
        return carry

    def guarded(carry, q_piece, g_piece, piece_pos, piece_stats):
        return lax.cond(
            jnp.max(piece_pos) >= first_key,
            piece_terms,
            keep_carry,
            carry,
            q_piece,
            g_piece,
            piece_pos,
            piece_stats,
        )

    start_keys = (
        jnp.zeros((tok_rows, heads_here, NOPE), jnp.float32),
        jnp.zeros((tok_rows, ROPE), jnp.float32),
        jnp.zeros((tok_rows, heads_here, VDIM), jnp.float32),
    )
    q_piece = lax.all_gather(query, "ctx", axis=0, tiled=True)
    g_piece = lax.all_gather(grad_out, "ctx", axis=0, tiled=True)
    rows = q_piece.shape[0]
    piece_pos = all_pos
    piece_stats = all_stats

    def sub_step(index, inner):
        first_row = index * block
        return guarded(
            inner,
            lax.dynamic_slice_in_dim(q_piece, first_row, block),
            lax.dynamic_slice_in_dim(g_piece, first_row, block),
            lax.dynamic_slice_in_dim(piece_pos, first_row, block),
            lax.dynamic_slice_in_dim(piece_stats, first_row, block),
        )

    key_grad, rope_grad, value_grad = lax.fori_loop(0, rows // block, sub_step, start_keys)
    key_flat = key_grad.reshape(tok_rows, key_width).astype(jnp.bfloat16)
    value_flat = value_grad.reshape(tok_rows, heads_here * VDIM).astype(jnp.bfloat16)
    latent_grad = jnp.einsum(
        "tf,lf->tl", key_flat, w_uk, preferred_element_type=jnp.float32
    ) + jnp.einsum("tf,lf->tl", value_flat, w_uv, preferred_element_type=jnp.float32)
    key_terms = jnp.einsum("tl,tf->lf", normed_own, key_flat, preferred_element_type=jnp.float32)
    value_terms = jnp.einsum(
        "tl,tf->lf", normed_own, value_flat, preferred_element_type=jnp.float32
    )
    grad_w_uk, grad_w_uv = (
        lax.psum_scatter(
            key_terms.astype(jnp.bfloat16), "ctx", scatter_dimension=0, tiled=True
        ).astype(jnp.float32),
        lax.psum_scatter(
            value_terms.astype(jnp.bfloat16), "ctx", scatter_dimension=0, tiled=True
        ).astype(jnp.float32),
    )
    summed_latent, summed_rope = (
        lax.psum(latent_grad.astype(jnp.bfloat16), "head").astype(jnp.float32),
        lax.psum(rope_grad.astype(jnp.bfloat16), "head").astype(jnp.float32),
    )
    grad_kv_row = jnp.concatenate([norm_back(x_hat, inverse, summed_latent), summed_rope], axis=1)
    return (grad_query, grad_kv_row, grad_w_uk, grad_w_uv)


def solution(mesh):
    placed = (
        P("ctx", "head"),
        P("ctx", None),
        P(None, "head"),
        P(None, "head"),
        P("ctx", "head"),
        P(),
    )
    return jax.shard_map(
        local,
        mesh=mesh,
        in_specs=placed,
        out_specs=(P("ctx", "head"), P("ctx", None), P("ctx", "head"), P("ctx", "head")),
        check_vma=False,
    )
```

profile of v0, /device:TPU:6, one launch (start us, length us, event | category | flops | bytes accessed | tf_op | source)
XLA Modules:
  0.0 626.9 jit_solution(9421776580001384816)
XLA Ops:
  7.2 1.7 copy.73
  9.0 1.6 copy.75
  10.7 1.7 copy.74
  20.2 5.8 sort.17
  27.2 1.4 fusion.38
  28.6 1.4 fusion.37
  30.0 48.5 %all-gather.4.cloned.1.call-done = bf16[4096,576]{1,0:T(8,128)(2,1)} async-done(((bf16[128,576]{1,0:T(8,128)(2,1)}), bf16[4096,576]{1,0:T(8,128)(2,1)}) %all-gather.4.cloned.1.call-update) | async-done | bytes 4718608 | tf_op jit(solution)/shard_map/all_gather | solution.py:51
  78.5 2.7 broadcast_in_dim.90
  81.2 2.5 broadcast_in_dim.91.clone
  83.7 53.1 %while.55 = (s32[]{:T(128)}, bf16[4096,576]{0,1:T(8,128)(2,1)}, bf16[4096,512]{0,1:T(8,128)(2,1)}, s32[]{:T(128)}, s32[4096]{0:T(1024)S(1)}, /*index=5*/bf16[409...) while((s32[]{:T(128)}, bf16[4096,576]{0,1:T(8,128)(2,1)}, ...), condition=%wide.region_4.5_spmd, body=%wide.region_2.4_spmd.sunk | while | flops 541233664 | bytes 10640567 | solution.py:69
  83.8 5.3 gather_fusion
  92.7 5.3 gather_fusion
  101.5 5.3 gather_fusion
  110.4 5.3 gather_fusion
  119.2 5.3 gather_fusion
  128.1 5.3 gather_fusion
  136.8 22.2 %while.56 = (s32[]{:T(128)}, f32[4,128]{1,0:T(4,128)S(1)}, f32[4,128]{1,0:T(4,128)S(1)}, f32[4,128]{1,0:T(4,128)S(1)}, s32[]{:T(128)}, /*index=5*/s32[128]{0:T(1...) while((s32[]{:T(128)}, f32[4,128]{1,0:T(4,128)S(1)}, ...), condition=%wide.region_9.10_spmd, body=%wide.region_5.9_spmd.sunk | while | flops 170723328 | bytes 9085671 | solution.py:96
  136.8 1.3 constant_dynamic-slice_fusion.8
  138.6 1.2 select_reduce_fusion.2
  140.6 1.3 constant_dynamic-slice_fusion.8
  142.3 1.2 select_reduce_fusion.2
  144.3 1.3 constant_dynamic-slice_fusion.8
  146.1 1.2 select_reduce_fusion.2
  148.0 1.3 constant_dynamic-slice_fusion.8
  149.8 1.2 select_reduce_fusion.2
  151.7 1.3 constant_dynamic-slice_fusion.8
  153.5 1.2 select_reduce_fusion.2
  155.4 1.3 constant_dynamic-slice_fusion.8
  157.2 1.2 select_reduce_fusion.2
  159.1 47.4 %all_gather.14 = f32[4096,8]{0,1:T(8,128)S(1)} all-gather(f32[128,8]{0,1:T(8,128)S(1)} %pad_maximum_fusion.2), channel_id=1, replica_groups=mesh['ctx'=32,'head'=16] {'ctx'}, dimensions={0}, use_global_device_ids=true | all-gather | bytes 135168 | tf_op jit(solution)/shard_map/all_gather | solution.py:126
  206.5 12.0 %all-gather.6.cloned.1.call-done = bf16[4096,768]{0,1:T(8,128)(2,1)} async-done(((bf16[128,768]{0,1:T(8,128)(2,1)}), bf16[4096,768]{0,1:T(8,128)(2,1)}) %all-gather.6.cloned.1.call-update) | async-done | bytes 6291472 | tf_op jit(solution)/shard_map/all_gather | solution.py:185
  218.6 50.7 %while.58 = (s32[]{:T(128)}, f32[128,4,128]{2,0,1:T(8,128)S(1)}, f32[128,64]{0,1:T(8,128)S(1)}, f32[128,4,128]{2,0,1:T(8,128)S(1)}, s32[4096]{0:T(1024)S(1)}, /*...) while((s32[]{:T(128)}, f32[128,4,128]{2,0,1:T(8,128)S(1)}, ...), condition=%wide.region_18.19_spmd, body=%wide.region_14.18_spmd.sunk | while | flops 338108928 | bytes 13638557 | solution.py:201
  220.5 5.0 conditional.2
  220.5 1.2 constant_dynamic-slice_fusion.5
  227.5 5.0 conditional.2
  227.5 1.2 constant_dynamic-slice_fusion.5
  234.4 5.0 conditional.2
  243.3 5.0 conditional.2
  250.3 5.0 conditional.2
  257.3 5.0 conditional.2
  257.3 1.2 constant_dynamic-slice_fusion.5
  264.2 5.0 conditional.2
  269.4 1.3 fusion.51
  270.9 2.0 fusion.36
  273.0 1.2 convolution_convert_fusion.3
  274.3 28.9 %while.57 = (s32[]{:T(128)}, f32[128,4,128]{0,2,1:T(8,128)S(1)}, f32[128,4,64]{0,2,1:T(8,128)S(1)}, s32[]{:T(128)}, bf16[4096,576]{0,1:T(8,128)(2,1)}, /*index=5...) while((s32[]{:T(128)}, f32[128,4,128]{0,2,1:T(8,128)S(1)}, ...), condition=%wide.region_11.12_spmd, body=%wide.region_10.11_spmd.sunk | while | flops 270696960 | bytes 10822391 | solution.py:119
  274.3 1.3 constant_dynamic-slice_fusion.9
  276.1 1.3 fusion.126
  279.1 1.3 constant_dynamic-slice_fusion.9
  280.9 1.3 fusion.126
  283.9 1.3 constant_dynamic-slice_fusion.9
  285.7 1.3 fusion.126
  288.7 1.3 constant_dynamic-slice_fusion.9
  290.5 1.3 fusion.126
  293.6 1.3 constant_dynamic-slice_fusion.9
  295.3 1.3 fusion.126
  298.4 1.3 constant_dynamic-slice_fusion.9
  300.2 1.3 fusion.126
  305.3 56.8 %psum.15 = bf16[128,64]{0,1:T(8,128)(2,1)S(1)} all-reduce(bf16[128,64]{0,1:T(8,128)(2,1)S(1)} %convert_element_type.96), channel_id=1, replica_groups=mesh['ctx'=32,'head'=16] {'head'}, use_global_device_ids=true, to_apply=%region_21.22 | all-reduce | flops 8192 | bytes 32768 | tf_op jit(solution)/shard_map/psum | solution.py:221
  362.2 50.6 %all-reduce.2.cloned.1.call-done = bf16[128,512]{1,0:T(8,128)(2,1)} async-done(((bf16[128,512]{1,0:T(8,128)(2,1)}), bf16[128,512]{1,0:T(8,128)(2,1)}) %all-reduce.2.cloned.1.call-update) | async-done | bytes 131088 | tf_op jit(solution)/shard_map/psum | solution.py:220
  415.9 98.5 %reduce-scatter.3.cloned.1.call-done = bf16[16,512]{1,0:T(8,128)(2,1)} async-done(((bf16[512,512]{1,0:T(8,128)(2,1)}), bf16[16,512]{1,0:T(8,128)(2,1)}) %reduce-scatter.3.cloned.1.call-update) | async-done | bytes 16400 | tf_op jit(solution)/shard_map/reduce_scatter | solution.py:212
  514.4 1.3 convert_element_type.99
  515.7 103.0 %reduce-scatter.5.cloned.1.call-done = bf16[16,512]{1,0:T(8,128)(2,1)} async-done(((bf16[512,512]{1,0:T(8,128)(2,1)}), bf16[16,512]{1,0:T(8,128)(2,1)}) %reduce-scatter.5.cloned.1.call-update) | async-done | bytes 16400 | tf_op jit(solution)/shard_map/reduce_scatter | solution.py:215
  618.7 1.3 convert_element_type.101
  (287 shorter events, 90.1 us)
Async XLA Ops:
  7.2 71.3 %all-gather.4.cloned.1.call-start = ((), (), s32[]{:S(2)}) async-start(), calls=%async_computation.2 | async-start | bytes 5406720 | tf_op jit(solution)/shard_map/all_gather | solution.py:51
  8.9 197.6 %all-gather.8.cloned.1.call-start = ((), (), s32[]{:S(2)}) async-start(), calls=%async_computation.4 | async-start | bytes 4325376 | tf_op jit(solution)/shard_map/all_gather | solution.py:186
  10.7 207.8 %all-gather.6.cloned.1.call-start = ((), (), s32[]{:S(2)}) async-start(), calls=%async_computation.3 | async-start | bytes 6488064 | tf_op jit(solution)/shard_map/all_gather | solution.py:185
  12.5 400.3 %all-reduce.2.cloned.1.call-start = ((), (), s32[]{:S(2)}) async-start(), calls=%async_computation.5 | async-start | bytes 262144 | tf_op jit(solution)/shard_map/psum | solution.py:220
  29.9 53.8 %copy-start.1 = (bf16[512,512]{1,0:T(8,128)(2,1)S(1)}, bf16[512,512]{1,0:T(8,128)(2,1)}, u32[]{:S(2)}) copy-start(bf16[512,512]{1,0:T(8,128)(2,1)} %param.18) | copy-start | bytes 1572868
  30.0 53.8 %copy-start.2 = (bf16[512,512]{1,0:T(8,128)(2,1)S(1)}, bf16[512,512]{1,0:T(8,128)(2,1)}, u32[]{:S(2)}) copy-start(bf16[512,512]{1,0:T(8,128)(2,1)} %param.19) | copy-start | bytes 1572868
  218.6 54.4 %copy-start = (bf16[128,576]{1,0:T(8,128)(2,1)S(1)}, bf16[128,576]{1,0:T(8,128)(2,1)}, u32[]{:S(2)}) copy-start(bf16[128,576]{1,0:T(8,128)(2,1)} %copy.73) | copy-start | bytes 442372
  272.9 241.4 %reduce-scatter.3.cloned.1.call-start = ((), (), s32[]{:S(2)}) async-start(), calls=%async_computation.6 | async-start | bytes 540672 | tf_op jit(solution)/shard_map/reduce_scatter | solution.py:212
  274.2 344.5 %reduce-scatter.5.cloned.1.call-start = ((), (), s32[]{:S(2)}) async-start(), calls=%async_computation.7 | async-start | bytes 540672 | tf_op jit(solution)/shard_map/reduce_scatter | solution.py:215
Sparse Core Ops, SparseCore 0:
  11.7 66.7 all-gather.3
  81.6 63.8 all-gather.7
  149.1 69.4 all-gather.5
  273.0 139.7 all-reduce.1
  417.6 96.7 reduce-scatter.2
  519.1 99.4 reduce-scatter.4
where the time goes:
time: 630 us; the launch traced here: 627 us
  waiting for transfers between devices  313 us (50%)
  blocking collectives  104 us (17%)
  local copies, waits for them, and re-layouts  87.9 us (14%)
  matrix products  63.4 us (10%)
  other arithmetic  30 us (5%)
  between operations  17 us (3%)
  loops' own time  11.5 us (2%)
    reduce_scatter x1, waiting for transfers between devices, local(): lax.psum_scatter(value_terms.astype(jnp.bfloat16), 'ctx', scatter_dimensi...  103 us
    reduce_scatter x1, waiting for transfers between devices, local(): lax.psum_scatter(key_terms.astype(jnp.bfloat16), 'ctx', scatter_dimension...  98.5 us
    psum x1, blocking collectives, local(): lax.psum(rope_grad.astype(jnp.bfloat16), 'head').astype(jnp.float32)  56.8 us
    psum x1, waiting for transfers between devices, local(): lax.psum(latent_grad.astype(jnp.bfloat16), 'head').astype(jnp.float32)  50.6 us
    all_gather x1, waiting for transfers between devices, local(): latent_all = lax.all_gather(kv_row, 'ctx', axis=0, tiled=True)  48.5 us
    all_gather x1, blocking collectives, local(): all_stats = lax.all_gather(stats, 'ctx', axis=0, tiled=True)  47.4 us
    gather x12, local copies, waits for them, and re-layouts, expand(): rows = jnp.take(latent_all, picks, axis=0)  33.2 us
    dot_general x19, matrix products, score_rows(): jnp.einsum('thr,kr->htk', q_rope, k_rope, preferred_element_type=jnp.floa...  17 us
  transfers between devices with their start and end apart: 6, of which 5 were waited for; matrix products, arithmetic and copies ran while one was open for 21% of the time, Pallas kernels for 0%

commit v1 on v0

v1 whole, which is shorter than its diff:
```python
import functools
import math

import jax
import jax.numpy as jnp
from jax import lax
from jax.experimental import pallas as pl
from jax.experimental.pallas import tpu as pltpu
from jax.sharding import PartitionSpec as P

LATENT = 512
ROPE = 64
NOPE = 128
VDIM = 128
WIDTH_Q = NOPE + ROPE
HALF = 64
HEADS = 4
CHIPS = 16
SIDE = 4
PIECE = HALF // SIDE
ROWS = 2 * HALF
KEYS = 4096
QUERIES = 2 * CHIPS * PIECE
KEY_ROWS = 2 * ROWS + HALF
IN_ROWS = KEY_ROWS + 5 * PIECE
OUT_ROWS = KEY_ROWS + 3 * PIECE
CHUNK = 512
GROUP = 256
N_CHUNKS = KEYS // CHUNK
N_GROUPS = QUERIES // GROUP
Z_WIDTH = 640
LOG2E = 1.4426950408889634
SCALE = 1.0 / math.sqrt(WIDTH_Q)

eps = 1e-06
masked_low = -1e30
bf16 = jnp.bfloat16
f32 = jnp.float32
VMEM = pl.BlockSpec(memory_space=pltpu.VMEM)
SMEM = pl.BlockSpec(memory_space=pltpu.SMEM)


def dot(left, right, left_dim=1, right_dim=0):
    return lax.dot_general(
        left, right, (((left_dim,), (right_dim,)), ((), ())), preferred_element_type=f32
    )


def rms_rows(latent):
    values = latent.astype(f32)
    inverse = lax.rsqrt(jnp.mean(values * values, axis=-1, keepdims=True) + eps)
    return (values * inverse, inverse)


def expand_kernel(kv_ref, wk_ref, wv_ref, q_ref, g_ref, out_ref):
    normed = rms_rows(kv_ref[:, :LATENT])[0].astype(bf16)
    keys = dot(normed, wk_ref[...]).astype(bf16)
    values = dot(normed, wv_ref[...]).astype(bf16)
    rope = kv_ref[:, LATENT:]
    rope = jnp.concatenate([rope[:HALF], rope[HALF:]], axis=1)
    for x in range(HEADS):
        key = keys[:, x * NOPE : (x + 1) * NOPE]
        value = values[:, x * VDIM : (x + 1) * VDIM]
        q_nope = q_ref[:, x * WIDTH_Q : x * WIDTH_Q + NOPE]
        q_rope = q_ref[:, x * WIDTH_Q + NOPE : (x + 1) * WIDTH_Q]
        grad = g_ref[:, x * VDIM : (x + 1) * VDIM]
        for y in range(SIDE):
            slot = y * SIDE + x
            out_ref[slot, 0:ROWS] = key
            out_ref[slot, ROWS : 2 * ROWS] = value
            out_ref[slot, 2 * ROWS : KEY_ROWS] = rope
            first = slice(y * PIECE, (y + 1) * PIECE)
            second = slice(HALF + y * PIECE, HALF + (y + 1) * PIECE)
            low = KEY_ROWS
            out_ref[slot, low : low + PIECE] = q_nope[first]
            out_ref[slot, low + PIECE : low + 2 * PIECE] = q_nope[second]
            out_ref[slot, low + 2 * PIECE : low + 3 * PIECE] = grad[first]
            out_ref[slot, low + 3 * PIECE : low + 4 * PIECE] = grad[second]
            out_ref[slot, low + 4 * PIECE : low + 5 * PIECE] = jnp.concatenate(
                [q_rope[first], q_rope[second]], axis=1
            )


def attention_kernel(
    own_starts,
    other_starts,
    rank,
    group_chunks,
    qpos_ref,
    own_ref,
    other_ref,
    own_out,
    other_out,
    keys,
    values,
    queries,
    grads,
    scores,
    slopes,
    key_grads,
    value_grads,
    query_grads,
    key_sum,
    value_sum,
):
    pad = jnp.zeros((HALF, HALF), bf16)
    pad_piece = jnp.zeros((PIECE, HALF), bf16)

    def place(chip, carry):
        for starts, ref in ((own_starts, own_ref), (other_starts, other_ref)):
            rope = ref[chip, 2 * ROWS : KEY_ROWS]
            for half in range(2):
                at = pl.ds(pl.multiple_of(starts[2 * chip + half], HALF), HALF)
                keys[at, 0:NOPE] = ref[chip, half * HALF : (half + 1) * HALF]
                keys[at, NOPE : 2 * NOPE] = jnp.concatenate(
                    [rope[:, half * HALF : (half + 1) * HALF], pad], axis=1
                )
                values[at, :] = ref[chip, ROWS + half * HALF : ROWS + (half + 1) * HALF]
        low = KEY_ROWS
        q_rope = own_ref[chip, low + 4 * PIECE : low + 5 * PIECE]
        for half in range(2):
            at = pl.ds(pl.multiple_of(rank[2 * chip + half] * PIECE, PIECE), PIECE)
            queries[at, 0:NOPE] = own_ref[chip, low + half * PIECE : low + (half + 1) * PIECE]
            queries[at, NOPE : 2 * NOPE] = jnp.concatenate(
                [q_rope[:, half * HALF : (half + 1) * HALF], pad_piece], axis=1
            )
            grads[at, :] = own_ref[chip, low + (2 + half) * PIECE : low + (3 + half) * PIECE]
        return carry

    lax.fori_loop(0, CHIPS, place, 0)

    log_totals = []
    averages = []
    for group in range(N_GROUPS):
        lanes = slice(group * GROUP, (group + 1) * GROUP)
        q_group = queries[lanes, :]
        g_group = grads[lanes, :]
        q_pos = qpos_ref[0:1, lanes]

        def gather_stats(index, carry):
            top, weight_sum, weighted = carry
            at = pl.ds(pl.multiple_of(index * CHUNK, CHUNK), CHUNK)
            score = dot(keys[at, :], q_group, 1, 1) * (SCALE * LOG2E)
            k_pos = index * CHUNK + lax.broadcasted_iota(jnp.int32, (CHUNK, GROUP), 0)
            score = jnp.where(k_pos <= q_pos, score, masked_low)
            slope = dot(values[at, :], g_group, 1, 1)
            scores[at, lanes] = score
            slopes[at, lanes] = slope
            fresh = jnp.maximum(top, jnp.max(score, axis=0, keepdims=True))
            fade = jnp.exp2(top - fresh)
            weight = jnp.exp2(score - fresh)
            weight_sum = weight_sum * fade + jnp.sum(weight, axis=0, keepdims=True)
            weighted = weighted * fade + jnp.sum(weight * slope, axis=0, keepdims=True)
            return (fresh, weight_sum, weighted)

        zero = jnp.zeros((1, GROUP), f32)
        top, weight_sum, weighted = lax.fori_loop(
            0,
            group_chunks[group],
            gather_stats,
            (jnp.full((1, GROUP), masked_low, f32), zero, zero),
        )
        log_totals.append(top + jnp.log2(weight_sum))
        averages.append(weighted / weight_sum)

    query_grads[...] = jnp.zeros_like(query_grads)

    def gradients(index, carry):
        at = pl.ds(pl.multiple_of(index * CHUNK, CHUNK), CHUNK)
        key_sum[...] = jnp.zeros_like(key_sum)
        value_sum[...] = jnp.zeros_like(value_sum)
        for group in range(N_GROUPS):
            lanes = slice(group * GROUP, (group + 1) * GROUP)

            @pl.when(index < group_chunks[group])
            def _(lanes=lanes, group=group):
                probs = jnp.exp2(scores[at, lanes] - log_totals[group])
                score_grad = (probs * ((slopes[at, lanes] - averages[group]) * SCALE)).astype(bf16)
                value_sum[...] += dot(probs.astype(bf16), grads[lanes, :])
                key_sum[...] += dot(score_grad, queries[lanes, :])
                query_grads[lanes, :] += dot(score_grad, keys[at, :], 0, 0)

        key_grads[at, :] = key_sum[...].astype(bf16)
        value_grads[at, :] = value_sum[...].astype(bf16)
        return carry

    lax.fori_loop(0, N_CHUNKS, gradients, 0)

    def hand_out(chip, carry):
        low = KEY_ROWS
        for starts, ref in ((own_starts, own_out), (other_starts, other_out)):
            ropes = []
            for half in range(2):
                at = pl.ds(pl.multiple_of(starts[2 * chip + half], HALF), HALF)
                ref[chip, half * HALF : (half + 1) * HALF] = key_grads[at, 0:NOPE]
                ref[chip, ROWS + half * HALF : ROWS + (half + 1) * HALF] = value_grads[at, :]
                ropes.append(key_grads[at, NOPE:WIDTH_Q])
            ref[chip, 2 * ROWS : KEY_ROWS] = jnp.concatenate(ropes, axis=1)
        ropes = []
        for half in range(2):
            at = pl.ds(pl.multiple_of(rank[2 * chip + half] * PIECE, PIECE), PIECE)
            piece = query_grads[at, :].astype(bf16)
            own_out[chip, low + half * PIECE : low + (half + 1) * PIECE] = piece[:, 0:NOPE]
            ropes.append(piece[:, NOPE:WIDTH_Q])
        own_out[chip, low + 2 * PIECE : low + 3 * PIECE] = jnp.concatenate(ropes, axis=1)
        other_out[chip, low : low + 3 * PIECE] = jnp.zeros((3 * PIECE, NOPE), bf16)
        return carry

    lax.fori_loop(0, CHIPS, hand_out, 0)


def head_sums(slots_ref, low):
    parts = []
    for x in range(HEADS):
        total = slots_ref[x, low : low + ROWS].astype(f32)
        for y in range(1, SIDE):
            total = total + slots_ref[y * SIDE + x, low : low + ROWS].astype(f32)
        parts.append(total.astype(bf16))
    return jnp.concatenate(parts, axis=1)


def latent_kernel(slots_ref, wk_ref, wv_ref, out_ref):
    key_flat = head_sums(slots_ref, 0)
    value_flat = head_sums(slots_ref, ROWS)
    latent = dot(key_flat, wk_ref[...], 1, 1) + dot(value_flat, wv_ref[...], 1, 1)
    out_ref[:, :LATENT] = latent.astype(bf16)
    rope = slots_ref[0, 2 * ROWS : KEY_ROWS].astype(f32)
    for slot in range(1, CHIPS):
        rope = rope + slots_ref[slot, 2 * ROWS : KEY_ROWS].astype(f32)
    rope = jnp.concatenate([rope[:, :HALF], rope[:, HALF:]], axis=0)
    out_ref[:, LATENT:] = jnp.concatenate([rope, jnp.zeros_like(rope)], axis=1).astype(bf16)


def projection_kernel(core_ref, slots_ref, kv_ref, grad_q_ref, own_ref, other_ref, terms):
    normed = rms_rows(kv_ref[:, :LATENT])[0].astype(bf16)
    width = HEADS * NOPE
    terms[:, :width] = dot(normed, head_sums(slots_ref, 0), 0, 0).astype(bf16)
    terms[:, width:] = dot(normed, head_sums(slots_ref, ROWS), 0, 0).astype(bf16)
    rows = LATENT // (2 * CHIPS)
    core = core_ref[0]
    for chip in range(CHIPS):
        first = pl.multiple_of((2 * chip + core) * rows, rows)
        second = pl.multiple_of((2 * chip + 1 - core) * rows, rows)
        own_ref[chip] = terms[pl.ds(first, rows), :]
        other_ref[chip] = terms[pl.ds(second, rows), :]
    low = KEY_ROWS
    for y in range(SIDE):
        for half in range(2):
            parts = []
            for x in range(HEADS):
                slot = y * SIDE + x
                parts.append(slots_ref[slot, low + half * PIECE : low + (half + 1) * PIECE])
                rope = slots_ref[slot, low + 2 * PIECE : low + 3 * PIECE]
                parts.append(rope[:, half * HALF : (half + 1) * HALF])
            first = half * HALF + y * PIECE
            grad_q_ref[first : first + PIECE, :] = jnp.concatenate(parts, axis=1)


def norm_kernel(slots_ref, kv_ref, out_ref):
    total = jnp.sum(slots_ref[...].astype(f32), axis=0)
    x_hat, inverse = rms_rows(kv_ref[:, :LATENT])
    latent = total[:, :LATENT]
    latent = inverse * (latent - x_hat * jnp.mean(latent * x_hat, axis=-1, keepdims=True))
    row = jnp.concatenate([latent, total[:, LATENT:]], axis=1).astype(bf16)
    out_ref[...] = jnp.broadcast_to(row[None], out_ref.shape)


def call(kernel, shapes, specs, scratch=(), limit=32, flops=0, moved=0):
    shapes = [jax.ShapeDtypeStruct(*shape) for shape in shapes]
    single = len(shapes) == 1
    return pl.pallas_call(
        kernel,
        out_shape=shapes[0] if single else shapes,
        in_specs=specs,
        out_specs=VMEM if single else [VMEM] * len(shapes),
        scratch_shapes=scratch,
        compiler_params=pltpu.CompilerParams(vmem_limit_bytes=limit * 2**20),
        cost_estimate=pl.CostEstimate(flops=flops, bytes_accessed=moved, transcendentals=0),
    )


def local(query, kv_row, w_uk, w_uv, grad_out, block_start):
    ctx = lax.axis_index("ctx")
    chip, core = ctx // 2, ctx % 2
    z_size = lax.axis_size("head")
    z_rows = ROWS // z_size
    planes = [[2 * m + c for m in range(CHIPS)] for c in range(2)]
    swap = [(i, i ^ 1) for i in range(2 * CHIPS)]

    def over_chips(slots):
        return lax.all_to_all(slots, "ctx", 0, 0, axis_index_groups=planes)

    slots = call(expand_kernel, [((CHIPS, IN_ROWS, NOPE), bf16)], [VMEM] * 5)(
        kv_row, w_uk, w_uv, query, grad_out
    )
    own = over_chips(slots)
    other = lax.ppermute(own, "ctx", swap)

    starts = block_start.reshape(CHIPS, 2, 2)
    own_starts = lax.dynamic_index_in_dim(starts, core, 1, False).reshape(2 * CHIPS)
    other_starts = lax.dynamic_index_in_dim(starts, 1 - core, 1, False).reshape(2 * CHIPS)
    rank = jnp.sum((own_starts[None, :] < own_starts[:, None]).astype(jnp.int32), axis=1)
    places = jnp.arange(2 * CHIPS, dtype=jnp.int32)
    in_order = jnp.sum(jnp.where(rank[None, :] == places[:, None], own_starts[None, :], 0), axis=1)
    offset = (chip // SIDE) * PIECE
    q_pos = in_order[:, None] + offset + jnp.arange(PIECE, dtype=jnp.int32)[None, :]
    q_pos = jnp.broadcast_to(q_pos.reshape(1, QUERIES), (8, QUERIES))
    last = in_order.reshape(N_GROUPS, -1)[:, -1] + offset + PIECE - 1
    group_chunks = last // CHUNK + 1

    own_part, other_part = call(
        attention_kernel,
        [((CHIPS, OUT_ROWS, NOPE), bf16)] * 2,
        [SMEM] * 4 + [VMEM] * 3,
        [
            pltpu.VMEM((KEYS, 2 * NOPE), bf16),
            pltpu.VMEM((KEYS, VDIM), bf16),
            pltpu.VMEM((QUERIES, 2 * NOPE), bf16),
            pltpu.VMEM((QUERIES, VDIM), bf16),
            pltpu.VMEM((KEYS, QUERIES), f32),
            pltpu.VMEM((KEYS, QUERIES), f32),
            pltpu.VMEM((KEYS, 2 * NOPE), bf16),
            pltpu.VMEM((KEYS, VDIM), bf16),
            pltpu.VMEM((QUERIES, 2 * NOPE), f32),
            pltpu.VMEM((CHUNK, 2 * NOPE), f32),
            pltpu.VMEM((CHUNK, VDIM), f32),
        ],
        limit=48,
    )(own_starts, other_starts, rank, group_chunks, q_pos, own, other)
    summed = own_part + lax.ppermute(other_part, "ctx", swap)
    slots = over_chips(summed)

    z_part = call(latent_kernel, [((ROWS, Z_WIDTH), bf16)], [VMEM] * 3)(slots, w_uk, w_uv)
    z_part = z_part.reshape(z_size, z_rows, Z_WIDTH)
    z_slots = lax.all_to_all(z_part, "head", 0, 0)

    w_rows = LATENT // (2 * CHIPS)
    w_width = 2 * HEADS * NOPE
    grad_query, own_terms, other_terms = call(
        projection_kernel,
        [((ROWS, HEADS * WIDTH_Q), bf16)] + [((CHIPS, w_rows, w_width), bf16)] * 2,
        [SMEM] + [VMEM] * 2,
        [pltpu.VMEM((LATENT, w_width), bf16)],
        flops=2 * 128 * 512 * 1024,
        moved=8 * 2**20,
    )(core.reshape(1), slots, kv_row)
    own_terms = own_terms + lax.ppermute(other_terms, "ctx", swap)

    first_row = lax.axis_index("head") * z_rows
    kv_rows = lax.dynamic_slice_in_dim(kv_row, first_row, z_rows)
    rows = call(norm_kernel, [((z_size, z_rows, Z_WIDTH), bf16)], [VMEM] * 2)(z_slots, kv_rows)
    all_rows = lax.all_to_all(rows, "head", 0, 0).reshape(ROWS, Z_WIDTH)
    grad_kv_row = all_rows[:, : LATENT + ROPE].astype(f32)

    terms = jnp.sum(over_chips(own_terms).astype(f32), axis=0)
    half = HEADS * NOPE
    return (grad_query, grad_kv_row, terms[:, :half], terms[:, half:])


def solution(mesh):
    placed = (
        P("ctx", "head"),
        P("ctx", None),
        P(None, "head"),
        P(None, "head"),
        P("ctx", "head"),
        P(),
    )
    return jax.shard_map(
        local,
        mesh=mesh,
        in_specs=placed,
        out_specs=(P("ctx", "head"), P("ctx", None), P("ctx", "head"), P("ctx", "head")),
        check_vma=False,
    )
```

time: 630 us -> 156 us (0.25)
  the two profiles are of different devices: /device:TPU:6 before, /device:TPU:2 now
where the time goes in v1:
time: 156 us; the launch traced here: 155 us
  blocking collectives  55.6 us (36%)
  waiting for transfers between devices  38 us (24%)
  starting transfers between devices  31.7 us (20%)
  Pallas kernels  18.5 us (12%)
  local copies, waits for them, and re-layouts  7.45 us (5%)
  other arithmetic  2.77 us (2%)
    all_to_all x2, blocking collectives, over_chips(): return lax.all_to_all(slots, 'ctx', 0, 0, axis_index_groups=planes)  55.6 us
    pallas_call x1, Pallas kernels, local(): call(attention_kernel, [((CHIPS, OUT_ROWS, NOPE), bf16)] * 2, [SMEM] * 4...  14.9 us
    all_to_all x1, starting transfers between devices, local(): z_slots = lax.all_to_all(z_part, 'head', 0, 0)  14.9 us
    all_to_all x1, waiting for transfers between devices, local(): all_rows = lax.all_to_all(rows, 'head', 0, 0).reshape(ROWS, Z_WIDTH)  14 us
    all_to_all x1, waiting for transfers between devices, local(): z_slots = lax.all_to_all(z_part, 'head', 0, 0)  8.84 us
    all_to_all x1, waiting for transfers between devices, over_chips(): return lax.all_to_all(slots, 'ctx', 0, 0, axis_index_groups=planes)  8.01 us
    unnamed x18, local copies, waits for them, and re-layouts  6.3 us
    all_to_all x1, starting transfers between devices, local(): all_rows = lax.all_to_all(rows, 'head', 0, 0).reshape(ROWS, Z_WIDTH)  5.26 us
  transfers between devices with their start and end apart: 6, of which 6 were waited for; matrix products, arithmetic and copies ran while one was open for 2% of the time, Pallas kernels for 1%

profile of v1, /device:TPU:2, one launch (start us, length us, event | category | flops | bytes accessed | tf_op | source)
XLA Modules:
  0.0 154.8 jit_solution(6008429117150292174)
XLA Ops:
  0.6 1.1 copy.18.kv_ref
  1.7 0.0 copy-start
  1.7 1.0 copy-done
  2.7 0.0 copy-start.2
  2.7 1.0 copy-done.2
  3.8 0.0 copy-start.4
  3.8 0.9 copy-done.4
  4.7 0.0 copy-start.5
  4.7 0.9 copy-done.5
  5.6 0.4 shard_map.93
  6.0 0.0 copy-start.7
  6.0 29.7 %all_to_all.25.own_ref = bf16[16,400,128]{2,1,0:T(8,128)(2,1)S(1)} all-to-all(bf16[16,400,128]{2,1,0:T(8,128)(2,1)S(1)} %shard_map.93), channel_id=1, replica_groups={{0,32,64,96,128,160,192,224,256,288,320,352,384,416,448,480},{16,48,80,..., dimensions={0} | all-to-all | bytes 3276800 | tf_op jit(solution)/shard_map/all_to_all | solution.py:291
  35.7 1.9 %collective-permute-start = (bf16[16,400,128]{2,1,0:T(8,128)(2,1)S(1)}, bf16[16,400,128]{2,1,0:T(8,128)(2,1)S(1)}, u32[]{:S(2)}, u32[]{:S(2)}) collective-permute-start(bf16[16,400,128]{2,1,0:T(8,128)(2,1)S(1)} %all_to_all.25.own_ref), channel_id=1, source_target_pairs={{0,16},{16,0},{32,48},{48,32},{64,80},{80,64},{96,112},{112,96},{1... | collective-permute-start | bytes 4915208 | tf_op jit(solution)/shard_map/ppermute | solution.py:297
  37.6 0.0 copy-done.7
  37.6 0.1 reshape.60
  37.8 0.1 dynamic-slice_reduce_fusion
  37.8 0.1 reshape.61.own_starts
  37.9 0.2 convert_reduce_fusion.1.rank
  38.1 0.1 select_reduce_fusion
  38.2 0.1 reshape.63
  38.3 0.1 iota_add_fusion
  38.4 0.1 add.81
  38.5 0.1 reshape.62.other_starts
  38.6 0.2 add_reduce_fusion
  38.8 2.3 %collective-permute-done.other_ref = bf16[16,400,128]{2,1,0:T(8,128)(2,1)S(1)} collective-permute-done((bf16[16,400,128]{2,1,0:T(8,128)(2,1)S(1)}, bf16[16,400,128]{2,1,0:T(8,128)(2,1)S(1)}, u32[]{:S(2)}, u32[]{:S(2)}) %collective-permute-start) | collective-permute-done | bytes 1638432 | tf_op jit(solution)/shard_map/ppermute | solution.py:297
  41.1 0.0 copy-start.6
  41.1 1.2 copy-done.6
  42.2 14.9 %shard_map.94 = (bf16[16,368,128]{2,1,0:T(8,128)(2,1)S(1)}, bf16[16,368,128]{2,1,0:T(8,128)(2,1)S(1)}) custom-call(s32[32]{0:T(128)S(1)} %reshape.61.own_starts, s32[32]{0:T(128)S(1)} %reshape.62.other_starts, s32[32]{0:T(128)S(1)} %convert_reduce_fusion.1.rank, s32[2]{0:T(128)S(1)} %fusion.group_chunks, s32[8,512]{1,0:T(8,128)S(1)} %broadcast_in_dim.13.qpos_ref, ...), custom_call_target="tpu_custom_call" | custom-call | tf_op jit(solution)/shard_map/pallas_call | solution.py:311
  57.1 2.9 %collective-permute-start.1 = (bf16[16,368,128]{2,1,0:T(8,128)(2,1)S(1)}, bf16[16,368,128]{2,1,0:T(8,128)(2,1)S(1)}, u32[]{:S(2)}, u32[]{:S(2)}) collective-permute-start(bf16[16,368,128]{2,1,0:T(8,128)(2,1)S(1)} %get-tuple-element.10), channel_id=1, source_target_pairs={{0,16},{16,0},{32,48},{48,32},{64,80},{80,64},{96,112},{112,96},{1... | collective-permute-start | bytes 4521992 | tf_op jit(solution)/shard_map/ppermute | solution.py:330
  60.0 2.9 %collective-permute-done.1 = bf16[16,368,128]{2,1,0:T(8,128)(2,1)S(1)} collective-permute-done((bf16[16,368,128]{2,1,0:T(8,128)(2,1)S(1)}, bf16[16,368,128]{2,1,0:T(8,128)(2,1)S(1)}, u32[]{:S(2)}, u32[]{:S(2)}) %collective-permute-start.1) | collective-permute-done | bytes 1507360 | tf_op jit(solution)/shard_map/ppermute | solution.py:330
  63.0 0.4 add.82
  63.4 0.0 copy-start.1
  63.4 0.0 copy-start.3
  63.4 25.9 %all_to_all.26.slots_ref = bf16[16,368,128]{2,1,0:T(8,128)(2,1)S(1)} all-to-all(bf16[16,368,128]{2,1,0:T(8,128)(2,1)S(1)} %add.82), channel_id=1, replica_groups={{0,32,64,96,128,160,192,224,256,288,320,352,384,416,448,480},{16,48,80,..., dimensions={0} | all-to-all | bytes 3014656 | tf_op jit(solution)/shard_map/all_to_all | solution.py:291
  89.3 0.0 copy-done.1
  89.3 0.0 copy-done.3
  89.3 1.1 shard_map.96
  90.5 14.9 %all-to-all-start.2 = ((bf16[16,8,640]{2,1,0:T(8,128)(2,1)}), bf16[16,8,640]{2,1,0:T(8,128)(2,1)S(1)}, u32[]{:S(2)}, u32[]{:S(2)}) async-start(bf16[16,8,640]{2,1,0:T(8,128)(2,1)} %bitcast.1), calls=%async_computation.2 | async-start | bytes 327680 | tf_op jit(solution)/shard_map/all_to_all | solution.py:335
  105.4 1.2 shard_map.95
  106.6 1.9 %collective-permute-start.2 = (bf16[16,16,1024]{2,1,0:T(8,128)(2,1)S(1)}, bf16[16,16,1024]{2,1,0:T(8,128)(2,1)S(1)}, u32[]{:S(2)}, u32[]{:S(2)}) collective-permute-start(bf16[16,16,1024]{2,1,0:T(8,128)(2,1)S(1)} %get-tuple-element.13), channel_id=1, source_target_pairs={{0,16},{16,0},{32,48},{48,32},{64,80},{80,64},{96,112},{112,96},{1... | collective-permute-start | bytes 1572872 | tf_op jit(solution)/shard_map/ppermute | solution.py:347
  108.5 1.9 %collective-permute-done.2 = bf16[16,16,1024]{2,1,0:T(8,128)(2,1)S(1)} collective-permute-done((bf16[16,16,1024]{2,1,0:T(8,128)(2,1)S(1)}, bf16[16,16,1024]{2,1,0:T(8,128)(2,1)S(1)}, u32[]{:S(2)}, u32[]{:S(2)}) %collective-permute-start.2) | collective-permute-done | bytes 524320 | tf_op jit(solution)/shard_map/ppermute | solution.py:347
  110.4 1.0 add.84
  111.4 8.8 %all-to-all-done.2.slots_ref = bf16[16,8,640]{2,1,0:T(8,128)(2,1)S(1)} async-done(((bf16[16,8,640]{2,1,0:T(8,128)(2,1)}), bf16[16,8,640]{2,1,0:T(8,128)(2,1)S(1)}, u32[]{:S(2)}, u32[]{:S(2)}) %all-to-all-start.2) | async-done | bytes 163872 | tf_op jit(solution)/shard_map/all_to_all | solution.py:335
  120.2 4.8 %all-to-all-start.4 = ((bf16[16,16,1024]{2,1,0:T(8,128)(2,1)}), bf16[16,16,1024]{2,1,0:T(8,128)(2,1)S(1)}, u32[]{:S(2)}, u32[]{:S(2)}) async-start(bf16[16,16,1024]{2,1,0:T(8,128)(2,1)} %add.84), calls=%async_computation.4 | async-start | bytes 1048576 | tf_op jit(solution)/shard_map/all_to_all | solution.py:291
  125.0 0.8 shard_map.97
  125.9 8.0 %all-to-all-done.4 = bf16[16,16,1024]{2,1,0:T(8,128)(2,1)S(1)} async-done(((bf16[16,16,1024]{2,1,0:T(8,128)(2,1)}), bf16[16,16,1024]{2,1,0:T(8,128)(2,1)S(1)}, u32[]{:S(2)}, u32[]{:S(2)}) %all-to-all-start.4) | async-done | bytes 524320 | tf_op jit(solution)/shard_map/all_to_all | solution.py:291
  133.9 5.3 %all-to-all-start.3 = ((bf16[16,8,640]{2,1,0:T(8,128)(2,1)}), bf16[16,8,640]{2,1,0:T(8,128)(2,1)S(1)}, u32[]{:S(2)}, u32[]{:S(2)}) async-start(bf16[16,8,640]{2,1,0:T(8,128)(2,1)} %shard_map.97), calls=%async_computation.3 | async-start | bytes 327680 | tf_op jit(solution)/shard_map/all_to_all | solution.py:352
  139.2 0.1 convert_reduce_fusion
  139.3 0.6 fusion.1
  139.9 14.0 %all-to-all-done.3 = bf16[16,8,640]{2,1,0:T(8,128)(2,1)S(1)} async-done(((bf16[16,8,640]{2,1,0:T(8,128)(2,1)}), bf16[16,8,640]{2,1,0:T(8,128)(2,1)S(1)}, u32[]{:S(2)}, u32[]{:S(2)}) %all-to-all-start.3) | async-done | bytes 163872 | tf_op jit(solution)/shard_map/all_to_all | solution.py:352
  153.9 0.1 copy.22
  154.1 0.7 convert_element_type.10
  (4 shorter events, 0.0 us)
Async XLA Ops:
  1.7 1.0 copy-start
  2.7 1.0 copy-start.2
  3.8 0.9 copy-start.4
  4.7 0.9 copy-start.5
  6.0 31.6 %copy-start.7 = (s32[64]{0:T(128)S(1)}, s32[64]{0:T(128)}, u32[]{:S(2)}) copy-start(s32[64]{0:T(128)} %param.11) | copy-start | bytes 772
  35.7 5.4 %collective-permute-start = (bf16[16,400,128]{2,1,0:T(8,128)(2,1)S(1)}, bf16[16,400,128]{2,1,0:T(8,128)(2,1)S(1)}, u32[]{:S(2)}, u32[]{:S(2)}) collective-permute-start(bf16[16,400,128]{2,1,0:T(8,128)(2,1)S(1)} %all_to_all.25.own_ref), channel_id=1, source_target_pairs={{0,16},{16,0},{32,48},{48,32},{64,80},{80,64},{96,112},{112,96},{1... | collective-permute-start | bytes 4915208 | tf_op jit(solution)/shard_map/ppermute | solution.py:297
  41.1 1.2 copy-start.6
  57.1 5.8 %collective-permute-start.1 = (bf16[16,368,128]{2,1,0:T(8,128)(2,1)S(1)}, bf16[16,368,128]{2,1,0:T(8,128)(2,1)S(1)}, u32[]{:S(2)}, u32[]{:S(2)}) collective-permute-start(bf16[16,368,128]{2,1,0:T(8,128)(2,1)S(1)} %get-tuple-element.10), channel_id=1, source_target_pairs={{0,16},{16,0},{32,48},{48,32},{64,80},{80,64},{96,112},{112,96},{1... | collective-permute-start | bytes 4521992 | tf_op jit(solution)/shard_map/ppermute | solution.py:330
  63.4 26.0 %copy-start.1 = (bf16[512,512]{1,0:T(8,128)(2,1)S(1)}, bf16[512,512]{1,0:T(8,128)(2,1)}, u32[]{:S(2)}) copy-start(bf16[512,512]{1,0:T(8,128)(2,1)} %wk_ref.3) | copy-start | bytes 1572868
  63.4 26.0 %copy-start.3 = (bf16[512,512]{1,0:T(8,128)(2,1)S(1)}, bf16[512,512]{1,0:T(8,128)(2,1)}, u32[]{:S(2)}) copy-start(bf16[512,512]{1,0:T(8,128)(2,1)} %wv_ref.3) | copy-start | bytes 1572868
  90.5 29.7 %all-to-all-start.2 = ((bf16[16,8,640]{2,1,0:T(8,128)(2,1)}), bf16[16,8,640]{2,1,0:T(8,128)(2,1)S(1)}, u32[]{:S(2)}, u32[]{:S(2)}) async-start(bf16[16,8,640]{2,1,0:T(8,128)(2,1)} %bitcast.1), calls=%async_computation.2 | async-start | bytes 327680 | tf_op jit(solution)/shard_map/all_to_all | solution.py:335
  106.6 3.8 %collective-permute-start.2 = (bf16[16,16,1024]{2,1,0:T(8,128)(2,1)S(1)}, bf16[16,16,1024]{2,1,0:T(8,128)(2,1)S(1)}, u32[]{:S(2)}, u32[]{:S(2)}) collective-permute-start(bf16[16,16,1024]{2,1,0:T(8,128)(2,1)S(1)} %get-tuple-element.13), channel_id=1, source_target_pairs={{0,16},{16,0},{32,48},{48,32},{64,80},{80,64},{96,112},{112,96},{1... | collective-permute-start | bytes 1572872 | tf_op jit(solution)/shard_map/ppermute | solution.py:347
  120.2 13.7 %all-to-all-start.4 = ((bf16[16,16,1024]{2,1,0:T(8,128)(2,1)}), bf16[16,16,1024]{2,1,0:T(8,128)(2,1)S(1)}, u32[]{:S(2)}, u32[]{:S(2)}) async-start(bf16[16,16,1024]{2,1,0:T(8,128)(2,1)} %add.84), calls=%async_computation.4 | async-start | bytes 1048576 | tf_op jit(solution)/shard_map/all_to_all | solution.py:291
  133.9 20.0 %all-to-all-start.3 = ((bf16[16,8,640]{2,1,0:T(8,128)(2,1)}), bf16[16,8,640]{2,1,0:T(8,128)(2,1)S(1)}, u32[]{:S(2)}, u32[]{:S(2)}) async-start(bf16[16,8,640]{2,1,0:T(8,128)(2,1)} %shard_map.97), calls=%async_computation.3 | async-start | bytes 327680 | tf_op jit(solution)/shard_map/all_to_all | solution.py:352

commit v2 on v1

v2 whole, which is shorter than its diff:
```python
import math

import jax
import jax.numpy as jnp
from jax import lax
from jax.experimental import pallas as pl
from jax.experimental.pallas import tpu as pltpu
from jax.sharding import Mesh
from jax.sharding import PartitionSpec as P

LATENT = 512
ROPE = 64
NOPE = 128
VDIM = 128
WIDTH_Q = NOPE + ROPE
HALF = 64
BLOCKS = 64
HEADS = 4
SIDE = 4
CHIPS = SIDE * SIDE
PIECE = HALF // 2
ROWS = 2 * HALF
KEYS = 2 * CHIPS * HALF
QUERIES = 2 * CHIPS * PIECE
KEY_ROWS = 2 * HALF + PIECE
IN_ROWS = KEY_ROWS + 5 * PIECE
OUT_ROWS = KEY_ROWS + 3 * PIECE
W_ROWS = LATENT // (2 * CHIPS)
W_WIDTH = HEADS * (NOPE + VDIM)
CHUNK = 512
GROUP = 512
N_CHUNKS = KEYS // CHUNK
N_GROUPS = QUERIES // GROUP
LISTED = 2 * CHIPS
KEY_RANK, QUERY_RANK, KEY_START, QUERY_START, SEEN = (i * LISTED for i in range(5))
SPARE = SEEN + N_GROUPS
META = SPARE + 8
Z_WIDTH = 640
LOG2E = 1.4426950408889634
SCALE = 1.0 / math.sqrt(WIDTH_Q)

eps = 1e-06
masked_low = -1e30
bf16 = jnp.bfloat16
f32 = jnp.float32
VMEM = pl.BlockSpec(memory_space=pltpu.VMEM)
SMEM = pl.BlockSpec(memory_space=pltpu.SMEM)
ANY = pl.BlockSpec(memory_space=pl.ANY)


def dot(left, right, left_dim=1, right_dim=0):
    return lax.dot_general(
        left, right, (((left_dim,), (right_dim,)), ((), ())), preferred_element_type=f32
    )


def rms_rows(latent):
    values = latent.astype(f32)
    inverse = lax.rsqrt(jnp.mean(values * values, axis=-1, keepdims=True) + eps)
    return (values * inverse, inverse)


def list_blocks(block_start, meta, holder):
    half = lax.axis_index("y") % 2
    core = lax.axis_index("core")

    def find(index, carry):
        holder[block_start[index] // HALF] = index
        return carry

    lax.fori_loop(0, BLOCKS, find, 0)

    def count(place, carry):
        n_keys, n_queries = carry
        index = holder[place]
        is_key = index % 2 == half
        is_query = (index // 2) % 2 == core
        meta[jnp.where(is_key, KEY_RANK + index // 2, SPARE)] = n_keys
        meta[jnp.where(is_key, KEY_START + n_keys, SPARE)] = place * HALF
        n_keys = n_keys + is_key.astype(jnp.int32)
        of_query = 2 * (index // 4) + index % 2
        meta[jnp.where(is_query, QUERY_RANK + of_query, SPARE)] = n_queries
        meta[jnp.where(is_query, QUERY_START + n_queries, SPARE)] = place * HALF
        meta[jnp.where(is_query, SEEN + n_queries // (GROUP // PIECE), SPARE)] = n_keys
        return (n_keys, n_queries + is_query.astype(jnp.int32))

    lax.fori_loop(0, BLOCKS, count, (0, 0))


def pack_kernel(
    block_start,
    kv_any,
    wk_any,
    wv_any,
    q_any,
    g_any,
    out_ref,
    meta,
    kv_ref,
    wk_ref,
    wv_ref,
    q_ref,
    g_ref,
    holder,
    sems,
):
    pairs = [(kv_any, kv_ref), (wk_any, wk_ref), (wv_any, wv_ref), (q_any, q_ref), (g_any, g_ref)]
    copies = [
        pltpu.make_async_copy(source, target, sems.at[index])
        for index, (source, target) in enumerate(pairs)
    ]
    for copy in copies:
        copy.start()
    list_blocks(block_start, meta, holder)
    for copy in copies:
        copy.wait()
    values = kv_ref[:LATENT, :].astype(f32)
    inverse = lax.rsqrt(jnp.mean(values * values, axis=0, keepdims=True) + eps)
    normed = (values * inverse).T.astype(bf16)
    rope = kv_ref[LATENT:, :].astype(f32).T.astype(bf16)
    keys = dot(normed, wk_ref[...]).astype(bf16)
    values = dot(normed, wv_ref[...]).astype(bf16)
    for x in range(HEADS):
        key = keys[:, x * NOPE : (x + 1) * NOPE]
        value = values[:, x * VDIM : (x + 1) * VDIM]
        q_nope = q_ref[:, x * WIDTH_Q : x * WIDTH_Q + NOPE]
        q_rope = q_ref[:, x * WIDTH_Q + NOPE : (x + 1) * WIDTH_Q]
        grad = g_ref[:, x * VDIM : (x + 1) * VDIM]
        for y in range(SIDE):
            slot = y * SIDE + x
            low = (y % 2) * HALF
            out_ref[slot, :HALF] = key[low : low + HALF]
            out_ref[slot, HALF : 2 * HALF] = value[low : low + HALF]
            out_ref[slot, 2 * HALF : KEY_ROWS] = jnp.concatenate(
                [rope[low : low + PIECE], rope[low + PIECE : low + HALF]], axis=1
            )
            first = slice((y // 2) * PIECE, (y // 2 + 1) * PIECE)
            second = slice(HALF + (y // 2) * PIECE, HALF + (y // 2 + 1) * PIECE)
            low = KEY_ROWS
            out_ref[slot, low : low + PIECE] = q_nope[first]
            out_ref[slot, low + PIECE : low + 2 * PIECE] = q_nope[second]
            out_ref[slot, low + 2 * PIECE : low + 3 * PIECE] = grad[first]
            out_ref[slot, low + 3 * PIECE : low + 4 * PIECE] = grad[second]
            out_ref[slot, low + 4 * PIECE : low + 5 * PIECE] = jnp.concatenate(
                [q_rope[first], q_rope[second]], axis=1
            )


def place_positions(meta, k_pos):
    rows = lax.broadcasted_iota(jnp.int32, (HALF, NOPE), 0)

    def body(rank, carry):
        at = pl.ds(pl.multiple_of(rank * HALF, HALF), HALF)
        k_pos[at, :] = rows + meta[KEY_START + rank]
        return carry

    lax.fori_loop(0, LISTED, body, 0)


def query_positions(meta, group):
    lane = lax.broadcasted_iota(jnp.int32, (1, GROUP), 1)
    count = GROUP // PIECE
    start = jnp.zeros((1, GROUP), jnp.int32)
    for piece in range(count):
        start = jnp.where(lane // PIECE == piece, meta[QUERY_START + group * count + piece], start)
    return start + (lax.axis_index("y") // 2) * PIECE + lane % PIECE


def seen_chunks(meta, group):
    return (meta[SEEN + group] * HALF + CHUNK - 1) // CHUNK


def stats_kernel(
    meta, own_ref, other_ref, keys, values, queries, grads, stats, k_pos
):
    core = lax.axis_index("core")
    pad_key = jnp.zeros((HALF, HALF), bf16)
    pad = jnp.zeros((PIECE, HALF), bf16)

    def place(chip, carry):
        for ref, side in ((own_ref, core), (other_ref, 1 - core)):
            rank = meta[KEY_RANK + 2 * chip + side]
            at = pl.ds(pl.multiple_of(rank * HALF, HALF), HALF)
            rope = ref[chip, 2 * HALF : KEY_ROWS]
            rope = jnp.concatenate([rope[:, :HALF], rope[:, HALF:]], axis=0)
            keys[at, :NOPE] = ref[chip, :HALF]
            keys[at, NOPE:] = jnp.concatenate([rope, pad_key], axis=1)
            values[at, :] = ref[chip, HALF : 2 * HALF]
        low = KEY_ROWS
        q_rope = own_ref[chip, low + 4 * PIECE : low + 5 * PIECE]
        for half in range(2):
            rank = meta[QUERY_RANK + 2 * chip + half]
            at = pl.ds(pl.multiple_of(rank * PIECE, PIECE), PIECE)
            queries[at, :NOPE] = own_ref[chip, low + half * PIECE : low + (half + 1) * PIECE]
            queries[at, NOPE:] = jnp.concatenate(
                [q_rope[:, half * HALF : (half + 1) * HALF], pad], axis=1
            )
            grads[at, :] = own_ref[chip, low + (2 + half) * PIECE : low + (3 + half) * PIECE]
        return carry

    lax.fori_loop(0, CHIPS, place, 0)
    place_positions(meta, k_pos)

    for group in range(N_GROUPS):
        lanes = slice(group * GROUP, (group + 1) * GROUP)
        q_group = queries[lanes, :]
        g_group = grads[lanes, :]
        q_pos = query_positions(meta, group)

        def gather_stats(index, carry):
            top, weight_sum, weighted = carry
            at = pl.ds(pl.multiple_of(index * CHUNK, CHUNK), CHUNK)
            score = dot(keys[at, :], q_group, 1, 1) * (SCALE * LOG2E)
            key_at = jnp.concatenate([k_pos[at, :]] * (GROUP // NOPE), axis=1)
            score = jnp.where(key_at <= q_pos, score, masked_low)
            slope = dot(values[at, :], g_group, 1, 1)
            fresh = jnp.maximum(top, jnp.max(score, axis=0, keepdims=True))
            fade = jnp.exp2(top - fresh)
            weight = jnp.exp2(score - fresh)
            weight_sum = weight_sum * fade + jnp.sum(weight, axis=0, keepdims=True)
            weighted = weighted * fade + jnp.sum(weight * slope, axis=0, keepdims=True)
            return (fresh, weight_sum, weighted)

        zero = jnp.zeros((1, GROUP), f32)
        top, weight_sum, weighted = lax.fori_loop(
            0,
            seen_chunks(meta, group),
            gather_stats,
            (jnp.full((1, GROUP), masked_low, f32), zero, zero),
        )
        stats[:, lanes] = jnp.concatenate(
            [top, weight_sum, weighted, jnp.zeros((5, GROUP), f32)], axis=0
        )


def gradient_kernel(
    meta,
    keys,
    values,
    queries,
    grads,
    own_stats,
    other_stats,
    own_out,
    other_out,
    k_pos,
    key_grads,
    value_grads,
    query_grads,
    key_sum,
    value_sum,
):
    place_positions(meta, k_pos)
    own_top = own_stats[0:1, :]
    other_top = other_stats[0:1, :]
    top = jnp.maximum(own_top, other_top)
    own_fade = jnp.exp2(own_top - top)
    other_fade = jnp.exp2(other_top - top)
    weight_sum = own_stats[1:2, :] * own_fade + other_stats[1:2, :] * other_fade
    weighted = own_stats[2:3, :] * own_fade + other_stats[2:3, :] * other_fade
    log_total = top + jnp.log2(weight_sum)
    average = weighted / weight_sum
    query_grads[...] = jnp.zeros_like(query_grads)
    positions = [query_positions(meta, group) for group in range(N_GROUPS)]

    def gradients(index, carry):
        at = pl.ds(pl.multiple_of(index * CHUNK, CHUNK), CHUNK)
        key_sum[...] = jnp.zeros_like(key_sum)
        value_sum[...] = jnp.zeros_like(value_sum)
        for group in range(N_GROUPS):
            lanes = slice(group * GROUP, (group + 1) * GROUP)

            @pl.when(index < seen_chunks(meta, group))
            def _(lanes=lanes, q_pos=positions[group]):
                score = dot(keys[at, :], queries[lanes, :], 1, 1) * (SCALE * LOG2E)
                key_at = jnp.concatenate([k_pos[at, :]] * (GROUP // NOPE), axis=1)
                score = jnp.where(key_at <= q_pos, score - log_total[:, lanes], masked_low)
                slope = dot(values[at, :], grads[lanes, :], 1, 1)
                probs = jnp.exp2(score)
                score_grad = (probs * ((slope - average[:, lanes]) * SCALE)).astype(bf16)
                value_sum[...] += dot(probs.astype(bf16), grads[lanes, :])
                key_sum[...] += dot(score_grad, queries[lanes, :])
                query_grads[lanes, :] += dot(score_grad, keys[at, :], 0, 0)

        key_grads[at, :] = key_sum[...].astype(bf16)
        value_grads[at, :] = value_sum[...].astype(bf16)
        return carry

    lax.fori_loop(0, N_CHUNKS, gradients, 0)
    core = lax.axis_index("core")

    def hand_out(chip, carry):
        for ref, side in ((own_out, core), (other_out, 1 - core)):
            rank = meta[KEY_RANK + 2 * chip + side]
            at = pl.ds(pl.multiple_of(rank * HALF, HALF), HALF)
            ref[chip, :HALF] = key_grads[at, :NOPE]
            ref[chip, HALF : 2 * HALF] = value_grads[at, :]
            rope = key_grads[at, NOPE:WIDTH_Q]
            ref[chip, 2 * HALF : KEY_ROWS] = jnp.concatenate([rope[:PIECE], rope[PIECE:]], axis=1)
        low = KEY_ROWS
        ropes = []
        for half in range(2):
            rank = meta[QUERY_RANK + 2 * chip + half]
            at = pl.ds(pl.multiple_of(rank * PIECE, PIECE), PIECE)
            piece = query_grads[at, :].astype(bf16)
            own_out[chip, low + half * PIECE : low + (half + 1) * PIECE] = piece[:, :NOPE]
            ropes.append(piece[:, NOPE:WIDTH_Q])
        own_out[chip, low + 2 * PIECE : low + 3 * PIECE] = jnp.concatenate(ropes, axis=1)
        return carry

    lax.fori_loop(0, CHIPS, hand_out, 0)


def slot_sum(slots_ref, slots, low, rows):
    total = slots_ref[slots[0], low : low + rows].astype(f32)
    for slot in slots[1:]:
        total = total + slots_ref[slot, low : low + rows].astype(f32)
    return total


def head_sums(slots_ref, low):
    parts = []
    for x in range(HEADS):
        halves = [
            slot_sum(slots_ref, (y * SIDE + x, (y + 2) * SIDE + x), low, HALF) for y in range(2)
        ]
        parts.append(jnp.concatenate(halves, axis=0).astype(bf16))
    return jnp.concatenate(parts, axis=1)


def latent_kernel(slots_ref, wk_ref, wv_ref, out_ref):
    key_flat = head_sums(slots_ref, 0)
    value_flat = head_sums(slots_ref, HALF)
    latent = dot(key_flat, wk_ref[...], 1, 1) + dot(value_flat, wv_ref[...], 1, 1)
    out_ref[:, :LATENT] = latent.astype(bf16)
    ropes = []
    for y in range(2):
        slots = [row * SIDE + x for row in (y, y + 2) for x in range(HEADS)]
        rope = slot_sum(slots_ref, slots, 2 * HALF, PIECE)
        ropes += [rope[:, :HALF], rope[:, HALF:]]
    rope = jnp.concatenate(ropes, axis=0)
    out_ref[:, LATENT:] = jnp.concatenate([rope, jnp.zeros_like(rope)], axis=1).astype(bf16)


def projection_kernel(slots_ref, kv_ref, grad_q_ref, own_ref, other_ref, terms):
    values = kv_ref[:LATENT, :].astype(f32)
    inverse = lax.rsqrt(jnp.mean(values * values, axis=0, keepdims=True) + eps)
    normed = (values * inverse).astype(bf16)
    terms[:, : HEADS * NOPE] = dot(normed, head_sums(slots_ref, 0)).astype(bf16)
    terms[:, HEADS * NOPE :] = dot(normed, head_sums(slots_ref, HALF)).astype(bf16)
    core = lax.axis_index("core")
    y_here, x_here = lax.axis_index("y"), lax.axis_index("x")
    for dx in range(SIDE):
        for dy in range(SIDE):
            chip = (y_here ^ dy) * SIDE + (x_here ^ dx)
            first = pl.multiple_of((2 * chip + core) * W_ROWS, W_ROWS)
            second = pl.multiple_of((2 * chip + 1 - core) * W_ROWS, W_ROWS)
            own_ref[dx, dy] = terms[pl.ds(first, W_ROWS), :]
            other_ref[dx, dy] = terms[pl.ds(second, W_ROWS), :]
    low = KEY_ROWS
    for quarter in range(2):
        for half in range(2):
            parts = []
            for x in range(HEADS):
                slots = (2 * quarter * SIDE + x, (2 * quarter + 1) * SIDE + x)
                parts.append(slot_sum(slots_ref, slots, low + half * PIECE, PIECE))
                rope = slot_sum(slots_ref, slots, low + 2 * PIECE, PIECE)
                parts.append(rope[:, half * HALF : (half + 1) * HALF])
            first = half * HALF + quarter * PIECE
            grad_q_ref[first : first + PIECE, :] = jnp.concatenate(parts, axis=1).astype(bf16)


def norm_kernel(slots_ref, kv_ref, out_ref):
    total = jnp.sum(slots_ref[...].astype(f32), axis=0)
    x_hat, inverse = rms_rows(kv_ref[:, :LATENT])
    latent = total[:, :LATENT]
    latent = inverse * (latent - x_hat * jnp.mean(latent * x_hat, axis=-1, keepdims=True))
    row = jnp.concatenate([latent, total[:, LATENT:]], axis=1).astype(bf16)
    out_ref[...] = jnp.broadcast_to(row[None], out_ref.shape)


def call(kernel, shapes, specs, scratch=(), limit=32, flops=0, moved=0, out_specs=None):
    shapes = [jax.ShapeDtypeStruct(*shape) for shape in shapes]
    single = len(shapes) == 1
    if out_specs is None:
        out_specs = VMEM if single else [VMEM] * len(shapes)
    return pl.pallas_call(
        kernel,
        out_shape=shapes[0] if single else shapes,
        in_specs=specs,
        out_specs=out_specs,
        scratch_shapes=scratch,
        compiler_params=pltpu.CompilerParams(vmem_limit_bytes=limit * 2**20),
        cost_estimate=pl.CostEstimate(flops=flops, bytes_accessed=moved, transcendentals=0),
    )


def over_chips(slots):
    return lax.all_to_all(slots, ("y", "x"), 0, 0)


def swap(array, axis, bit):
    return lax.ppermute(array, axis, [(i, i ^ bit) for i in range(lax.axis_size(axis))])


def local(query, kv_row, w_uk, w_uv, grad_out, block_start):
    z_size = lax.axis_size("head")
    z_rows = ROWS // z_size
    kv_t = kv_row.T
    slots, meta = call(
        pack_kernel,
        [((CHIPS, IN_ROWS, NOPE), bf16), ((META,), jnp.int32)],
        [SMEM] + [ANY] * 5,
        [
            pltpu.VMEM((LATENT + ROPE, ROWS), bf16),
            pltpu.VMEM((LATENT, HEADS * NOPE), bf16),
            pltpu.VMEM((LATENT, HEADS * VDIM), bf16),
            pltpu.VMEM((ROWS, HEADS * WIDTH_Q), bf16),
            pltpu.VMEM((ROWS, HEADS * VDIM), bf16),
            pltpu.SMEM((BLOCKS,), jnp.int32),
            pltpu.SemaphoreType.DMA((5,)),
        ],
        limit=60,
        out_specs=[VMEM, SMEM],
    )(block_start, kv_t, w_uk, w_uv, query, grad_out)
    own = over_chips(slots)
    other = swap(own[:, :KEY_ROWS], "core", 1)

    keys, values, queries, grads, stats = call(
        stats_kernel,
        [
            ((KEYS, 2 * NOPE), bf16),
            ((KEYS, VDIM), bf16),
            ((QUERIES, 2 * NOPE), bf16),
            ((QUERIES, VDIM), bf16),
            ((8, QUERIES), f32),
        ],
        [SMEM] + [VMEM] * 2,
        [pltpu.VMEM((KEYS, NOPE), jnp.int32)],
    )(meta, own, other)
    own_part, other_part = call(
        gradient_kernel,
        [((CHIPS, OUT_ROWS, NOPE), bf16), ((CHIPS, KEY_ROWS, NOPE), bf16)],
        [SMEM] + [VMEM] * 6,
        [
            pltpu.VMEM((KEYS, NOPE), jnp.int32),
            pltpu.VMEM((KEYS, 2 * NOPE), bf16),
            pltpu.VMEM((KEYS, VDIM), bf16),
            pltpu.VMEM((QUERIES, 2 * NOPE), f32),
            pltpu.VMEM((CHUNK, 2 * NOPE), f32),
            pltpu.VMEM((CHUNK, VDIM), f32),
        ],
    )(meta, keys, values, queries, grads, stats, swap(stats, "y", 1))
    slots = over_chips(own_part.at[:, :KEY_ROWS].add(swap(other_part, "core", 1)))

    z_part = call(latent_kernel, [((ROWS, Z_WIDTH), bf16)], [VMEM] * 3)(slots, w_uk, w_uv)
    z_slots = lax.all_to_all(z_part.reshape(z_size, z_rows, Z_WIDTH), "head", 0, 0)

    grad_query, own_terms, other_terms = call(
        projection_kernel,
        [((ROWS, HEADS * WIDTH_Q), bf16)] + [((SIDE, SIDE, W_ROWS, W_WIDTH), bf16)] * 2,
        [VMEM] * 2,
        [pltpu.VMEM((LATENT, W_WIDTH), bf16)],
        flops=2 * ROWS * LATENT * W_WIDTH,
        moved=8 * 2**20,
    )(slots, kv_t)
    terms = own_terms + swap(other_terms, "core", 1)
    for axis in ("x", "y"):
        total = terms[0].astype(f32)
        for bit in range(1, SIDE):
            total = total + swap(terms[bit], axis, bit).astype(f32)
        terms = total.astype(bf16)

    first_row = lax.axis_index("head") * z_rows
    kv_rows = lax.dynamic_slice_in_dim(kv_row, first_row, z_rows)
    rows = call(norm_kernel, [((z_size, z_rows, Z_WIDTH), bf16)], [VMEM] * 2)(z_slots, kv_rows)
    all_rows = lax.all_to_all(rows, "head", 0, 0).reshape(ROWS, Z_WIDTH)
    grad_kv_row = all_rows[:, : LATENT + ROPE].astype(f32)
    width = HEADS * NOPE
    return (grad_query, grad_kv_row, total[:, :width], total[:, width:])


def solution(mesh):
    axes = ("y", "x", "core")
    devices = mesh.devices.reshape(SIDE, SIDE, 2, mesh.shape["head"])
    placed = (
        P(axes, "head"),
        P(axes, None),
        P(None, "head"),
        P(None, "head"),
        P(axes, "head"),
        P(),
    )
    return jax.shard_map(
        local,
        mesh=Mesh(devices, (*axes, "head")),
        in_specs=placed,
        out_specs=(P(axes, "head"), P(axes, None), P(axes, "head"), P(axes, "head")),
        check_vma=False,
    )
```

time: 156 us -> 142 us (0.910)
  the two profiles are of different devices: /device:TPU:2 before, /device:TPU:32 now
where the time goes in v2:
time: 142 us; the launch traced here: 141 us
  starting transfers between devices  51.5 us (36%)
  blocking collectives  48.8 us (34%)
  Pallas kernels  22.1 us (16%)
  waiting for transfers between devices  15.5 us (11%)
    all_to_all x2, blocking collectives, over_chips(): return lax.all_to_all(slots, ('y', 'x'), 0, 0)  48.8 us
    ppermute x10, starting transfers between devices, swap(): lax.ppermute(array, axis, [(i, i ^ bit) for i in range(lax.axis_size(axis...  28.8 us
    all_to_all x1, starting transfers between devices, local(): lax.all_to_all(z_part.reshape(z_size, z_rows, Z_WIDTH), 'head', 0, 0)  15.2 us
    ppermute x10, waiting for transfers between devices, swap(): lax.ppermute(array, axis, [(i, i ^ bit) for i in range(lax.axis_size(axis...  10.4 us
    pallas_call x1, Pallas kernels, local(): call(gradient_kernel, [((CHIPS, OUT_ROWS, NOPE), bf16), ((CHIPS, KEY_ROWS...  8.43 us
    all_to_all x1, starting transfers between devices, local(): all_rows = lax.all_to_all(rows, 'head', 0, 0).reshape(ROWS, Z_WIDTH)  7.56 us
    pallas_call x1, Pallas kernels, local(): call(stats_kernel, [((KEYS, 2 * NOPE), bf16), ((KEYS, VDIM), bf16), ((QUE...  5.48 us
    pallas_call x1, Pallas kernels, local(): call(pack_kernel, [((CHIPS, IN_ROWS, NOPE), bf16), ((META,), jnp.int32)],...  4.99 us
  transfers between devices with their start and end apart: 12, of which 6 were waited for; matrix products, arithmetic and copies ran while one was open for 1% of the time, Pallas kernels for 1%

profile of v2, /device:TPU:32, one launch (start us, length us, event | category | flops | bytes accessed | tf_op | source)
XLA Modules:
  0.0 141.3 jit_solution(5630702833583725113)
XLA Ops:
  0.6 5.0 %shard_map.93 = (bf16[16,320,128]{2,1,0:T(8,128)(2,1)}, s32[138]{0:T(256)}) custom-call(s32[64]{0:T(128)} %block_start.1, bf16[576,128]{1,0:T(8,128)(2,1)} %bitcast.26, bf16[512,512]{1,0:T(8,128)(2,1)} %wk_ref.1, bf16[512,512]{1,0:T(8,128)(2,1)} %wv_ref.1, bf16[128,768]{1,0:T(8,128)(2,1)} %q_any.1, bf16[128,512]{1,0:T(8,128)(2,1)} %g_any.1), custom_call_target="tpu_custom_call" | custom-call | tf_op jit(solution)/shard_map/pallas_call | solution.py:410
  5.6 27.0 %all_to_all.20.own_ref = bf16[16,320,128]{2,1,0:T(8,128)(2,1)S(1)} all-to-all(bf16[16,320,128]{2,1,0:T(8,128)(2,1)} %get-tuple-element.29), channel_id=1, replica_groups=mesh['y'=4,'x'=4,'core'=2,'head'=16] {'y','x'}, dimensions={0} | all-to-all | bytes 2621440 | tf_op jit(solution)/shard_map/all_to_all | solution.py:399
  32.6 0.0 copy-start.3
  32.7 1.9 %collective-permute-start = (bf16[16,160,128]{2,1,0:T(8,128)(2,1)S(1)}, bf16[16,160,128]{2,1,0:T(8,128)(2,1)S(1)}, u32[]{:S(2)}, u32[]{:S(2)}) collective-permute-start(bf16[16,160,128]{2,1,0:T(8,128)(2,1)S(1)} %slice.73), channel_id=1, source_target_pairs={{0,16},{16,0},{1,17},{17,1},{2,18},{18,2},{3,19},{19,3},{4,20},{20... | collective-permute-start | bytes 1966088 | tf_op jit(solution)/shard_map/ppermute | solution.py:403
  34.6 2.1 %collective-permute-done.other_ref = bf16[16,160,128]{2,1,0:T(8,128)(2,1)S(1)} collective-permute-done((bf16[16,160,128]{2,1,0:T(8,128)(2,1)S(1)}, bf16[16,160,128]{2,1,0:T(8,128)(2,1)S(1)}, u32[]{:S(2)}, u32[]{:S(2)}) %collective-permute-start) | collective-permute-done | bytes 655392 | tf_op jit(solution)/shard_map/ppermute | solution.py:403
  36.7 0.0 copy-done.3
  36.7 5.5 %shard_map.94 = (bf16[2048,256]{1,0:T(8,128)(2,1)S(1)}, bf16[2048,128]{1,0:T(8,128)(2,1)S(1)}, bf16[1024,256]{1,0:T(8,128)(2,1)S(1)}, bf16[1024,128]{1,0:T(8,128)(2,1)S(1)}, f32[8,1024]{1,0:T(8,128)S(1)}) custom-call(s32[138]{0:T(256)S(1)} %copy-done.3, bf16[16,320,128]{2,1,0:T(8,128)(2,1)S(1)} %all_to_all.20.own_ref, ...), custom_call_target="tpu_custom_call" | custom-call | tf_op jit(solution)/shard_map/pallas_call | solution.py:429
  42.2 2.2 %collective-permute-start.1 = (f32[8,1024]{1,0:T(8,128)S(1)}, f32[8,1024]{1,0:T(8,128)S(1)}, u32[]{:S(2)}, u32[]{:S(2)}) collective-permute-start(f32[8,1024]{1,0:T(8,128)S(1)} %get-tuple-element.34.own_stats), channel_id=1, source_target_pairs={{0,128},{128,0},{256,384},{384,256},{1,129},{129,1},{257,385},{385... | collective-permute-start | bytes 98312 | tf_op jit(solution)/shard_map/ppermute | solution.py:403
  44.4 3.6 %collective-permute-done.1.other_stats = f32[8,1024]{1,0:T(8,128)S(1)} collective-permute-done((f32[8,1024]{1,0:T(8,128)S(1)}, f32[8,1024]{1,0:T(8,128)S(1)}, u32[]{:S(2)}, u32[]{:S(2)}) %collective-permute-start.1) | collective-permute-done | bytes 32800 | tf_op jit(solution)/shard_map/ppermute | solution.py:403
  48.0 8.4 %shard_map.95 = (bf16[16,256,128]{2,1,0:T(8,128)(2,1)S(1)}, bf16[16,160,128]{2,1,0:T(8,128)(2,1)S(1)}) custom-call(s32[138]{0:T(256)S(1)} %copy-done.3, bf16[2048,256]{1,0:T(8,128)(2,1)S(1)} %get-tuple-element.30.keys, bf16[2048,128]{1,0:T(8,128)(2,1)S(1)} %get-tuple-element.31.values, bf16[1024,256]{1,0:T(8,128)(2,1)S(1)} %get-tuple-element.32.queries, ...), custom_call_target="tpu_custom_call" | custom-call | tf_op jit(solution)/shard_map/pallas_call | solution.py:441
  56.4 1.9 %collective-permute-start.2 = (bf16[16,160,128]{2,1,0:T(8,128)(2,1)S(1)}, bf16[16,160,128]{2,1,0:T(8,128)(2,1)S(1)}, u32[]{:S(2)}, u32[]{:S(2)}) collective-permute-start(bf16[16,160,128]{2,1,0:T(8,128)(2,1)S(1)} %get-tuple-element.36), channel_id=1, source_target_pairs={{0,16},{16,0},{1,17},{17,1},{2,18},{18,2},{3,19},{19,3},{4,20},{20... | collective-permute-start | bytes 1966088 | tf_op jit(solution)/shard_map/ppermute | solution.py:403
  58.3 2.1 %collective-permute-done.2 = bf16[16,160,128]{2,1,0:T(8,128)(2,1)S(1)} collective-permute-done((bf16[16,160,128]{2,1,0:T(8,128)(2,1)S(1)}, bf16[16,160,128]{2,1,0:T(8,128)(2,1)S(1)}, u32[]{:S(2)}, u32[]{:S(2)}) %collective-permute-start.2) | collective-permute-done | bytes 655392 | tf_op jit(solution)/shard_map/ppermute | solution.py:403
  60.4 0.3 add_dynamic-update-slice_fusion
  60.7 0.0 copy-start.2
  60.7 0.0 copy-start
  60.7 0.0 copy-start.1
  60.7 21.8 %all_to_all.21.slots_ref = bf16[16,256,128]{2,1,0:T(8,128)(2,1)S(1)} all-to-all(bf16[16,256,128]{2,1,0:T(8,128)(2,1)S(1)} %add_dynamic-update-slice_fusion), channel_id=1, replica_groups=mesh['y'=4,'x'=4,'core'=2,'head'=16] {'y','x'}, dimensions={0} | all-to-all | bytes 2097152 | tf_op jit(solution)/shard_map/all_to_all | solution.py:399
  82.6 0.0 copy-done.2
  82.6 1.2 shard_map.96
  83.8 1.9 %collective-permute-start.3 = (bf16[4,4,16,1024]{3,2,1,0:T(8,128)(2,1)S(1)}, bf16[4,4,16,1024]{3,2,1,0:T(8,128)(2,1)S(1)}, u32[]{:S(2)}, u32[]{:S(2)}) collective-permute-start(bf16[4,4,16,1024]{3,2,1,0:T(8,128)(2,1)S(1)} %get-tuple-element.39), channel_id=1, source_target_pairs={{0,16},{16,0},{1,17},{17,1},{2,18},{18,2},{3,19},{19,3},{4,20},{20... | collective-permute-start | bytes 1572872 | tf_op jit(solution)/shard_map/ppermute | solution.py:403
  85.7 0.0 copy-done
  85.7 0.0 copy-done.1
  85.7 1.2 shard_map.97
  86.8 15.2 %all-to-all-start.2 = ((bf16[16,8,640]{2,1,0:T(8,128)(2,1)}), bf16[16,8,640]{2,1,0:T(8,128)(2,1)S(1)}, u32[]{:S(2)}, u32[]{:S(2)}) async-start(bf16[16,8,640]{2,1,0:T(8,128)(2,1)} %bitcast.1), calls=%async_computation.2 | async-start | bytes 327680 | tf_op jit(solution)/shard_map/all_to_all | solution.py:457
  102.0 0.0 collective-permute-done.3
  102.0 0.2 add.33
  102.3 2.5 %collective-permute-start.4 = (bf16[4,16,1024]{2,1,0:T(8,128)(2,1)S(1)}, bf16[4,16,1024]{2,1,0:T(8,128)(2,1)S(1)}, u32[]{:S(2)}, u32[]{:S(2)}) collective-permute-start(bf16[4,16,1024]{2,1,0:T(8,128)(2,1)S(1)} %get-tuple-element.40), channel_id=1, source_target_pairs={{0,32},{32,0},{64,96},{96,64},{1,33},{33,1},{65,97},{97,65},{2,34}... | collective-permute-start | bytes 393224 | tf_op jit(solution)/shard_map/ppermute | solution.py:403
  104.8 3.3 %collective-permute-start.5 = (bf16[4,16,1024]{2,1,0:T(8,128)(2,1)S(1)}, bf16[4,16,1024]{2,1,0:T(8,128)(2,1)S(1)}, u32[]{:S(2)}, u32[]{:S(2)}) collective-permute-start(bf16[4,16,1024]{2,1,0:T(8,128)(2,1)S(1)} %get-tuple-element.42), channel_id=1, source_target_pairs={{0,64},{32,96},{64,0},{96,32},{1,65},{33,97},{65,1},{97,33},{2,66}... | collective-permute-start | bytes 393224 | tf_op jit(solution)/shard_map/ppermute | solution.py:403
  108.1 4.6 %collective-permute-start.6 = (bf16[4,16,1024]{2,1,0:T(8,128)(2,1)S(1)}, bf16[4,16,1024]{2,1,0:T(8,128)(2,1)S(1)}, u32[]{:S(2)}, u32[]{:S(2)}) collective-permute-start(bf16[4,16,1024]{2,1,0:T(8,128)(2,1)S(1)} %get-tuple-element.41), channel_id=1, source_target_pairs={{0,96},{32,64},{64,32},{96,0},{1,97},{33,65},{65,33},{97,1},{2,98}... | collective-permute-start | bytes 393224 | tf_op jit(solution)/shard_map/ppermute | solution.py:403
  112.7 0.1 constant_dynamic-slice_fusion
  112.8 0.1 copy.12.kv_ref
  112.9 4.5 %all-to-all-done.2.slots_ref = bf16[16,8,640]{2,1,0:T(8,128)(2,1)S(1)} async-done(((bf16[16,8,640]{2,1,0:T(8,128)(2,1)}), bf16[16,8,640]{2,1,0:T(8,128)(2,1)S(1)}, u32[]{:S(2)}, u32[]{:S(2)}) %all-to-all-start.2) | async-done | bytes 163872 | tf_op jit(solution)/shard_map/all_to_all | solution.py:457
  117.4 0.8 shard_map.98
  118.3 7.6 %all-to-all-start.3 = ((bf16[16,8,640]{2,1,0:T(8,128)(2,1)}), bf16[16,8,640]{2,1,0:T(8,128)(2,1)S(1)}, u32[]{:S(2)}, u32[]{:S(2)}) async-start(bf16[16,8,640]{2,1,0:T(8,128)(2,1)} %shard_map.98), calls=%async_computation.3 | async-start | bytes 327680 | tf_op jit(solution)/shard_map/all_to_all | solution.py:477
  125.8 0.0 collective-permute-done.4
  125.9 0.0 collective-permute-done.5
  125.9 0.0 collective-permute-done.6
  125.9 0.1 fusion.2
  126.0 1.9 %collective-permute-start.7 = (bf16[16,1024]{1,0:T(8,128)(2,1)S(1)}, bf16[16,1024]{1,0:T(8,128)(2,1)S(1)}, u32[]{:S(2)}, u32[]{:S(2)}) collective-permute-start(bf16[16,1024]{1,0:T(8,128)(2,1)S(1)} %get-tuple-element.43), channel_id=1, source_target_pairs={{0,128},{128,0},{256,384},{384,256},{1,129},{129,1},{257,385},{385... | collective-permute-start | bytes 98312 | tf_op jit(solution)/shard_map/ppermute | solution.py:403
  127.9 4.2 %collective-permute-start.8 = (bf16[16,1024]{1,0:T(8,128)(2,1)S(1)}, bf16[16,1024]{1,0:T(8,128)(2,1)S(1)}, u32[]{:S(2)}, u32[]{:S(2)}) collective-permute-start(bf16[16,1024]{1,0:T(8,128)(2,1)S(1)} %get-tuple-element.45), channel_id=1, source_target_pairs={{0,256},{128,384},{256,0},{384,128},{1,257},{129,385},{257,1},{385... | collective-permute-start | bytes 98312 | tf_op jit(solution)/shard_map/ppermute | solution.py:403
  132.1 4.3 %collective-permute-start.9 = (bf16[16,1024]{1,0:T(8,128)(2,1)S(1)}, bf16[16,1024]{1,0:T(8,128)(2,1)S(1)}, u32[]{:S(2)}, u32[]{:S(2)}) collective-permute-start(bf16[16,1024]{1,0:T(8,128)(2,1)S(1)} %get-tuple-element.44), channel_id=1, source_target_pairs={{0,384},{128,256},{256,128},{384,0},{1,385},{129,257},{257,129},{3... | collective-permute-start | bytes 98312 | tf_op jit(solution)/shard_map/ppermute | solution.py:403
  136.4 0.0 collective-permute-done.7
  136.4 0.0 collective-permute-done.8
  136.4 2.7 %collective-permute-done.9 = bf16[16,1024]{1,0:T(8,128)(2,1)S(1)} collective-permute-done((bf16[16,1024]{1,0:T(8,128)(2,1)S(1)}, bf16[16,1024]{1,0:T(8,128)(2,1)S(1)}, u32[]{:S(2)}, u32[]{:S(2)}) %collective-permute-start.9) | collective-permute-done | bytes 32800 | tf_op jit(solution)/shard_map/ppermute | solution.py:403
  139.2 0.6 fusion.5
  139.8 0.6 all-to-all-done.3
  140.4 0.1 copy.13
  140.5 0.7 convert_element_type.36
  (4 shorter events, 0.1 us)
Async XLA Ops:
  32.6 4.0 %copy-start.3 = (s32[138]{0:T(256)S(1)}, s32[138]{0:T(256)}, u32[]{:S(2)}) copy-start(s32[138]{0:T(256)} %get-tuple-element.28.meta) | copy-start | bytes 1660
  32.7 4.0 %collective-permute-start = (bf16[16,160,128]{2,1,0:T(8,128)(2,1)S(1)}, bf16[16,160,128]{2,1,0:T(8,128)(2,1)S(1)}, u32[]{:S(2)}, u32[]{:S(2)}) collective-permute-start(bf16[16,160,128]{2,1,0:T(8,128)(2,1)S(1)} %slice.73), channel_id=1, source_target_pairs={{0,16},{16,0},{1,17},{17,1},{2,18},{18,2},{3,19},{19,3},{4,20},{20... | collective-permute-start | bytes 1966088 | tf_op jit(solution)/shard_map/ppermute | solution.py:403
  42.2 5.8 %collective-permute-start.1 = (f32[8,1024]{1,0:T(8,128)S(1)}, f32[8,1024]{1,0:T(8,128)S(1)}, u32[]{:S(2)}, u32[]{:S(2)}) collective-permute-start(f32[8,1024]{1,0:T(8,128)S(1)} %get-tuple-element.34.own_stats), channel_id=1, source_target_pairs={{0,128},{128,0},{256,384},{384,256},{1,129},{129,1},{257,385},{385... | collective-permute-start | bytes 98312 | tf_op jit(solution)/shard_map/ppermute | solution.py:403
  56.4 4.0 %collective-permute-start.2 = (bf16[16,160,128]{2,1,0:T(8,128)(2,1)S(1)}, bf16[16,160,128]{2,1,0:T(8,128)(2,1)S(1)}, u32[]{:S(2)}, u32[]{:S(2)}) collective-permute-start(bf16[16,160,128]{2,1,0:T(8,128)(2,1)S(1)} %get-tuple-element.36), channel_id=1, source_target_pairs={{0,16},{16,0},{1,17},{17,1},{2,18},{18,2},{3,19},{19,3},{4,20},{20... | collective-permute-start | bytes 1966088 | tf_op jit(solution)/shard_map/ppermute | solution.py:403
  60.7 21.9 %copy-start.2 = (bf16[128,576]{0,1:T(8,128)(2,1)S(1)}, bf16[128,576]{0,1:T(8,128)(2,1)}, u32[]{:S(2)}) copy-start(bf16[128,576]{0,1:T(8,128)(2,1)} %param.9) | copy-start | bytes 442372
  60.7 24.9 %copy-start = (bf16[512,512]{1,0:T(8,128)(2,1)S(1)}, bf16[512,512]{1,0:T(8,128)(2,1)}, u32[]{:S(2)}) copy-start(bf16[512,512]{1,0:T(8,128)(2,1)} %wk_ref.1) | copy-start | bytes 1572868
  60.7 24.9 %copy-start.1 = (bf16[512,512]{1,0:T(8,128)(2,1)S(1)}, bf16[512,512]{1,0:T(8,128)(2,1)}, u32[]{:S(2)}) copy-start(bf16[512,512]{1,0:T(8,128)(2,1)} %wv_ref.1) | copy-start | bytes 1572868
  83.8 18.3 %collective-permute-start.3 = (bf16[4,4,16,1024]{3,2,1,0:T(8,128)(2,1)S(1)}, bf16[4,4,16,1024]{3,2,1,0:T(8,128)(2,1)S(1)}, u32[]{:S(2)}, u32[]{:S(2)}) collective-permute-start(bf16[4,4,16,1024]{3,2,1,0:T(8,128)(2,1)S(1)} %get-tuple-element.39), channel_id=1, source_target_pairs={{0,16},{16,0},{1,17},{17,1},{2,18},{18,2},{3,19},{19,3},{4,20},{20... | collective-permute-start | bytes 1572872 | tf_op jit(solution)/shard_map/ppermute | solution.py:403
  86.8 30.6 %all-to-all-start.2 = ((bf16[16,8,640]{2,1,0:T(8,128)(2,1)}), bf16[16,8,640]{2,1,0:T(8,128)(2,1)S(1)}, u32[]{:S(2)}, u32[]{:S(2)}) async-start(bf16[16,8,640]{2,1,0:T(8,128)(2,1)} %bitcast.1), calls=%async_computation.2 | async-start | bytes 327680 | tf_op jit(solution)/shard_map/all_to_all | solution.py:457
  102.3 23.6 %collective-permute-start.4 = (bf16[4,16,1024]{2,1,0:T(8,128)(2,1)S(1)}, bf16[4,16,1024]{2,1,0:T(8,128)(2,1)S(1)}, u32[]{:S(2)}, u32[]{:S(2)}) collective-permute-start(bf16[4,16,1024]{2,1,0:T(8,128)(2,1)S(1)} %get-tuple-element.40), channel_id=1, source_target_pairs={{0,32},{32,0},{64,96},{96,64},{1,33},{33,1},{65,97},{97,65},{2,34}... | collective-permute-start | bytes 393224 | tf_op jit(solution)/shard_map/ppermute | solution.py:403
  104.8 21.1 %collective-permute-start.5 = (bf16[4,16,1024]{2,1,0:T(8,128)(2,1)S(1)}, bf16[4,16,1024]{2,1,0:T(8,128)(2,1)S(1)}, u32[]{:S(2)}, u32[]{:S(2)}) collective-permute-start(bf16[4,16,1024]{2,1,0:T(8,128)(2,1)S(1)} %get-tuple-element.42), channel_id=1, source_target_pairs={{0,64},{32,96},{64,0},{96,32},{1,65},{33,97},{65,1},{97,33},{2,66}... | collective-permute-start | bytes 393224 | tf_op jit(solution)/shard_map/ppermute | solution.py:403
  108.1 17.8 %collective-permute-start.6 = (bf16[4,16,1024]{2,1,0:T(8,128)(2,1)S(1)}, bf16[4,16,1024]{2,1,0:T(8,128)(2,1)S(1)}, u32[]{:S(2)}, u32[]{:S(2)}) collective-permute-start(bf16[4,16,1024]{2,1,0:T(8,128)(2,1)S(1)} %get-tuple-element.41), channel_id=1, source_target_pairs={{0,96},{32,64},{64,32},{96,0},{1,97},{33,65},{65,33},{97,1},{2,98}... | collective-permute-start | bytes 393224 | tf_op jit(solution)/shard_map/ppermute | solution.py:403
  118.3 22.1 %all-to-all-start.3 = ((bf16[16,8,640]{2,1,0:T(8,128)(2,1)}), bf16[16,8,640]{2,1,0:T(8,128)(2,1)S(1)}, u32[]{:S(2)}, u32[]{:S(2)}) async-start(bf16[16,8,640]{2,1,0:T(8,128)(2,1)} %shard_map.98), calls=%async_computation.3 | async-start | bytes 327680 | tf_op jit(solution)/shard_map/all_to_all | solution.py:477
  126.0 10.4 %collective-permute-start.7 = (bf16[16,1024]{1,0:T(8,128)(2,1)S(1)}, bf16[16,1024]{1,0:T(8,128)(2,1)S(1)}, u32[]{:S(2)}, u32[]{:S(2)}) collective-permute-start(bf16[16,1024]{1,0:T(8,128)(2,1)S(1)} %get-tuple-element.43), channel_id=1, source_target_pairs={{0,128},{128,0},{256,384},{384,256},{1,129},{129,1},{257,385},{385... | collective-permute-start | bytes 98312 | tf_op jit(solution)/shard_map/ppermute | solution.py:403
  127.9 8.5 %collective-permute-start.8 = (bf16[16,1024]{1,0:T(8,128)(2,1)S(1)}, bf16[16,1024]{1,0:T(8,128)(2,1)S(1)}, u32[]{:S(2)}, u32[]{:S(2)}) collective-permute-start(bf16[16,1024]{1,0:T(8,128)(2,1)S(1)} %get-tuple-element.45), channel_id=1, source_target_pairs={{0,256},{128,384},{256,0},{384,128},{1,257},{129,385},{257,1},{385... | collective-permute-start | bytes 98312 | tf_op jit(solution)/shard_map/ppermute | solution.py:403
  132.1 7.0 %collective-permute-start.9 = (bf16[16,1024]{1,0:T(8,128)(2,1)S(1)}, bf16[16,1024]{1,0:T(8,128)(2,1)S(1)}, u32[]{:S(2)}, u32[]{:S(2)}) collective-permute-start(bf16[16,1024]{1,0:T(8,128)(2,1)S(1)} %get-tuple-element.44), channel_id=1, source_target_pairs={{0,384},{128,256},{256,128},{384,0},{1,385},{129,257},{257,129},{3... | collective-permute-start | bytes 98312 | tf_op jit(solution)/shard_map/ppermute | solution.py:403

commit v3 on v2

--- a/solution.py
+++ b/solution.py
@@ -27,14 +27,11 @@
 OUT_ROWS = KEY_ROWS + 3 * PIECE
 W_ROWS = LATENT // (2 * CHIPS)
 W_WIDTH = HEADS * (NOPE + VDIM)
-CHUNK = 512
+CHUNK = 1024
 GROUP = 512
 N_CHUNKS = KEYS // CHUNK
 N_GROUPS = QUERIES // GROUP
-LISTED = 2 * CHIPS
-KEY_RANK, QUERY_RANK, KEY_START, QUERY_START, SEEN = (i * LISTED for i in range(5))
-SPARE = SEEN + N_GROUPS
-META = SPARE + 8
+UNROLL = CHIPS
 Z_WIDTH = 640
 LOG2E = 1.4426950408889634
 SCALE = 1.0 / math.sqrt(WIDTH_Q)
@@ -60,31 +57,36 @@
     return (values * inverse, inverse)
 
 
-def list_blocks(block_start, meta, holder):
+def list_blocks(starts, meta, q_pos):
     half = lax.axis_index("y") % 2
     core = lax.axis_index("core")
-
-    def find(index, carry):
-        holder[block_start[index] // HALF] = index
-        return carry
-
-    lax.fori_loop(0, BLOCKS, find, 0)
-
-    def count(place, carry):
-        n_keys, n_queries = carry
-        index = holder[place]
-        is_key = index % 2 == half
-        is_query = (index // 2) % 2 == core
-        meta[jnp.where(is_key, KEY_RANK + index // 2, SPARE)] = n_keys
-        meta[jnp.where(is_key, KEY_START + n_keys, SPARE)] = place * HALF
-        n_keys = n_keys + is_key.astype(jnp.int32)
-        of_query = 2 * (index // 4) + index % 2
-        meta[jnp.where(is_query, QUERY_RANK + of_query, SPARE)] = n_queries
-        meta[jnp.where(is_query, QUERY_START + n_queries, SPARE)] = place * HALF
-        meta[jnp.where(is_query, SEEN + n_queries // (GROUP // PIECE), SPARE)] = n_keys
-        return (n_keys, n_queries + is_query.astype(jnp.int32))
-
-    lax.fori_loop(0, BLOCKS, count, (0, 0))
+    shape = (BLOCKS, BLOCKS)
+    across = jnp.broadcast_to(starts[...], shape)
+    down = across.T
+    row = lax.broadcasted_iota(jnp.int32, shape, 0)
+    lane = lax.broadcasted_iota(jnp.int32, shape, 1)
+
+    def tally(where, axis):
+        return jnp.sum(where.astype(jnp.int32), axis=axis, keepdims=True)
+
+    key_rank = tally((down < across) & (row % 2 == half), 0)
+    query_rank = tally((down < across) & ((row // 2) % 2 == core), 0)
+    query_rank_down = tally((across < down) & ((lane // 2) % 2 == core), 1)
+    is_query = (row[:, :1] // 2) % 2 == core
+    shape = (BLOCKS, QUERIES)
+    piece = lax.broadcasted_iota(jnp.int32, shape, 1) // PIECE
+    mine = (query_rank_down == piece) & is_query
+    position = jnp.sum(jnp.where(mine, down[:, :1], 0), axis=0, keepdims=True)
+    seen = []
+    for group in range(N_GROUPS):
+        last = position[:, (group + 1) * GROUP - 1 : (group + 1) * GROUP]
+        seen.append(tally((across[:1] <= last) & (lane[:1] % 2 == half), 1))
+    seen = jnp.concatenate(seen + [jnp.zeros((1, BLOCKS - N_GROUPS), jnp.int32)], axis=1)
+    rest = jnp.zeros((5, BLOCKS), jnp.int32)
+    meta[...] = jnp.concatenate([key_rank, query_rank, seen, rest], axis=0)
+    offset = lax.broadcasted_iota(jnp.int32, (1, QUERIES), 1) % PIECE
+    offset = offset + (lax.axis_index("y") // 2) * PIECE
+    q_pos[...] = jnp.broadcast_to(position + offset, q_pos.shape)
 
 
 def pack_kernel(
@@ -94,46 +96,34 @@
     wv_any,
     q_any,
     g_any,
-    out_ref,
+    out_any,
     meta,
+    q_pos,
     kv_ref,
     wk_ref,
     wv_ref,
     q_ref,
     g_ref,
-    holder,
+    out_ref,
     sems,
+    out_sems,
 ):
-    pairs = [(kv_any, kv_ref), (wk_any, wk_ref), (wv_any, wv_ref), (q_any, q_ref), (g_any, g_ref)]
+    pairs = [(q_any, q_ref), (g_any, g_ref), (kv_any, kv_ref), (wk_any, wk_ref), (wv_any, wv_ref)]
     copies = [
         pltpu.make_async_copy(source, target, sems.at[index])
         for index, (source, target) in enumerate(pairs)
     ]
     for copy in copies:
         copy.start()
-    list_blocks(block_start, meta, holder)
-    for copy in copies:
-        copy.wait()
-    values = kv_ref[:LATENT, :].astype(f32)
-    inverse = lax.rsqrt(jnp.mean(values * values, axis=0, keepdims=True) + eps)
-    normed = (values * inverse).T.astype(bf16)
-    rope = kv_ref[LATENT:, :].astype(f32).T.astype(bf16)
-    keys = dot(normed, wk_ref[...]).astype(bf16)
-    values = dot(normed, wv_ref[...]).astype(bf16)
+    list_blocks(block_start, meta, q_pos)
+    copies[0].wait()
+    copies[1].wait()
     for x in range(HEADS):
-        key = keys[:, x * NOPE : (x + 1) * NOPE]
-        value = values[:, x * VDIM : (x + 1) * VDIM]
         q_nope = q_ref[:, x * WIDTH_Q : x * WIDTH_Q + NOPE]
         q_rope = q_ref[:, x * WIDTH_Q + NOPE : (x + 1) * WIDTH_Q]
         grad = g_ref[:, x * VDIM : (x + 1) * VDIM]
         for y in range(SIDE):
             slot = y * SIDE + x
-            low = (y % 2) * HALF
-            out_ref[slot, :HALF] = key[low : low + HALF]
-            out_ref[slot, HALF : 2 * HALF] = value[low : low + HALF]
-            out_ref[slot, 2 * HALF : KEY_ROWS] = jnp.concatenate(
-                [rope[low : low + PIECE], rope[low + PIECE : low + HALF]], axis=1
-            )
             first = slice((y // 2) * PIECE, (y // 2 + 1) * PIECE)
             second = slice(HALF + (y // 2) * PIECE, HALF + (y // 2 + 1) * PIECE)
             low = KEY_ROWS
@@ -144,34 +134,54 @@
             out_ref[slot, low + 4 * PIECE : low + 5 * PIECE] = jnp.concatenate(
                 [q_rope[first], q_rope[second]], axis=1
             )
-
-
-def place_positions(meta, k_pos):
+    copies[2].wait()
+    values = kv_ref[:LATENT, :].astype(f32)
+    inverse = lax.rsqrt(jnp.mean(values * values, axis=0, keepdims=True) + eps)
+    normed = (values * inverse).T.astype(bf16)
+    rope = kv_ref[LATENT:, :].astype(f32).T.astype(bf16)
+    copies[3].wait()
+    keys = dot(normed, wk_ref[...]).astype(bf16)
+    copies[4].wait()
+    values = dot(normed, wv_ref[...]).astype(bf16)
+    sent = []
+    for y in range(SIDE):
+        low = (y % 2) * HALF
+        for x in range(HEADS):
+            slot = y * SIDE + x
+            out_ref[slot, :HALF] = keys[low : low + HALF, x * NOPE : (x + 1) * NOPE]
+            out_ref[slot, HALF : 2 * HALF] = values[low : low + HALF, x * VDIM : (x + 1) * VDIM]
+            out_ref[slot, 2 * HALF : KEY_ROWS] = jnp.concatenate(
+                [rope[low : low + PIECE], rope[low + PIECE : low + HALF]], axis=1
+            )
+        part = pl.ds(y * SIDE, SIDE)
+        sent.append(pltpu.make_async_copy(out_ref.at[part], out_any.at[part], out_sems.at[y]))
+        sent[-1].start()
+    for copy in sent:
+        copy.wait()
+
+
+def key_block(chip, core):
+    return (2 * chip + core) * 2 + lax.axis_index("y") % 2
+
+
+def place_positions(block_start, meta, k_pos):
     rows = lax.broadcasted_iota(jnp.int32, (HALF, NOPE), 0)
 
-    def body(rank, carry):
-        at = pl.ds(pl.multiple_of(rank * HALF, HALF), HALF)
-        k_pos[at, :] = rows + meta[KEY_START + rank]
+    def body(index, carry):
+        block = 2 * index + lax.axis_index("y") % 2
+        at = pl.ds(pl.multiple_of(meta[0, block] * HALF, HALF), HALF)
+        k_pos[at, :] = rows + block_start[block]
         return carry
 
-    lax.fori_loop(0, LISTED, body, 0)
-
-
-def query_positions(meta, group):
-    lane = lax.broadcasted_iota(jnp.int32, (1, GROUP), 1)
-    count = GROUP // PIECE
-    start = jnp.zeros((1, GROUP), jnp.int32)
-    for piece in range(count):
-        start = jnp.where(lane // PIECE == piece, meta[QUERY_START + group * count + piece], start)
-    return start + (lax.axis_index("y") // 2) * PIECE + lane % PIECE
+    lax.fori_loop(0, 2 * CHIPS, body, 0, unroll=UNROLL)
 
 
 def seen_chunks(meta, group):
-    return (meta[SEEN + group] * HALF + CHUNK - 1) // CHUNK
+    return (meta[2, group] * HALF + CHUNK - 1) // CHUNK
 
 
 def stats_kernel(
-    meta, own_ref, other_ref, keys, values, queries, grads, stats, k_pos
+    block_start, meta, q_pos, own_ref, other_ref, keys, values, queries, grads, stats, k_pos
 ):
     core = lax.axis_index("core")
     pad_key = jnp.zeros((HALF, HALF), bf16)
@@ -179,7 +189,7 @@
 
     def place(chip, carry):
         for ref, side in ((own_ref, core), (other_ref, 1 - core)):
-            rank = meta[KEY_RANK + 2 * chip + side]
+            rank = meta[0, key_block(chip, side)]
             at = pl.ds(pl.multiple_of(rank * HALF, HALF), HALF)
             rope = ref[chip, 2 * HALF : KEY_ROWS]
             rope = jnp.concatenate([rope[:, :HALF], rope[:, HALF:]], axis=0)
@@ -189,7 +199,7 @@
         low = KEY_ROWS
         q_rope = own_ref[chip, low + 4 * PIECE : low + 5 * PIECE]
         for half in range(2):
-            rank = meta[QUERY_RANK + 2 * chip + half]
+            rank = meta[1, (2 * chip + core) * 2 + half]
             at = pl.ds(pl.multiple_of(rank * PIECE, PIECE), PIECE)
             queries[at, :NOPE] = own_ref[chip, low + half * PIECE : low + (half + 1) * PIECE]
             queries[at, NOPE:] = jnp.concatenate(
@@ -198,21 +208,21 @@
             grads[at, :] = own_ref[chip, low + (2 + half) * PIECE : low + (3 + half) * PIECE]
         return carry
 
-    lax.fori_loop(0, CHIPS, place, 0)
-    place_positions(meta, k_pos)
+    lax.fori_loop(0, CHIPS, place, 0, unroll=UNROLL)
+    place_positions(block_start, meta, k_pos)
 
     for group in range(N_GROUPS):
         lanes = slice(group * GROUP, (group + 1) * GROUP)
         q_group = queries[lanes, :]
         g_group = grads[lanes, :]
-        q_pos = query_positions(meta, group)
+        q_at = q_pos[0:1, lanes]
 
         def gather_stats(index, carry):
             top, weight_sum, weighted = carry
             at = pl.ds(pl.multiple_of(index * CHUNK, CHUNK), CHUNK)
             score = dot(keys[at, :], q_group, 1, 1) * (SCALE * LOG2E)
             key_at = jnp.concatenate([k_pos[at, :]] * (GROUP // NOPE), axis=1)
-            score = jnp.where(key_at <= q_pos, score, masked_low)
+            score = jnp.where(key_at <= q_at, score, masked_low)
             slope = dot(values[at, :], g_group, 1, 1)
             fresh = jnp.maximum(top, jnp.max(score, axis=0, keepdims=True))
             fade = jnp.exp2(top - fresh)
@@ -234,7 +244,9 @@
 
 
 def gradient_kernel(
+    block_start,
     meta,
+    q_pos,
     keys,
     values,
     queries,
@@ -250,7 +262,7 @@
     key_sum,
     value_sum,
 ):
-    place_positions(meta, k_pos)
+    place_positions(block_start, meta, k_pos)
     own_top = own_stats[0:1, :]
     other_top = other_stats[0:1, :]
     top = jnp.maximum(own_top, other_top)
@@ -261,7 +273,6 @@
     log_total = top + jnp.log2(weight_sum)
     average = weighted / weight_sum
     query_grads[...] = jnp.zeros_like(query_grads)
-    positions = [query_positions(meta, group) for group in range(N_GROUPS)]
 
     def gradients(index, carry):
         at = pl.ds(pl.multiple_of(index * CHUNK, CHUNK), CHUNK)
@@ -271,10 +282,11 @@
             lanes = slice(group * GROUP, (group + 1) * GROUP)
 
             @pl.when(index < seen_chunks(meta, group))
-            def _(lanes=lanes, q_pos=positions[group]):
+            def _(lanes=lanes):
                 score = dot(keys[at, :], queries[lanes, :], 1, 1) * (SCALE * LOG2E)
                 key_at = jnp.concatenate([k_pos[at, :]] * (GROUP // NOPE), axis=1)
-                score = jnp.where(key_at <= q_pos, score - log_total[:, lanes], masked_low)
+                visible = key_at <= q_pos[0:1, lanes]
+                score = jnp.where(visible, score - log_total[:, lanes], masked_low)
                 slope = dot(values[at, :], grads[lanes, :], 1, 1)
                 probs = jnp.exp2(score)
                 score_grad = (probs * ((slope - average[:, lanes]) * SCALE)).astype(bf16)
@@ -291,7 +303,7 @@
 
     def hand_out(chip, carry):
         for ref, side in ((own_out, core), (other_out, 1 - core)):
-            rank = meta[KEY_RANK + 2 * chip + side]
+            rank = meta[0, key_block(chip, side)]
             at = pl.ds(pl.multiple_of(rank * HALF, HALF), HALF)
             ref[chip, :HALF] = key_grads[at, :NOPE]
             ref[chip, HALF : 2 * HALF] = value_grads[at, :]
@@ -300,7 +312,7 @@
         low = KEY_ROWS
         ropes = []
         for half in range(2):
-            rank = meta[QUERY_RANK + 2 * chip + half]
+            rank = meta[1, (2 * chip + core) * 2 + half]
             at = pl.ds(pl.multiple_of(rank * PIECE, PIECE), PIECE)
             piece = query_grads[at, :].astype(bf16)
             own_out[chip, low + half * PIECE : low + (half + 1) * PIECE] = piece[:, :NOPE]
@@ -308,7 +320,7 @@
         own_out[chip, low + 2 * PIECE : low + 3 * PIECE] = jnp.concatenate(ropes, axis=1)
         return carry
 
-    lax.fori_loop(0, CHIPS, hand_out, 0)
+    lax.fori_loop(0, CHIPS, hand_out, 0, unroll=UNROLL)
 
 
 def slot_sum(slots_ref, slots, low, rows):
@@ -395,38 +407,32 @@
     )
 
 
-def over_chips(slots):
-    return lax.all_to_all(slots, ("y", "x"), 0, 0)
-
-
-def swap(array, axis, bit):
-    return lax.ppermute(array, axis, [(i, i ^ bit) for i in range(lax.axis_size(axis))])
-
-
-def local(query, kv_row, w_uk, w_uv, grad_out, block_start):
-    z_size = lax.axis_size("head")
-    z_rows = ROWS // z_size
-    kv_t = kv_row.T
-    slots, meta = call(
+def run_pack(*args):
+    return call(
         pack_kernel,
-        [((CHIPS, IN_ROWS, NOPE), bf16), ((META,), jnp.int32)],
-        [SMEM] + [ANY] * 5,
+        [
+            ((CHIPS, IN_ROWS, NOPE), bf16),
+            ((8, BLOCKS), jnp.int32),
+            ((8, QUERIES), jnp.int32),
+        ],
+        [VMEM] + [ANY] * 5,
         [
             pltpu.VMEM((LATENT + ROPE, ROWS), bf16),
             pltpu.VMEM((LATENT, HEADS * NOPE), bf16),
             pltpu.VMEM((LATENT, HEADS * VDIM), bf16),
             pltpu.VMEM((ROWS, HEADS * WIDTH_Q), bf16),
             pltpu.VMEM((ROWS, HEADS * VDIM), bf16),
-            pltpu.SMEM((BLOCKS,), jnp.int32),
+            pltpu.VMEM((CHIPS, IN_ROWS, NOPE), bf16),
             pltpu.SemaphoreType.DMA((5,)),
+            pltpu.SemaphoreType.DMA((SIDE,)),
         ],
         limit=60,
-        out_specs=[VMEM, SMEM],
-    )(block_start, kv_t, w_uk, w_uv, query, grad_out)
-    own = over_chips(slots)
-    other = swap(own[:, :KEY_ROWS], "core", 1)
-
-    keys, values, queries, grads, stats = call(
+        out_specs=[ANY, VMEM, VMEM],
+    )(*args)
+
+
+def run_stats(*args):
+    return call(
         stats_kernel,
         [
             ((KEYS, 2 * NOPE), bf16),
@@ -435,13 +441,16 @@
             ((QUERIES, VDIM), bf16),
             ((8, QUERIES), f32),
         ],
-        [SMEM] + [VMEM] * 2,
+        [SMEM] * 2 + [VMEM] * 3,
         [pltpu.VMEM((KEYS, NOPE), jnp.int32)],
-    )(meta, own, other)
-    own_part, other_part = call(
+    )(*args)
+
+
+def run_gradient(*args):
+    return call(
         gradient_kernel,
         [((CHIPS, OUT_ROWS, NOPE), bf16), ((CHIPS, KEY_ROWS, NOPE), bf16)],
-        [SMEM] + [VMEM] * 6,
+        [SMEM] * 2 + [VMEM] * 7,
         [
             pltpu.VMEM((KEYS, NOPE), jnp.int32),
             pltpu.VMEM((KEYS, 2 * NOPE), bf16),
@@ -450,12 +459,35 @@
             pltpu.VMEM((CHUNK, 2 * NOPE), f32),
             pltpu.VMEM((CHUNK, VDIM), f32),
         ],
-    )(meta, keys, values, queries, grads, stats, swap(stats, "y", 1))
+    )(*args)
+
+
+def over_chips(slots):
+    return lax.all_to_all(slots, ("y", "x"), 0, 0)
+
+
+def swap(array, axis, bit):
+    return lax.ppermute(array, axis, [(i, i ^ bit) for i in range(lax.axis_size(axis))])
+
+
+def local(query, kv_row, w_uk, w_uv, grad_out, block_start):
+    z_size = lax.axis_size("head")
+    z_rows = ROWS // z_size
+    kv_t = kv_row.T
+    slots, meta, q_pos = run_pack(
+        block_start.reshape(1, BLOCKS), kv_t, w_uk, w_uv, query, grad_out
+    )
+    own = over_chips(slots)
+    other = swap(own[:, :KEY_ROWS], "core", 1)
+
+    *placed, stats = run_stats(block_start, meta, q_pos, own, other)
+    own_part, other_part = run_gradient(
+        block_start, meta, q_pos, *placed, stats, swap(stats, "y", 1)
+    )
     slots = over_chips(own_part.at[:, :KEY_ROWS].add(swap(other_part, "core", 1)))
 
     z_part = call(latent_kernel, [((ROWS, Z_WIDTH), bf16)], [VMEM] * 3)(slots, w_uk, w_uv)
-    z_slots = lax.all_to_all(z_part.reshape(z_size, z_rows, Z_WIDTH), "head", 0, 0)
-
+    z_part, slots = lax.optimization_barrier((z_part, slots))
     grad_query, own_terms, other_terms = call(
         projection_kernel,
         [((ROWS, HEADS * WIDTH_Q), bf16)] + [((SIDE, SIDE, W_ROWS, W_WIDTH), bf16)] * 2,
@@ -471,6 +503,7 @@
             total = total + swap(terms[bit], axis, bit).astype(f32)
         terms = total.astype(bf16)
 
+    z_slots = lax.all_to_all(z_part.reshape(z_size, z_rows, Z_WIDTH), "head", 0, 0)
     first_row = lax.axis_index("head") * z_rows
     kv_rows = lax.dynamic_slice_in_dim(kv_row, first_row, z_rows)
     rows = call(norm_kernel, [((z_size, z_rows, Z_WIDTH), bf16)], [VMEM] * 2)(z_slots, kv_rows)

time: 142 us -> 139 us (0.979)
  Pallas kernels: 22.1 us -> 18.4 us
  starting transfers between devices: 51.5 us -> 53.2 us
    pallas_call x3, Pallas kernels: 18.9 us -> 15.2 us  [the longest x1 6.92 us: run_gradient(): call(gradient_kernel, [((CHIPS, OUT_ROWS, NOPE), bf16), ((CHIPS, KEY_ROWS...]
    ppermute x10, starting transfers between devices: 28.8 us -> 30.4 us  [swap(): lax.ppermute(array, axis, [(i, i ^ bit) for i in range(lax.axis_size(axis...]
where the time goes in v3:
time: 139 us; the launch traced here: 138 us
  starting transfers between devices  53.2 us (38%)
  blocking collectives  47.8 us (34%)
  Pallas kernels  18.4 us (13%)
  waiting for transfers between devices  15.7 us (11%)
    all_to_all x2, blocking collectives, over_chips(): return lax.all_to_all(slots, ('y', 'x'), 0, 0)  47.8 us
    ppermute x10, starting transfers between devices, swap(): lax.ppermute(array, axis, [(i, i ^ bit) for i in range(lax.axis_size(axis...  30.4 us
    all_to_all x1, starting transfers between devices, local(): lax.all_to_all(z_part.reshape(z_size, z_rows, Z_WIDTH), 'head', 0, 0)  15.2 us
    ppermute x10, waiting for transfers between devices, swap(): lax.ppermute(array, axis, [(i, i ^ bit) for i in range(lax.axis_size(axis...  10.6 us
    all_to_all x1, starting transfers between devices, local(): all_rows = lax.all_to_all(rows, 'head', 0, 0).reshape(ROWS, Z_WIDTH)  7.56 us
    pallas_call x1, Pallas kernels, run_gradient(): call(gradient_kernel, [((CHIPS, OUT_ROWS, NOPE), bf16), ((CHIPS, KEY_ROWS...  6.92 us
    all_to_all x1, waiting for transfers between devices, local(): lax.all_to_all(z_part.reshape(z_size, z_rows, Z_WIDTH), 'head', 0, 0)  4.5 us
    pallas_call x1, Pallas kernels, run_pack(): call(pack_kernel, [((CHIPS, IN_ROWS, NOPE), bf16), ((8, BLOCKS), jnp.int3...  4.28 us
  transfers between devices with their start and end apart: 12, of which 6 were waited for; matrix products, arithmetic and copies ran while one was open for 1% of the time, Pallas kernels for 1%

profile of v3, /device:TPU:32, one launch (start us, length us, event | category | flops | bytes accessed | tf_op | source)
XLA Modules:
  0.0 138.3 jit_solution(4220345709127815403)
XLA Ops:
  0.6 4.3 %shard_map.93 = (bf16[16,320,128]{2,1,0:T(8,128)(2,1)}, s32[8,64]{1,0:T(8,128)}, s32[8,1024]{1,0:T(8,128)}) custom-call(s32[1,64]{1,0:T(1,128)} %bitcast.29, bf16[576,128]{1,0:T(8,128)(2,1)} %bitcast.27, bf16[512,512]{1,0:T(8,128)(2,1)} %wk_ref.1, bf16[512,512]{1,0:T(8,128)(2,1)} %wv_ref.1, bf16[128,768]{1,0:T(8,128)(2,1)} %q_any.1, bf16[128,512]{1,0:T(8,128)(2,1)} %g_any.1), custom_call_target="tpu_custom_call" | custom-call | tf_op jit(solution)/shard_map/pallas_call | solution.py:411
  4.9 27.0 %all_to_all.20.own_ref = bf16[16,320,128]{2,1,0:T(8,128)(2,1)S(1)} all-to-all(bf16[16,320,128]{2,1,0:T(8,128)(2,1)} %get-tuple-element.33), channel_id=1, replica_groups=mesh['y'=4,'x'=4,'core'=2,'head'=16] {'y','x'}, dimensions={0} | all-to-all | bytes 2621440 | tf_op jit(solution)/shard_map/all_to_all | solution.py:466
  31.9 0.0 copy-start.3
  31.9 0.0 copy-start.4
  31.9 0.0 copy-start.5
  32.0 1.9 %collective-permute-start = (bf16[16,160,128]{2,1,0:T(8,128)(2,1)S(1)}, bf16[16,160,128]{2,1,0:T(8,128)(2,1)S(1)}, u32[]{:S(2)}, u32[]{:S(2)}) collective-permute-start(bf16[16,160,128]{2,1,0:T(8,128)(2,1)S(1)} %slice.73), channel_id=1, source_target_pairs={{0,16},{16,0},{1,17},{17,1},{2,18},{18,2},{3,19},{19,3},{4,20},{20... | collective-permute-start | bytes 1966088 | tf_op jit(solution)/shard_map/ppermute | solution.py:470
  33.9 2.1 %collective-permute-done.other_ref = bf16[16,160,128]{2,1,0:T(8,128)(2,1)S(1)} collective-permute-done((bf16[16,160,128]{2,1,0:T(8,128)(2,1)S(1)}, bf16[16,160,128]{2,1,0:T(8,128)(2,1)S(1)}, u32[]{:S(2)}, u32[]{:S(2)}) %collective-permute-start) | collective-permute-done | bytes 655392 | tf_op jit(solution)/shard_map/ppermute | solution.py:470
  36.0 0.0 copy-done.3
  36.0 0.0 copy-done.4
  36.0 0.0 copy-done.5
  36.0 4.0 %shard_map.94 = (bf16[2048,256]{1,0:T(8,128)(2,1)S(1)}, bf16[2048,128]{1,0:T(8,128)(2,1)S(1)}, bf16[1024,256]{1,0:T(8,128)(2,1)S(1)}, bf16[1024,128]{1,0:T(8,128)(2,1)S(1)}, f32[8,1024]{1,0:T(8,128)S(1)}) custom-call(s32[64]{0:T(128)S(1)} %copy-done.5, s32[8,64]{1,0:T(8,128)S(1)} %copy-done.4, s32[8,1024]{1,0:T(8,128)S(1)} %copy-done.3, ...), custom_call_target="tpu_custom_call" | custom-call | tf_op jit(solution)/shard_map/pallas_call | solution.py:435
  40.0 1.9 %collective-permute-start.1 = (f32[8,1024]{1,0:T(8,128)S(1)}, f32[8,1024]{1,0:T(8,128)S(1)}, u32[]{:S(2)}, u32[]{:S(2)}) collective-permute-start(f32[8,1024]{1,0:T(8,128)S(1)} %get-tuple-element.38.own_stats), channel_id=1, source_target_pairs={{0,128},{128,0},{256,384},{384,256},{1,129},{129,1},{257,385},{385... | collective-permute-start | bytes 98312 | tf_op jit(solution)/shard_map/ppermute | solution.py:470
  41.9 4.1 %collective-permute-done.1.other_stats = f32[8,1024]{1,0:T(8,128)S(1)} collective-permute-done((f32[8,1024]{1,0:T(8,128)S(1)}, f32[8,1024]{1,0:T(8,128)S(1)}, u32[]{:S(2)}, u32[]{:S(2)}) %collective-permute-start.1) | collective-permute-done | bytes 32800 | tf_op jit(solution)/shard_map/ppermute | solution.py:470
  46.1 6.9 %shard_map.95 = (bf16[16,256,128]{2,1,0:T(8,128)(2,1)S(1)}, bf16[16,160,128]{2,1,0:T(8,128)(2,1)S(1)}) custom-call(s32[64]{0:T(128)S(1)} %copy-done.5, s32[8,64]{1,0:T(8,128)S(1)} %copy-done.4, s32[8,1024]{1,0:T(8,128)S(1)} %copy-done.3, bf16[2048,256]{1,0:T(8,128)(2,1)S(1)} %get-tuple-element.34.keys, bf16[2048,128]{1,0:T(8,128)(2,1)S(1)} %get-tuple-element.35.values, ...), custom_call_target="tpu_custom_call" | custom-call | tf_op jit(solution)/shard_map/pallas_call | solution.py:450
  53.0 3.8 %collective-permute-start.2 = (bf16[16,160,128]{2,1,0:T(8,128)(2,1)S(1)}, bf16[16,160,128]{2,1,0:T(8,128)(2,1)S(1)}, u32[]{:S(2)}, u32[]{:S(2)}) collective-permute-start(bf16[16,160,128]{2,1,0:T(8,128)(2,1)S(1)} %get-tuple-element.40), channel_id=1, source_target_pairs={{0,16},{16,0},{1,17},{17,1},{2,18},{18,2},{3,19},{19,3},{4,20},{20... | collective-permute-start | bytes 1966088 | tf_op jit(solution)/shard_map/ppermute | solution.py:470
  56.8 1.7 %collective-permute-done.2 = bf16[16,160,128]{2,1,0:T(8,128)(2,1)S(1)} collective-permute-done((bf16[16,160,128]{2,1,0:T(8,128)(2,1)S(1)}, bf16[16,160,128]{2,1,0:T(8,128)(2,1)S(1)}, u32[]{:S(2)}, u32[]{:S(2)}) %collective-permute-start.2) | collective-permute-done | bytes 655392 | tf_op jit(solution)/shard_map/ppermute | solution.py:470
  58.5 0.3 add_dynamic-update-slice_fusion
  58.9 0.0 copy-start
  58.9 0.0 copy-start.1
  58.9 20.8 %all_to_all.21.slots_ref = bf16[16,256,128]{2,1,0:T(8,128)(2,1)S(1)} all-to-all(bf16[16,256,128]{2,1,0:T(8,128)(2,1)S(1)} %add_dynamic-update-slice_fusion), channel_id=1, replica_groups=mesh['y'=4,'x'=4,'core'=2,'head'=16] {'y','x'}, dimensions={0} | all-to-all | bytes 2097152 | tf_op jit(solution)/shard_map/all_to_all | solution.py:466
  79.6 0.0 copy-done
  79.6 0.0 copy-done.1
  79.7 0.0 copy-start.2
  79.7 1.2 shard_map.96
  80.8 0.0 copy-done.2
  80.8 1.2 shard_map.97
  82.0 1.9 %collective-permute-start.3 = (bf16[4,4,16,1024]{3,2,1,0:T(8,128)(2,1)S(1)}, bf16[4,4,16,1024]{3,2,1,0:T(8,128)(2,1)S(1)}, u32[]{:S(2)}, u32[]{:S(2)}) collective-permute-start(bf16[4,4,16,1024]{3,2,1,0:T(8,128)(2,1)S(1)} %get-tuple-element.45), channel_id=1, source_target_pairs={{0,16},{16,0},{1,17},{17,1},{2,18},{18,2},{3,19},{19,3},{4,20},{20... | collective-permute-start | bytes 1572872 | tf_op jit(solution)/shard_map/ppermute | solution.py:470
  83.9 15.2 %all-to-all-start.2 = ((bf16[16,8,640]{2,1,0:T(8,128)(2,1)}), bf16[16,8,640]{2,1,0:T(8,128)(2,1)S(1)}, u32[]{:S(2)}, u32[]{:S(2)}) async-start(bf16[16,8,640]{2,1,0:T(8,128)(2,1)} %bitcast.2), calls=%async_computation.2 | async-start | bytes 327680 | tf_op jit(solution)/shard_map/all_to_all | solution.py:506
  99.1 0.0 collective-permute-done.3
  99.1 0.2 add.33
  99.3 2.5 %collective-permute-start.4 = (bf16[4,16,1024]{2,1,0:T(8,128)(2,1)S(1)}, bf16[4,16,1024]{2,1,0:T(8,128)(2,1)S(1)}, u32[]{:S(2)}, u32[]{:S(2)}) collective-permute-start(bf16[4,16,1024]{2,1,0:T(8,128)(2,1)S(1)} %get-tuple-element.46), channel_id=1, source_target_pairs={{0,32},{32,0},{64,96},{96,64},{1,33},{33,1},{65,97},{97,65},{2,34}... | collective-permute-start | bytes 393224 | tf_op jit(solution)/shard_map/ppermute | solution.py:470
  101.8 3.3 %collective-permute-start.5 = (bf16[4,16,1024]{2,1,0:T(8,128)(2,1)S(1)}, bf16[4,16,1024]{2,1,0:T(8,128)(2,1)S(1)}, u32[]{:S(2)}, u32[]{:S(2)}) collective-permute-start(bf16[4,16,1024]{2,1,0:T(8,128)(2,1)S(1)} %get-tuple-element.48), channel_id=1, source_target_pairs={{0,64},{32,96},{64,0},{96,32},{1,65},{33,97},{65,1},{97,33},{2,66}... | collective-permute-start | bytes 393224 | tf_op jit(solution)/shard_map/ppermute | solution.py:470
  105.1 4.7 %collective-permute-start.6 = (bf16[4,16,1024]{2,1,0:T(8,128)(2,1)S(1)}, bf16[4,16,1024]{2,1,0:T(8,128)(2,1)S(1)}, u32[]{:S(2)}, u32[]{:S(2)}) collective-permute-start(bf16[4,16,1024]{2,1,0:T(8,128)(2,1)S(1)} %get-tuple-element.47), channel_id=1, source_target_pairs={{0,96},{32,64},{64,32},{96,0},{1,97},{33,65},{65,33},{97,1},{2,98}... | collective-permute-start | bytes 393224 | tf_op jit(solution)/shard_map/ppermute | solution.py:470
  109.8 0.1 constant_dynamic-slice_fusion
  109.9 0.1 copy.12.kv_ref
  110.0 4.5 %all-to-all-done.2.slots_ref = bf16[16,8,640]{2,1,0:T(8,128)(2,1)S(1)} async-done(((bf16[16,8,640]{2,1,0:T(8,128)(2,1)}), bf16[16,8,640]{2,1,0:T(8,128)(2,1)S(1)}, u32[]{:S(2)}, u32[]{:S(2)}) %all-to-all-start.2) | async-done | bytes 163872 | tf_op jit(solution)/shard_map/all_to_all | solution.py:506
  114.5 0.8 shard_map.98
  115.3 7.6 %all-to-all-start.3 = ((bf16[16,8,640]{2,1,0:T(8,128)(2,1)}), bf16[16,8,640]{2,1,0:T(8,128)(2,1)S(1)}, u32[]{:S(2)}, u32[]{:S(2)}) async-start(bf16[16,8,640]{2,1,0:T(8,128)(2,1)} %shard_map.98), calls=%async_computation.3 | async-start | bytes 327680 | tf_op jit(solution)/shard_map/all_to_all | solution.py:510
  122.9 0.0 collective-permute-done.4
  122.9 0.0 collective-permute-done.5
  122.9 0.0 collective-permute-done.6
  122.9 0.1 fusion.2
  123.0 1.9 %collective-permute-start.7 = (bf16[16,1024]{1,0:T(8,128)(2,1)S(1)}, bf16[16,1024]{1,0:T(8,128)(2,1)S(1)}, u32[]{:S(2)}, u32[]{:S(2)}) collective-permute-start(bf16[16,1024]{1,0:T(8,128)(2,1)S(1)} %get-tuple-element.49), channel_id=1, source_target_pairs={{0,128},{128,0},{256,384},{384,256},{1,129},{129,1},{257,385},{385... | collective-permute-start | bytes 98312 | tf_op jit(solution)/shard_map/ppermute | solution.py:470
  125.0 4.2 %collective-permute-start.8 = (bf16[16,1024]{1,0:T(8,128)(2,1)S(1)}, bf16[16,1024]{1,0:T(8,128)(2,1)S(1)}, u32[]{:S(2)}, u32[]{:S(2)}) collective-permute-start(bf16[16,1024]{1,0:T(8,128)(2,1)S(1)} %get-tuple-element.51), channel_id=1, source_target_pairs={{0,256},{128,384},{256,0},{384,128},{1,257},{129,385},{257,1},{385... | collective-permute-start | bytes 98312 | tf_op jit(solution)/shard_map/ppermute | solution.py:470
  129.2 4.3 %collective-permute-start.9 = (bf16[16,1024]{1,0:T(8,128)(2,1)S(1)}, bf16[16,1024]{1,0:T(8,128)(2,1)S(1)}, u32[]{:S(2)}, u32[]{:S(2)}) collective-permute-start(bf16[16,1024]{1,0:T(8,128)(2,1)S(1)} %get-tuple-element.50), channel_id=1, source_target_pairs={{0,384},{128,256},{256,128},{384,0},{1,385},{129,257},{257,129},{3... | collective-permute-start | bytes 98312 | tf_op jit(solution)/shard_map/ppermute | solution.py:470
  133.5 0.0 collective-permute-done.7
  133.5 0.0 collective-permute-done.8
  133.5 2.7 %collective-permute-done.9 = bf16[16,1024]{1,0:T(8,128)(2,1)S(1)} collective-permute-done((bf16[16,1024]{1,0:T(8,128)(2,1)S(1)}, bf16[16,1024]{1,0:T(8,128)(2,1)S(1)}, u32[]{:S(2)}, u32[]{:S(2)}) %collective-permute-start.9) | collective-permute-done | bytes 32800 | tf_op jit(solution)/shard_map/ppermute | solution.py:470
  136.2 0.6 fusion.5
  136.9 0.6 all-to-all-done.3
  137.5 0.1 copy.13
  137.6 0.7 convert_element_type.36
  (4 shorter events, 0.1 us)
Async XLA Ops:
  31.9 4.0 %copy-start.3 = (s32[8,1024]{1,0:T(8,128)S(1)}, s32[8,1024]{1,0:T(8,128)}, u32[]{:S(2)}) copy-start(s32[8,1024]{1,0:T(8,128)} %get-tuple-element.32.q_pos) | copy-start | bytes 98308
  31.9 4.0 %copy-start.4 = (s32[8,64]{1,0:T(8,128)S(1)}, s32[8,64]{1,0:T(8,128)}, u32[]{:S(2)}) copy-start(s32[8,64]{1,0:T(8,128)} %get-tuple-element.31.meta) | copy-start | bytes 6148
  31.9 4.0 %copy-start.5 = (s32[64]{0:T(128)S(1)}, s32[64]{0:T(128)}, u32[]{:S(2)}) copy-start(s32[64]{0:T(128)} %block_start.3) | copy-start | bytes 772
  32.0 4.0 %collective-permute-start = (bf16[16,160,128]{2,1,0:T(8,128)(2,1)S(1)}, bf16[16,160,128]{2,1,0:T(8,128)(2,1)S(1)}, u32[]{:S(2)}, u32[]{:S(2)}) collective-permute-start(bf16[16,160,128]{2,1,0:T(8,128)(2,1)S(1)} %slice.73), channel_id=1, source_target_pairs={{0,16},{16,0},{1,17},{17,1},{2,18},{18,2},{3,19},{19,3},{4,20},{20... | collective-permute-start | bytes 1966088 | tf_op jit(solution)/shard_map/ppermute | solution.py:470
  40.0 6.1 %collective-permute-start.1 = (f32[8,1024]{1,0:T(8,128)S(1)}, f32[8,1024]{1,0:T(8,128)S(1)}, u32[]{:S(2)}, u32[]{:S(2)}) collective-permute-start(f32[8,1024]{1,0:T(8,128)S(1)} %get-tuple-element.38.own_stats), channel_id=1, source_target_pairs={{0,128},{128,0},{256,384},{384,256},{1,129},{129,1},{257,385},{385... | collective-permute-start | bytes 98312 | tf_op jit(solution)/shard_map/ppermute | solution.py:470
  53.0 5.5 %collective-permute-start.2 = (bf16[16,160,128]{2,1,0:T(8,128)(2,1)S(1)}, bf16[16,160,128]{2,1,0:T(8,128)(2,1)S(1)}, u32[]{:S(2)}, u32[]{:S(2)}) collective-permute-start(bf16[16,160,128]{2,1,0:T(8,128)(2,1)S(1)} %get-tuple-element.40), channel_id=1, source_target_pairs={{0,16},{16,0},{1,17},{17,1},{2,18},{18,2},{3,19},{19,3},{4,20},{20... | collective-permute-start | bytes 1966088 | tf_op jit(solution)/shard_map/ppermute | solution.py:470
  58.9 20.8 %copy-start = (bf16[512,512]{1,0:T(8,128)(2,1)S(1)}, bf16[512,512]{1,0:T(8,128)(2,1)}, u32[]{:S(2)}) copy-start(bf16[512,512]{1,0:T(8,128)(2,1)} %wk_ref.1) | copy-start | bytes 1572868
  58.9 20.8 %copy-start.1 = (bf16[512,512]{1,0:T(8,128)(2,1)S(1)}, bf16[512,512]{1,0:T(8,128)(2,1)}, u32[]{:S(2)}) copy-start(bf16[512,512]{1,0:T(8,128)(2,1)} %wv_ref.1) | copy-start | bytes 1572868
  79.7 1.2 copy-start.2
  82.0 17.1 %collective-permute-start.3 = (bf16[4,4,16,1024]{3,2,1,0:T(8,128)(2,1)S(1)}, bf16[4,4,16,1024]{3,2,1,0:T(8,128)(2,1)S(1)}, u32[]{:S(2)}, u32[]{:S(2)}) collective-permute-start(bf16[4,4,16,1024]{3,2,1,0:T(8,128)(2,1)S(1)} %get-tuple-element.45), channel_id=1, source_target_pairs={{0,16},{16,0},{1,17},{17,1},{2,18},{18,2},{3,19},{19,3},{4,20},{20... | collective-permute-start | bytes 1572872 | tf_op jit(solution)/shard_map/ppermute | solution.py:470
  83.9 30.6 %all-to-all-start.2 = ((bf16[16,8,640]{2,1,0:T(8,128)(2,1)}), bf16[16,8,640]{2,1,0:T(8,128)(2,1)S(1)}, u32[]{:S(2)}, u32[]{:S(2)}) async-start(bf16[16,8,640]{2,1,0:T(8,128)(2,1)} %bitcast.2), calls=%async_computation.2 | async-start | bytes 327680 | tf_op jit(solution)/shard_map/all_to_all | solution.py:506
  99.3 23.6 %collective-permute-start.4 = (bf16[4,16,1024]{2,1,0:T(8,128)(2,1)S(1)}, bf16[4,16,1024]{2,1,0:T(8,128)(2,1)S(1)}, u32[]{:S(2)}, u32[]{:S(2)}) collective-permute-start(bf16[4,16,1024]{2,1,0:T(8,128)(2,1)S(1)} %get-tuple-element.46), channel_id=1, source_target_pairs={{0,32},{32,0},{64,96},{96,64},{1,33},{33,1},{65,97},{97,65},{2,34}... | collective-permute-start | bytes 393224 | tf_op jit(solution)/shard_map/ppermute | solution.py:470
  101.8 21.1 %collective-permute-start.5 = (bf16[4,16,1024]{2,1,0:T(8,128)(2,1)S(1)}, bf16[4,16,1024]{2,1,0:T(8,128)(2,1)S(1)}, u32[]{:S(2)}, u32[]{:S(2)}) collective-permute-start(bf16[4,16,1024]{2,1,0:T(8,128)(2,1)S(1)} %get-tuple-element.48), channel_id=1, source_target_pairs={{0,64},{32,96},{64,0},{96,32},{1,65},{33,97},{65,1},{97,33},{2,66}... | collective-permute-start | bytes 393224 | tf_op jit(solution)/shard_map/ppermute | solution.py:470
  105.1 17.8 %collective-permute-start.6 = (bf16[4,16,1024]{2,1,0:T(8,128)(2,1)S(1)}, bf16[4,16,1024]{2,1,0:T(8,128)(2,1)S(1)}, u32[]{:S(2)}, u32[]{:S(2)}) collective-permute-start(bf16[4,16,1024]{2,1,0:T(8,128)(2,1)S(1)} %get-tuple-element.47), channel_id=1, source_target_pairs={{0,96},{32,64},{64,32},{96,0},{1,97},{33,65},{65,33},{97,1},{2,98}... | collective-permute-start | bytes 393224 | tf_op jit(solution)/shard_map/ppermute | solution.py:470
  115.3 22.1 %all-to-all-start.3 = ((bf16[16,8,640]{2,1,0:T(8,128)(2,1)}), bf16[16,8,640]{2,1,0:T(8,128)(2,1)S(1)}, u32[]{:S(2)}, u32[]{:S(2)}) async-start(bf16[16,8,640]{2,1,0:T(8,128)(2,1)} %shard_map.98), calls=%async_computation.3 | async-start | bytes 327680 | tf_op jit(solution)/shard_map/all_to_all | solution.py:510
  123.0 10.4 %collective-permute-start.7 = (bf16[16,1024]{1,0:T(8,128)(2,1)S(1)}, bf16[16,1024]{1,0:T(8,128)(2,1)S(1)}, u32[]{:S(2)}, u32[]{:S(2)}) collective-permute-start(bf16[16,1024]{1,0:T(8,128)(2,1)S(1)} %get-tuple-element.49), channel_id=1, source_target_pairs={{0,128},{128,0},{256,384},{384,256},{1,129},{129,1},{257,385},{385... | collective-permute-start | bytes 98312 | tf_op jit(solution)/shard_map/ppermute | solution.py:470
  125.0 8.5 %collective-permute-start.8 = (bf16[16,1024]{1,0:T(8,128)(2,1)S(1)}, bf16[16,1024]{1,0:T(8,128)(2,1)S(1)}, u32[]{:S(2)}, u32[]{:S(2)}) collective-permute-start(bf16[16,1024]{1,0:T(8,128)(2,1)S(1)} %get-tuple-element.51), channel_id=1, source_target_pairs={{0,256},{128,384},{256,0},{384,128},{1,257},{129,385},{257,1},{385... | collective-permute-start | bytes 98312 | tf_op jit(solution)/shard_map/ppermute | solution.py:470
  129.2 7.0 %collective-permute-start.9 = (bf16[16,1024]{1,0:T(8,128)(2,1)S(1)}, bf16[16,1024]{1,0:T(8,128)(2,1)S(1)}, u32[]{:S(2)}, u32[]{:S(2)}) collective-permute-start(bf16[16,1024]{1,0:T(8,128)(2,1)S(1)} %get-tuple-element.50), channel_id=1, source_target_pairs={{0,384},{128,256},{256,128},{384,0},{1,385},{129,257},{257,129},{3... | collective-permute-start | bytes 98312 | tf_op jit(solution)/shard_map/ppermute | solution.py:470

commit v4 on v3

--- a/solution.py
+++ b/solution.py
@@ -180,22 +180,11 @@
     return (meta[2, group] * HALF + CHUNK - 1) // CHUNK
 
 
-def stats_kernel(
-    block_start, meta, q_pos, own_ref, other_ref, keys, values, queries, grads, stats, k_pos
-):
+def place_kernel(block_start, meta, own_ref, queries, grads, k_pos):
     core = lax.axis_index("core")
-    pad_key = jnp.zeros((HALF, HALF), bf16)
     pad = jnp.zeros((PIECE, HALF), bf16)
 
     def place(chip, carry):
-        for ref, side in ((own_ref, core), (other_ref, 1 - core)):
-            rank = meta[0, key_block(chip, side)]
-            at = pl.ds(pl.multiple_of(rank * HALF, HALF), HALF)
-            rope = ref[chip, 2 * HALF : KEY_ROWS]
-            rope = jnp.concatenate([rope[:, :HALF], rope[:, HALF:]], axis=0)
-            keys[at, :NOPE] = ref[chip, :HALF]
-            keys[at, NOPE:] = jnp.concatenate([rope, pad_key], axis=1)
-            values[at, :] = ref[chip, HALF : 2 * HALF]
         low = KEY_ROWS
         q_rope = own_ref[chip, low + 4 * PIECE : low + 5 * PIECE]
         for half in range(2):
@@ -211,6 +200,37 @@
     lax.fori_loop(0, CHIPS, place, 0, unroll=UNROLL)
     place_positions(block_start, meta, k_pos)
 
+
+def stats_kernel(
+    meta,
+    q_pos,
+    own_ref,
+    other_ref,
+    queries,
+    grads,
+    k_pos,
+    keys,
+    stats,
+    scores,
+    slopes,
+    values,
+):
+    core = lax.axis_index("core")
+    pad = jnp.zeros((HALF, HALF), bf16)
+
+    def place(chip, carry):
+        for ref, side in ((own_ref, core), (other_ref, 1 - core)):
+            rank = meta[0, key_block(chip, side)]
+            at = pl.ds(pl.multiple_of(rank * HALF, HALF), HALF)
+            rope = ref[chip, 2 * HALF : KEY_ROWS]
+            rope = jnp.concatenate([rope[:, :HALF], rope[:, HALF:]], axis=0)
+            keys[at, :NOPE] = ref[chip, :HALF]
+            keys[at, NOPE:] = jnp.concatenate([rope, pad], axis=1)
+            values[at, :] = ref[chip, HALF : 2 * HALF]
+        return carry
+
+    lax.fori_loop(0, CHIPS, place, 0, unroll=UNROLL)
+
     for group in range(N_GROUPS):
         lanes = slice(group * GROUP, (group + 1) * GROUP)
         q_group = queries[lanes, :]
@@ -224,6 +244,8 @@
             key_at = jnp.concatenate([k_pos[at, :]] * (GROUP // NOPE), axis=1)
             score = jnp.where(key_at <= q_at, score, masked_low)
             slope = dot(values[at, :], g_group, 1, 1)
+            scores[at, lanes] = score
+            slopes[at, lanes] = slope
             fresh = jnp.maximum(top, jnp.max(score, axis=0, keepdims=True))
             fade = jnp.exp2(top - fresh)
             weight = jnp.exp2(score - fresh)
@@ -244,25 +266,22 @@
 
 
 def gradient_kernel(
-    block_start,
     meta,
-    q_pos,
     keys,
-    values,
     queries,
     grads,
+    scores,
+    slopes,
     own_stats,
     other_stats,
     own_out,
     other_out,
-    k_pos,
     key_grads,
     value_grads,
     query_grads,
     key_sum,
     value_sum,
 ):
-    place_positions(block_start, meta, k_pos)
     own_top = own_stats[0:1, :]
     other_top = other_stats[0:1, :]
     top = jnp.maximum(own_top, other_top)
@@ -283,13 +302,9 @@
 
             @pl.when(index < seen_chunks(meta, group))
             def _(lanes=lanes):
-                score = dot(keys[at, :], queries[lanes, :], 1, 1) * (SCALE * LOG2E)
-                key_at = jnp.concatenate([k_pos[at, :]] * (GROUP // NOPE), axis=1)
-                visible = key_at <= q_pos[0:1, lanes]
-                score = jnp.where(visible, score - log_total[:, lanes], masked_low)
-                slope = dot(values[at, :], grads[lanes, :], 1, 1)
-                probs = jnp.exp2(score)
-                score_grad = (probs * ((slope - average[:, lanes]) * SCALE)).astype(bf16)
+                probs = jnp.exp2(scores[at, lanes] - log_total[:, lanes])
+                slope = (slopes[at, lanes] - average[:, lanes]) * SCALE
+                score_grad = (probs * slope).astype(bf16)
                 value_sum[...] += dot(probs.astype(bf16), grads[lanes, :])
                 key_sum[...] += dot(score_grad, queries[lanes, :])
                 query_grads[lanes, :] += dot(score_grad, keys[at, :], 0, 0)
@@ -340,7 +355,9 @@
     return jnp.concatenate(parts, axis=1)
 
 
-def latent_kernel(slots_ref, wk_ref, wv_ref, out_ref):
+def latent_kernel(
+    slots_ref, wk_ref, wv_ref, kv_ref, out_ref, grad_q_ref, own_ref, other_ref, terms
+):
     key_flat = head_sums(slots_ref, 0)
     value_flat = head_sums(slots_ref, HALF)
     latent = dot(key_flat, wk_ref[...], 1, 1) + dot(value_flat, wv_ref[...], 1, 1)
@@ -352,14 +369,11 @@
         ropes += [rope[:, :HALF], rope[:, HALF:]]
     rope = jnp.concatenate(ropes, axis=0)
     out_ref[:, LATENT:] = jnp.concatenate([rope, jnp.zeros_like(rope)], axis=1).astype(bf16)
-
-
-def projection_kernel(slots_ref, kv_ref, grad_q_ref, own_ref, other_ref, terms):
     values = kv_ref[:LATENT, :].astype(f32)
     inverse = lax.rsqrt(jnp.mean(values * values, axis=0, keepdims=True) + eps)
     normed = (values * inverse).astype(bf16)
-    terms[:, : HEADS * NOPE] = dot(normed, head_sums(slots_ref, 0)).astype(bf16)
-    terms[:, HEADS * NOPE :] = dot(normed, head_sums(slots_ref, HALF)).astype(bf16)
+    terms[:, : HEADS * NOPE] = dot(normed, key_flat).astype(bf16)
+    terms[:, HEADS * NOPE :] = dot(normed, value_flat).astype(bf16)
     core = lax.axis_index("core")
     y_here, x_here = lax.axis_index("y"), lax.axis_index("x")
     for dx in range(SIDE):
@@ -431,18 +445,29 @@
     )(*args)
 
 
+def run_place(*args):
+    return call(
+        place_kernel,
+        [((QUERIES, 2 * NOPE), bf16), ((QUERIES, VDIM), bf16), ((KEYS, NOPE), jnp.int32)],
+        [SMEM] * 2 + [VMEM],
+        limit=16,
+        flops=10**8,
+        moved=4 * 2**20,
+    )(*args)
+
+
 def run_stats(*args):
     return call(
         stats_kernel,
         [
             ((KEYS, 2 * NOPE), bf16),
-            ((KEYS, VDIM), bf16),
-            ((QUERIES, 2 * NOPE), bf16),
-            ((QUERIES, VDIM), bf16),
             ((8, QUERIES), f32),
+            ((KEYS, QUERIES), f32),
+            ((KEYS, QUERIES), f32),
         ],
-        [SMEM] * 2 + [VMEM] * 3,
-        [pltpu.VMEM((KEYS, NOPE), jnp.int32)],
+        [SMEM] + [VMEM] * 6,
+        [pltpu.VMEM((KEYS, VDIM), bf16)],
+        limit=28,
     )(*args)
 
 
@@ -450,15 +475,15 @@
     return call(
         gradient_kernel,
         [((CHIPS, OUT_ROWS, NOPE), bf16), ((CHIPS, KEY_ROWS, NOPE), bf16)],
-        [SMEM] * 2 + [VMEM] * 7,
+        [SMEM] + [VMEM] * 7,
         [
-            pltpu.VMEM((KEYS, NOPE), jnp.int32),
             pltpu.VMEM((KEYS, 2 * NOPE), bf16),
             pltpu.VMEM((KEYS, VDIM), bf16),
             pltpu.VMEM((QUERIES, 2 * NOPE), f32),
             pltpu.VMEM((CHUNK, 2 * NOPE), f32),
             pltpu.VMEM((CHUNK, VDIM), f32),
         ],
+        limit=28,
     )(*args)
 
 
@@ -480,22 +505,20 @@
     own = over_chips(slots)
     other = swap(own[:, :KEY_ROWS], "core", 1)
 
-    *placed, stats = run_stats(block_start, meta, q_pos, own, other)
+    queries, grads, k_pos = run_place(block_start, meta, own)
+    keys, stats, scores, slopes = run_stats(meta, q_pos, own, other, queries, grads, k_pos)
     own_part, other_part = run_gradient(
-        block_start, meta, q_pos, *placed, stats, swap(stats, "y", 1)
+        meta, keys, queries, grads, scores, slopes, stats, swap(stats, "y", 1)
     )
     slots = over_chips(own_part.at[:, :KEY_ROWS].add(swap(other_part, "core", 1)))
 
-    z_part = call(latent_kernel, [((ROWS, Z_WIDTH), bf16)], [VMEM] * 3)(slots, w_uk, w_uv)
-    z_part, slots = lax.optimization_barrier((z_part, slots))
-    grad_query, own_terms, other_terms = call(
-        projection_kernel,
-        [((ROWS, HEADS * WIDTH_Q), bf16)] + [((SIDE, SIDE, W_ROWS, W_WIDTH), bf16)] * 2,
-        [VMEM] * 2,
+    z_part, grad_query, own_terms, other_terms = call(
+        latent_kernel,
+        [((ROWS, Z_WIDTH), bf16), ((ROWS, HEADS * WIDTH_Q), bf16)]
+        + [((SIDE, SIDE, W_ROWS, W_WIDTH), bf16)] * 2,
+        [VMEM] * 4,
         [pltpu.VMEM((LATENT, W_WIDTH), bf16)],
-        flops=2 * ROWS * LATENT * W_WIDTH,
-        moved=8 * 2**20,
-    )(slots, kv_t)
+    )(slots, w_uk, w_uv, kv_t)
     terms = own_terms + swap(other_terms, "core", 1)
     for axis in ("x", "y"):
         total = terms[0].astype(f32)

time: 139 us -> 136 us (0.978)
  Pallas kernels: 18.4 us -> 16 us
  blocking collectives: 47.8 us -> 49.4 us
  waiting for transfers between devices: 15.7 us -> 14.2 us
    pallas_call x1, Pallas kernels: 6.92 us -> 4.78 us  [run_gradient(): call(gradient_kernel, [((CHIPS, OUT_ROWS, NOPE), bf16), ((CHIPS, KEY_ROWS...]
    all_to_all x2, blocking collectives: 47.8 us -> 49.4 us  [over_chips(): return lax.all_to_all(slots, ('y', 'x'), 0, 0)]
    ppermute x10, waiting for transfers between devices: 10.6 us -> 9.11 us  [swap(): lax.ppermute(array, axis, [(i, i ^ bit) for i in range(lax.axis_size(axis...]
where the time goes in v4:
time: 136 us; the launch traced here: 135 us
  starting transfers between devices  51.9 us (38%)
  blocking collectives  49.4 us (36%)
  Pallas kernels  16 us (12%)
  waiting for transfers between devices  14.2 us (10%)
    all_to_all x2, blocking collectives, over_chips(): return lax.all_to_all(slots, ('y', 'x'), 0, 0)  49.4 us
    ppermute x10, starting transfers between devices, swap(): lax.ppermute(array, axis, [(i, i ^ bit) for i in range(lax.axis_size(axis...  29.2 us
    all_to_all x1, starting transfers between devices, local(): lax.all_to_all(z_part.reshape(z_size, z_rows, Z_WIDTH), 'head', 0, 0)  15.2 us
    ppermute x10, waiting for transfers between devices, swap(): lax.ppermute(array, axis, [(i, i ^ bit) for i in range(lax.axis_size(axis...  9.11 us
    all_to_all x1, starting transfers between devices, local(): all_rows = lax.all_to_all(rows, 'head', 0, 0).reshape(ROWS, Z_WIDTH)  7.56 us
    pallas_call x1, Pallas kernels, run_gradient(): call(gradient_kernel, [((CHIPS, OUT_ROWS, NOPE), bf16), ((CHIPS, KEY_ROWS...  4.78 us
    all_to_all x1, waiting for transfers between devices, local(): lax.all_to_all(z_part.reshape(z_size, z_rows, Z_WIDTH), 'head', 0, 0)  4.5 us
    pallas_call x1, Pallas kernels, run_pack(): call(pack_kernel, [((CHIPS, IN_ROWS, NOPE), bf16), ((8, BLOCKS), jnp.int3...  4.28 us
  transfers between devices with their start and end apart: 12, of which 6 were waited for; matrix products, arithmetic and copies ran while one was open for 1% of the time, Pallas kernels for 1%

profile of v4, /device:TPU:32, one launch (start us, length us, event | category | flops | bytes accessed | tf_op | source)
XLA Modules:
  0.0 134.8 jit_solution(9458817926010076652)
XLA Ops:
  0.6 4.3 %shard_map.93 = (bf16[16,320,128]{2,1,0:T(8,128)(2,1)}, s32[8,64]{1,0:T(8,128)}, s32[8,1024]{1,0:T(8,128)}) custom-call(s32[1,64]{1,0:T(1,128)} %bitcast.29, bf16[576,128]{1,0:T(8,128)(2,1)} %bitcast.27, bf16[512,512]{1,0:T(8,128)(2,1)} %wk_ref.1, bf16[512,512]{1,0:T(8,128)(2,1)} %wv_ref.1, bf16[128,768]{1,0:T(8,128)(2,1)} %q_any.1, bf16[128,512]{1,0:T(8,128)(2,1)} %g_any.1), custom_call_target="tpu_custom_call" | custom-call | tf_op jit(solution)/shard_map/pallas_call | solution.py:425
  4.9 27.0 %all_to_all.20.own_ref = bf16[16,320,128]{2,1,0:T(8,128)(2,1)S(1)} all-to-all(bf16[16,320,128]{2,1,0:T(8,128)(2,1)} %get-tuple-element.34), channel_id=1, replica_groups=mesh['y'=4,'x'=4,'core'=2,'head'=16] {'y','x'}, dimensions={0} | all-to-all | bytes 2621440 | tf_op jit(solution)/shard_map/all_to_all | solution.py:491
  31.9 0.0 copy-start.3
  31.9 0.0 copy-start.5
  31.9 0.0 copy-start.4
  32.0 1.9 %collective-permute-start = (bf16[16,160,128]{2,1,0:T(8,128)(2,1)S(1)}, bf16[16,160,128]{2,1,0:T(8,128)(2,1)S(1)}, u32[]{:S(2)}, u32[]{:S(2)}) collective-permute-start(bf16[16,160,128]{2,1,0:T(8,128)(2,1)S(1)} %slice.73), channel_id=1, source_target_pairs={{0,16},{16,0},{1,17},{17,1},{2,18},{18,2},{3,19},{19,3},{4,20},{20... | collective-permute-start | bytes 1966088 | tf_op jit(solution)/shard_map/ppermute | solution.py:495
  33.9 0.0 copy-done.3
  33.9 0.0 copy-done.5
  33.9 0.9 shard_map.94
  34.9 1.1 collective-permute-done.other_ref
  36.0 0.0 copy-done.4
  36.0 3.6 %shard_map.95 = (bf16[2048,256]{1,0:T(8,128)(2,1)S(1)}, f32[8,1024]{1,0:T(8,128)S(1)}, f32[2048,1024]{1,0:T(8,128)S(1)}, f32[2048,1024]{1,0:T(8,128)S(1)}) custom-call(s32[8,64]{1,0:T(8,128)S(1)} %copy-done.3, s32[8,1024]{1,0:T(8,128)S(1)} %copy-done.4, bf16[16,320,128]{2,1,0:T(8,128)(2,1)S(1)} %all_to_all.20.own_ref, ...), custom_call_target="tpu_custom_call" | custom-call | tf_op jit(solution)/shard_map/pallas_call | solution.py:460
  39.6 2.6 %collective-permute-start.1 = (f32[8,1024]{1,0:T(8,128)S(1)}, f32[8,1024]{1,0:T(8,128)S(1)}, u32[]{:S(2)}, u32[]{:S(2)}) collective-permute-start(f32[8,1024]{1,0:T(8,128)S(1)} %get-tuple-element.41.own_stats), channel_id=1, source_target_pairs={{0,128},{128,0},{256,384},{384,256},{1,129},{129,1},{257,385},{385... | collective-permute-start | bytes 98312 | tf_op jit(solution)/shard_map/ppermute | solution.py:495
  42.2 3.2 %collective-permute-done.1.other_stats = f32[8,1024]{1,0:T(8,128)S(1)} collective-permute-done((f32[8,1024]{1,0:T(8,128)S(1)}, f32[8,1024]{1,0:T(8,128)S(1)}, u32[]{:S(2)}, u32[]{:S(2)}) %collective-permute-start.1) | collective-permute-done | bytes 32800 | tf_op jit(solution)/shard_map/ppermute | solution.py:495
  45.4 4.8 %shard_map.96 = (bf16[16,256,128]{2,1,0:T(8,128)(2,1)S(1)}, bf16[16,160,128]{2,1,0:T(8,128)(2,1)S(1)}) custom-call(s32[8,64]{1,0:T(8,128)S(1)} %copy-done.3, bf16[2048,256]{1,0:T(8,128)(2,1)S(1)} %get-tuple-element.38.keys, bf16[1024,256]{1,0:T(8,128)(2,1)S(1)} %get-tuple-element.35.queries, bf16[1024,128]{1,0:T(8,128)(2,1)S(1)} %get-tuple-element.36.grads, ...), custom_call_target="tpu_custom_call" | custom-call | tf_op jit(solution)/shard_map/pallas_call | solution.py:475
  50.2 1.9 %collective-permute-start.2 = (bf16[16,160,128]{2,1,0:T(8,128)(2,1)S(1)}, bf16[16,160,128]{2,1,0:T(8,128)(2,1)S(1)}, u32[]{:S(2)}, u32[]{:S(2)}) collective-permute-start(bf16[16,160,128]{2,1,0:T(8,128)(2,1)S(1)} %get-tuple-element.43), channel_id=1, source_target_pairs={{0,16},{16,0},{1,17},{17,1},{2,18},{18,2},{3,19},{19,3},{4,20},{20... | collective-permute-start | bytes 1966088 | tf_op jit(solution)/shard_map/ppermute | solution.py:495
  52.1 2.1 %collective-permute-done.2 = bf16[16,160,128]{2,1,0:T(8,128)(2,1)S(1)} collective-permute-done((bf16[16,160,128]{2,1,0:T(8,128)(2,1)S(1)}, bf16[16,160,128]{2,1,0:T(8,128)(2,1)S(1)}, u32[]{:S(2)}, u32[]{:S(2)}) %collective-permute-start.2) | collective-permute-done | bytes 655392 | tf_op jit(solution)/shard_map/ppermute | solution.py:495
  54.2 0.3 add_dynamic-update-slice_fusion
  54.5 0.0 copy-start
  54.5 0.0 copy-start.1
  54.5 0.0 copy-start.2
  54.6 22.4 %all_to_all.21.slots_ref = bf16[16,256,128]{2,1,0:T(8,128)(2,1)S(1)} all-to-all(bf16[16,256,128]{2,1,0:T(8,128)(2,1)S(1)} %add_dynamic-update-slice_fusion), channel_id=1, replica_groups=mesh['y'=4,'x'=4,'core'=2,'head'=16] {'y','x'}, dimensions={0} | all-to-all | bytes 2097152 | tf_op jit(solution)/shard_map/all_to_all | solution.py:491
  76.9 0.0 copy-done
  76.9 0.0 copy-done.1
  76.9 0.0 copy-done.2
  76.9 1.5 %shard_map.97 = (bf16[128,640]{1,0:T(8,128)(2,1)}, bf16[128,768]{1,0:T(8,128)(2,1)}, bf16[4,4,16,1024]{3,2,1,0:T(8,128)(2,1)S(1)}, bf16[4,4,16,1024]{3,2,1,0:T(8,128)(2,1)S(1)}) custom-call(bf16[16,256,128]{2,1,0:T(8,128)(2,1)S(1)} %all_to_all.21.slots_ref, bf16[512,512]{1,0:T(8,128)(2,1)S(1)} %copy-done, bf16[512,512]{1,0:T(8,128)(2,1)S(1)} %copy-done.1, ...), custom_call_target="tpu_custom_call" | custom-call | tf_op jit(solution)/shard_map/pallas_call | solution.py:515
  78.4 1.9 %collective-permute-start.3 = (bf16[4,4,16,1024]{3,2,1,0:T(8,128)(2,1)S(1)}, bf16[4,4,16,1024]{3,2,1,0:T(8,128)(2,1)S(1)}, u32[]{:S(2)}, u32[]{:S(2)}) collective-permute-start(bf16[4,4,16,1024]{3,2,1,0:T(8,128)(2,1)S(1)} %get-tuple-element.47), channel_id=1, source_target_pairs={{0,16},{16,0},{1,17},{17,1},{2,18},{18,2},{3,19},{19,3},{4,20},{20... | collective-permute-start | bytes 1572872 | tf_op jit(solution)/shard_map/ppermute | solution.py:495
  80.3 15.2 %all-to-all-start.2 = ((bf16[16,8,640]{2,1,0:T(8,128)(2,1)}), bf16[16,8,640]{2,1,0:T(8,128)(2,1)S(1)}, u32[]{:S(2)}, u32[]{:S(2)}) async-start(bf16[16,8,640]{2,1,0:T(8,128)(2,1)} %bitcast.2), calls=%async_computation.2 | async-start | bytes 327680 | tf_op jit(solution)/shard_map/all_to_all | solution.py:529
  95.5 0.0 collective-permute-done.3
  95.5 0.2 add.33
  95.8 2.5 %collective-permute-start.4 = (bf16[4,16,1024]{2,1,0:T(8,128)(2,1)S(1)}, bf16[4,16,1024]{2,1,0:T(8,128)(2,1)S(1)}, u32[]{:S(2)}, u32[]{:S(2)}) collective-permute-start(bf16[4,16,1024]{2,1,0:T(8,128)(2,1)S(1)} %get-tuple-element.48), channel_id=1, source_target_pairs={{0,32},{32,0},{64,96},{96,64},{1,33},{33,1},{65,97},{97,65},{2,34}... | collective-permute-start | bytes 393224 | tf_op jit(solution)/shard_map/ppermute | solution.py:495
  98.2 3.3 %collective-permute-start.5 = (bf16[4,16,1024]{2,1,0:T(8,128)(2,1)S(1)}, bf16[4,16,1024]{2,1,0:T(8,128)(2,1)S(1)}, u32[]{:S(2)}, u32[]{:S(2)}) collective-permute-start(bf16[4,16,1024]{2,1,0:T(8,128)(2,1)S(1)} %get-tuple-element.50), channel_id=1, source_target_pairs={{0,64},{32,96},{64,0},{96,32},{1,65},{33,97},{65,1},{97,33},{2,66}... | collective-permute-start | bytes 393224 | tf_op jit(solution)/shard_map/ppermute | solution.py:495
  101.6 4.6 %collective-permute-start.6 = (bf16[4,16,1024]{2,1,0:T(8,128)(2,1)S(1)}, bf16[4,16,1024]{2,1,0:T(8,128)(2,1)S(1)}, u32[]{:S(2)}, u32[]{:S(2)}) collective-permute-start(bf16[4,16,1024]{2,1,0:T(8,128)(2,1)S(1)} %get-tuple-element.49), channel_id=1, source_target_pairs={{0,96},{32,64},{64,32},{96,0},{1,97},{33,65},{65,33},{97,1},{2,98}... | collective-permute-start | bytes 393224 | tf_op jit(solution)/shard_map/ppermute | solution.py:495
  106.2 0.1 constant_dynamic-slice_fusion
  106.3 0.1 copy.12.kv_ref
  106.4 4.5 %all-to-all-done.2.slots_ref = bf16[16,8,640]{2,1,0:T(8,128)(2,1)S(1)} async-done(((bf16[16,8,640]{2,1,0:T(8,128)(2,1)}), bf16[16,8,640]{2,1,0:T(8,128)(2,1)S(1)}, u32[]{:S(2)}, u32[]{:S(2)}) %all-to-all-start.2) | async-done | bytes 163872 | tf_op jit(solution)/shard_map/all_to_all | solution.py:529
  110.9 0.8 shard_map.98
  111.8 7.6 %all-to-all-start.3 = ((bf16[16,8,640]{2,1,0:T(8,128)(2,1)}), bf16[16,8,640]{2,1,0:T(8,128)(2,1)S(1)}, u32[]{:S(2)}, u32[]{:S(2)}) async-start(bf16[16,8,640]{2,1,0:T(8,128)(2,1)} %shard_map.98), calls=%async_computation.3 | async-start | bytes 327680 | tf_op jit(solution)/shard_map/all_to_all | solution.py:533
  119.3 0.0 collective-permute-done.4
  119.3 0.0 collective-permute-done.5
  119.4 0.0 collective-permute-done.6
  119.4 0.1 fusion.2
  119.5 1.9 %collective-permute-start.7 = (bf16[16,1024]{1,0:T(8,128)(2,1)S(1)}, bf16[16,1024]{1,0:T(8,128)(2,1)S(1)}, u32[]{:S(2)}, u32[]{:S(2)}) collective-permute-start(bf16[16,1024]{1,0:T(8,128)(2,1)S(1)} %get-tuple-element.51), channel_id=1, source_target_pairs={{0,128},{128,0},{256,384},{384,256},{1,129},{129,1},{257,385},{385... | collective-permute-start | bytes 98312 | tf_op jit(solution)/shard_map/ppermute | solution.py:495
  121.4 4.2 %collective-permute-start.8 = (bf16[16,1024]{1,0:T(8,128)(2,1)S(1)}, bf16[16,1024]{1,0:T(8,128)(2,1)S(1)}, u32[]{:S(2)}, u32[]{:S(2)}) collective-permute-start(bf16[16,1024]{1,0:T(8,128)(2,1)S(1)} %get-tuple-element.53), channel_id=1, source_target_pairs={{0,256},{128,384},{256,0},{384,128},{1,257},{129,385},{257,1},{385... | collective-permute-start | bytes 98312 | tf_op jit(solution)/shard_map/ppermute | solution.py:495
  125.6 4.3 %collective-permute-start.9 = (bf16[16,1024]{1,0:T(8,128)(2,1)S(1)}, bf16[16,1024]{1,0:T(8,128)(2,1)S(1)}, u32[]{:S(2)}, u32[]{:S(2)}) collective-permute-start(bf16[16,1024]{1,0:T(8,128)(2,1)S(1)} %get-tuple-element.52), channel_id=1, source_target_pairs={{0,384},{128,256},{256,128},{384,0},{1,385},{129,257},{257,129},{3... | collective-permute-start | bytes 98312 | tf_op jit(solution)/shard_map/ppermute | solution.py:495
  129.9 0.0 collective-permute-done.7
  129.9 0.0 collective-permute-done.8
  129.9 2.7 %collective-permute-done.9 = bf16[16,1024]{1,0:T(8,128)(2,1)S(1)} collective-permute-done((bf16[16,1024]{1,0:T(8,128)(2,1)S(1)}, bf16[16,1024]{1,0:T(8,128)(2,1)S(1)}, u32[]{:S(2)}, u32[]{:S(2)}) %collective-permute-start.9) | collective-permute-done | bytes 32800 | tf_op jit(solution)/shard_map/ppermute | solution.py:495
  132.7 0.6 fusion.5
  133.3 0.6 all-to-all-done.3
  133.9 0.1 copy.13
  134.0 0.7 convert_element_type.36
  (4 shorter events, 0.1 us)
Async XLA Ops:
  31.9 2.0 %copy-start.3 = (s32[8,64]{1,0:T(8,128)S(1)}, s32[8,64]{1,0:T(8,128)}, u32[]{:S(2)}) copy-start(s32[8,64]{1,0:T(8,128)} %get-tuple-element.32.meta) | copy-start | bytes 6148
  31.9 2.0 %copy-start.5 = (s32[64]{0:T(128)S(1)}, s32[64]{0:T(128)}, u32[]{:S(2)}) copy-start(s32[64]{0:T(128)} %block_start.1) | copy-start | bytes 772
  31.9 4.0 %copy-start.4 = (s32[8,1024]{1,0:T(8,128)S(1)}, s32[8,1024]{1,0:T(8,128)}, u32[]{:S(2)}) copy-start(s32[8,1024]{1,0:T(8,128)} %get-tuple-element.33.q_pos) | copy-start | bytes 98308
  32.0 4.0 %collective-permute-start = (bf16[16,160,128]{2,1,0:T(8,128)(2,1)S(1)}, bf16[16,160,128]{2,1,0:T(8,128)(2,1)S(1)}, u32[]{:S(2)}, u32[]{:S(2)}) collective-permute-start(bf16[16,160,128]{2,1,0:T(8,128)(2,1)S(1)} %slice.73), channel_id=1, source_target_pairs={{0,16},{16,0},{1,17},{17,1},{2,18},{18,2},{3,19},{19,3},{4,20},{20... | collective-permute-start | bytes 1966088 | tf_op jit(solution)/shard_map/ppermute | solution.py:495
  39.6 5.8 %collective-permute-start.1 = (f32[8,1024]{1,0:T(8,128)S(1)}, f32[8,1024]{1,0:T(8,128)S(1)}, u32[]{:S(2)}, u32[]{:S(2)}) collective-permute-start(f32[8,1024]{1,0:T(8,128)S(1)} %get-tuple-element.41.own_stats), channel_id=1, source_target_pairs={{0,128},{128,0},{256,384},{384,256},{1,129},{129,1},{257,385},{385... | collective-permute-start | bytes 98312 | tf_op jit(solution)/shard_map/ppermute | solution.py:495
  50.2 4.0 %collective-permute-start.2 = (bf16[16,160,128]{2,1,0:T(8,128)(2,1)S(1)}, bf16[16,160,128]{2,1,0:T(8,128)(2,1)S(1)}, u32[]{:S(2)}, u32[]{:S(2)}) collective-permute-start(bf16[16,160,128]{2,1,0:T(8,128)(2,1)S(1)} %get-tuple-element.43), channel_id=1, source_target_pairs={{0,16},{16,0},{1,17},{17,1},{2,18},{18,2},{3,19},{19,3},{4,20},{20... | collective-permute-start | bytes 1966088 | tf_op jit(solution)/shard_map/ppermute | solution.py:495
  54.5 22.4 %copy-start = (bf16[512,512]{1,0:T(8,128)(2,1)S(1)}, bf16[512,512]{1,0:T(8,128)(2,1)}, u32[]{:S(2)}) copy-start(bf16[512,512]{1,0:T(8,128)(2,1)} %wk_ref.1) | copy-start | bytes 1572868
  54.5 22.4 %copy-start.1 = (bf16[512,512]{1,0:T(8,128)(2,1)S(1)}, bf16[512,512]{1,0:T(8,128)(2,1)}, u32[]{:S(2)}) copy-start(bf16[512,512]{1,0:T(8,128)(2,1)} %wv_ref.1) | copy-start | bytes 1572868
  54.5 22.4 %copy-start.2 = (bf16[128,576]{0,1:T(8,128)(2,1)S(1)}, bf16[128,576]{0,1:T(8,128)(2,1)}, u32[]{:S(2)}) copy-start(bf16[128,576]{0,1:T(8,128)(2,1)} %param.9) | copy-start | bytes 442372
  78.4 17.1 %collective-permute-start.3 = (bf16[4,4,16,1024]{3,2,1,0:T(8,128)(2,1)S(1)}, bf16[4,4,16,1024]{3,2,1,0:T(8,128)(2,1)S(1)}, u32[]{:S(2)}, u32[]{:S(2)}) collective-permute-start(bf16[4,4,16,1024]{3,2,1,0:T(8,128)(2,1)S(1)} %get-tuple-element.47), channel_id=1, source_target_pairs={{0,16},{16,0},{1,17},{17,1},{2,18},{18,2},{3,19},{19,3},{4,20},{20... | collective-permute-start | bytes 1572872 | tf_op jit(solution)/shard_map/ppermute | solution.py:495
  80.3 30.6 %all-to-all-start.2 = ((bf16[16,8,640]{2,1,0:T(8,128)(2,1)}), bf16[16,8,640]{2,1,0:T(8,128)(2,1)S(1)}, u32[]{:S(2)}, u32[]{:S(2)}) async-start(bf16[16,8,640]{2,1,0:T(8,128)(2,1)} %bitcast.2), calls=%async_computation.2 | async-start | bytes 327680 | tf_op jit(solution)/shard_map/all_to_all | solution.py:529
  95.8 23.6 %collective-permute-start.4 = (bf16[4,16,1024]{2,1,0:T(8,128)(2,1)S(1)}, bf16[4,16,1024]{2,1,0:T(8,128)(2,1)S(1)}, u32[]{:S(2)}, u32[]{:S(2)}) collective-permute-start(bf16[4,16,1024]{2,1,0:T(8,128)(2,1)S(1)} %get-tuple-element.48), channel_id=1, source_target_pairs={{0,32},{32,0},{64,96},{96,64},{1,33},{33,1},{65,97},{97,65},{2,34}... | collective-permute-start | bytes 393224 | tf_op jit(solution)/shard_map/ppermute | solution.py:495
  98.2 21.1 %collective-permute-start.5 = (bf16[4,16,1024]{2,1,0:T(8,128)(2,1)S(1)}, bf16[4,16,1024]{2,1,0:T(8,128)(2,1)S(1)}, u32[]{:S(2)}, u32[]{:S(2)}) collective-permute-start(bf16[4,16,1024]{2,1,0:T(8,128)(2,1)S(1)} %get-tuple-element.50), channel_id=1, source_target_pairs={{0,64},{32,96},{64,0},{96,32},{1,65},{33,97},{65,1},{97,33},{2,66}... | collective-permute-start | bytes 393224 | tf_op jit(solution)/shard_map/ppermute | solution.py:495
  101.6 17.8 %collective-permute-start.6 = (bf16[4,16,1024]{2,1,0:T(8,128)(2,1)S(1)}, bf16[4,16,1024]{2,1,0:T(8,128)(2,1)S(1)}, u32[]{:S(2)}, u32[]{:S(2)}) collective-permute-start(bf16[4,16,1024]{2,1,0:T(8,128)(2,1)S(1)} %get-tuple-element.49), channel_id=1, source_target_pairs={{0,96},{32,64},{64,32},{96,0},{1,97},{33,65},{65,33},{97,1},{2,98}... | collective-permute-start | bytes 393224 | tf_op jit(solution)/shard_map/ppermute | solution.py:495
  111.8 22.1 %all-to-all-start.3 = ((bf16[16,8,640]{2,1,0:T(8,128)(2,1)}), bf16[16,8,640]{2,1,0:T(8,128)(2,1)S(1)}, u32[]{:S(2)}, u32[]{:S(2)}) async-start(bf16[16,8,640]{2,1,0:T(8,128)(2,1)} %shard_map.98), calls=%async_computation.3 | async-start | bytes 327680 | tf_op jit(solution)/shard_map/all_to_all | solution.py:533
  119.5 10.4 %collective-permute-start.7 = (bf16[16,1024]{1,0:T(8,128)(2,1)S(1)}, bf16[16,1024]{1,0:T(8,128)(2,1)S(1)}, u32[]{:S(2)}, u32[]{:S(2)}) collective-permute-start(bf16[16,1024]{1,0:T(8,128)(2,1)S(1)} %get-tuple-element.51), channel_id=1, source_target_pairs={{0,128},{128,0},{256,384},{384,256},{1,129},{129,1},{257,385},{385... | collective-permute-start | bytes 98312 | tf_op jit(solution)/shard_map/ppermute | solution.py:495
  121.4 8.5 %collective-permute-start.8 = (bf16[16,1024]{1,0:T(8,128)(2,1)S(1)}, bf16[16,1024]{1,0:T(8,128)(2,1)S(1)}, u32[]{:S(2)}, u32[]{:S(2)}) collective-permute-start(bf16[16,1024]{1,0:T(8,128)(2,1)S(1)} %get-tuple-element.53), channel_id=1, source_target_pairs={{0,256},{128,384},{256,0},{384,128},{1,257},{129,385},{257,1},{385... | collective-permute-start | bytes 98312 | tf_op jit(solution)/shard_map/ppermute | solution.py:495
  125.6 7.0 %collective-permute-start.9 = (bf16[16,1024]{1,0:T(8,128)(2,1)S(1)}, bf16[16,1024]{1,0:T(8,128)(2,1)S(1)}, u32[]{:S(2)}, u32[]{:S(2)}) collective-permute-start(bf16[16,1024]{1,0:T(8,128)(2,1)S(1)} %get-tuple-element.52), channel_id=1, source_target_pairs={{0,384},{128,256},{256,128},{384,0},{1,385},{129,257},{257,129},{3... | collective-permute-start | bytes 98312 | tf_op jit(solution)/shard_map/ppermute | solution.py:495

commit v5 on v4

--- a/solution.py
+++ b/solution.py
@@ -134,6 +134,9 @@
             out_ref[slot, low + 4 * PIECE : low + 5 * PIECE] = jnp.concatenate(
                 [q_rope[first], q_rope[second]], axis=1
             )
+    part = (slice(None), pl.ds(KEY_ROWS, IN_ROWS - KEY_ROWS))
+    sent = [pltpu.make_async_copy(out_ref.at[part], out_any.at[part], out_sems.at[SIDE])]
+    sent[0].start()
     copies[2].wait()
     values = kv_ref[:LATENT, :].astype(f32)
     inverse = lax.rsqrt(jnp.mean(values * values, axis=0, keepdims=True) + eps)
@@ -143,7 +146,6 @@
     keys = dot(normed, wk_ref[...]).astype(bf16)
     copies[4].wait()
     values = dot(normed, wv_ref[...]).astype(bf16)
-    sent = []
     for y in range(SIDE):
         low = (y % 2) * HALF
         for x in range(HEADS):
@@ -153,7 +155,7 @@
             out_ref[slot, 2 * HALF : KEY_ROWS] = jnp.concatenate(
                 [rope[low : low + PIECE], rope[low + PIECE : low + HALF]], axis=1
             )
-        part = pl.ds(y * SIDE, SIDE)
+        part = (pl.ds(y * SIDE, SIDE), pl.ds(0, KEY_ROWS))
         sent.append(pltpu.make_async_copy(out_ref.at[part], out_any.at[part], out_sems.at[y]))
         sent[-1].start()
     for copy in sent:
@@ -176,8 +178,12 @@
     lax.fori_loop(0, 2 * CHIPS, body, 0, unroll=UNROLL)
 
 
-def seen_chunks(meta, group):
-    return (meta[2, group] * HALF + CHUNK - 1) // CHUNK
+def step_rows(group):
+    return CHUNK // 2 if group == 0 else CHUNK
+
+
+def seen_steps(meta, group):
+    return (meta[2, group] * HALF + step_rows(group) - 1) // step_rows(group)
 
 
 def place_kernel(block_start, meta, own_ref, queries, grads, k_pos):
@@ -237,9 +243,11 @@
         g_group = grads[lanes, :]
         q_at = q_pos[0:1, lanes]
 
-        def gather_stats(index, carry):
+        rows = step_rows(group)
+
+        def gather_stats(index, carry, lanes=lanes, rows=rows):
             top, weight_sum, weighted = carry
-            at = pl.ds(pl.multiple_of(index * CHUNK, CHUNK), CHUNK)
+            at = pl.ds(pl.multiple_of(index * rows, rows), rows)
             score = dot(keys[at, :], q_group, 1, 1) * (SCALE * LOG2E)
             key_at = jnp.concatenate([k_pos[at, :]] * (GROUP // NOPE), axis=1)
             score = jnp.where(key_at <= q_at, score, masked_low)
@@ -256,7 +264,7 @@
         zero = jnp.zeros((1, GROUP), f32)
         top, weight_sum, weighted = lax.fori_loop(
             0,
-            seen_chunks(meta, group),
+            seen_steps(meta, group),
             gather_stats,
             (jnp.full((1, GROUP), masked_low, f32), zero, zero),
         )
@@ -299,15 +307,19 @@
         value_sum[...] = jnp.zeros_like(value_sum)
         for group in range(N_GROUPS):
             lanes = slice(group * GROUP, (group + 1) * GROUP)
-
-            @pl.when(index < seen_chunks(meta, group))
-            def _(lanes=lanes):
-                probs = jnp.exp2(scores[at, lanes] - log_total[:, lanes])
-                slope = (slopes[at, lanes] - average[:, lanes]) * SCALE
-                score_grad = (probs * slope).astype(bf16)
-                value_sum[...] += dot(probs.astype(bf16), grads[lanes, :])
-                key_sum[...] += dot(score_grad, queries[lanes, :])
-                query_grads[lanes, :] += dot(score_grad, keys[at, :], 0, 0)
+            rows = step_rows(group)
+            for step in range(CHUNK // rows):
+
+                @pl.when(index * (CHUNK // rows) + step < seen_steps(meta, group))
+                def _(lanes=lanes, rows=rows, step=step):
+                    part = slice(step * rows, (step + 1) * rows)
+                    at = pl.ds(pl.multiple_of(index * CHUNK + step * rows, rows), rows)
+                    probs = jnp.exp2(scores[at, lanes] - log_total[:, lanes])
+                    slope = (slopes[at, lanes] - average[:, lanes]) * SCALE
+                    score_grad = (probs * slope).astype(bf16)
+                    value_sum[part, :] += dot(probs.astype(bf16), grads[lanes, :])
+                    key_sum[part, :] += dot(score_grad, queries[lanes, :])
+                    query_grads[lanes, :] += dot(score_grad, keys[at, :], 0, 0)
 
         key_grads[at, :] = key_sum[...].astype(bf16)
         value_grads[at, :] = value_sum[...].astype(bf16)
@@ -438,7 +450,7 @@
             pltpu.VMEM((ROWS, HEADS * VDIM), bf16),
             pltpu.VMEM((CHIPS, IN_ROWS, NOPE), bf16),
             pltpu.SemaphoreType.DMA((5,)),
-            pltpu.SemaphoreType.DMA((SIDE,)),
+            pltpu.SemaphoreType.DMA((SIDE + 1,)),
         ],
         limit=60,
         out_specs=[ANY, VMEM, VMEM],

time: 136 us -> 135 us (level)
  no operation moved by 1% of the time
where the time goes in v5:
time: 135 us; the launch traced here: 134 us
  starting transfers between devices  51.6 us (38%)
  blocking collectives  48.5 us (36%)
  Pallas kernels  16.1 us (12%)
  waiting for transfers between devices  14.6 us (11%)
    all_to_all x2, blocking collectives, over_chips(): return lax.all_to_all(slots, ('y', 'x'), 0, 0)  48.5 us
    ppermute x10, starting transfers between devices, swap(): lax.ppermute(array, axis, [(i, i ^ bit) for i in range(lax.axis_size(axis...  28.8 us
    all_to_all x1, starting transfers between devices, local(): lax.all_to_all(z_part.reshape(z_size, z_rows, Z_WIDTH), 'head', 0, 0)  15.2 us
    ppermute x10, waiting for transfers between devices, swap(): lax.ppermute(array, axis, [(i, i ^ bit) for i in range(lax.axis_size(axis...  9.48 us
    all_to_all x1, starting transfers between devices, local(): all_rows = lax.all_to_all(rows, 'head', 0, 0).reshape(ROWS, Z_WIDTH)  7.56 us
    pallas_call x1, Pallas kernels, run_gradient(): call(gradient_kernel, [((CHIPS, OUT_ROWS, NOPE), bf16), ((CHIPS, KEY_ROWS...  4.99 us
    all_to_all x1, waiting for transfers between devices, local(): lax.all_to_all(z_part.reshape(z_size, z_rows, Z_WIDTH), 'head', 0, 0)  4.5 us
    pallas_call x1, Pallas kernels, run_pack(): call(pack_kernel, [((CHIPS, IN_ROWS, NOPE), bf16), ((8, BLOCKS), jnp.int3...  4.07 us
  transfers between devices with their start and end apart: 12, of which 6 were waited for; matrix products, arithmetic and copies ran while one was open for 1% of the time, Pallas kernels for 1%

profile of v5, /device:TPU:32, one launch (start us, length us, event | category | flops | bytes accessed | tf_op | source)
XLA Modules:
  0.0 134.1 jit_solution(9104536965905082090)
XLA Ops:
  0.6 4.1 %shard_map.93 = (bf16[16,320,128]{2,1,0:T(8,128)(2,1)}, s32[8,64]{1,0:T(8,128)}, s32[8,1024]{1,0:T(8,128)}) custom-call(s32[1,64]{1,0:T(1,128)} %bitcast.29, bf16[576,128]{1,0:T(8,128)(2,1)} %bitcast.27, bf16[512,512]{1,0:T(8,128)(2,1)} %wk_ref.1, bf16[512,512]{1,0:T(8,128)(2,1)} %wv_ref.1, bf16[128,768]{1,0:T(8,128)(2,1)} %q_any.1, bf16[128,512]{1,0:T(8,128)(2,1)} %g_any.1), custom_call_target="tpu_custom_call" | custom-call | tf_op jit(solution)/shard_map/pallas_call | solution.py:437
  4.7 27.0 %all_to_all.20.own_ref = bf16[16,320,128]{2,1,0:T(8,128)(2,1)S(1)} all-to-all(bf16[16,320,128]{2,1,0:T(8,128)(2,1)} %get-tuple-element.34), channel_id=1, replica_groups=mesh['y'=4,'x'=4,'core'=2,'head'=16] {'y','x'}, dimensions={0} | all-to-all | bytes 2621440 | tf_op jit(solution)/shard_map/all_to_all | solution.py:503
  31.7 0.0 copy-start.3
  31.7 0.0 copy-start.5
  31.7 0.0 copy-start.4
  31.8 1.9 %collective-permute-start = (bf16[16,160,128]{2,1,0:T(8,128)(2,1)S(1)}, bf16[16,160,128]{2,1,0:T(8,128)(2,1)S(1)}, u32[]{:S(2)}, u32[]{:S(2)}) collective-permute-start(bf16[16,160,128]{2,1,0:T(8,128)(2,1)S(1)} %slice.73), channel_id=1, source_target_pairs={{0,16},{16,0},{1,17},{17,1},{2,18},{18,2},{3,19},{19,3},{4,20},{20... | collective-permute-start | bytes 1966088 | tf_op jit(solution)/shard_map/ppermute | solution.py:507
  33.7 0.0 copy-done.3
  33.7 0.0 copy-done.5
  33.7 0.9 shard_map.94
  34.7 1.1 collective-permute-done.other_ref
  35.8 0.0 copy-done.4
  35.8 3.8 %shard_map.95 = (bf16[2048,256]{1,0:T(8,128)(2,1)S(1)}, f32[8,1024]{1,0:T(8,128)S(1)}, f32[2048,1024]{1,0:T(8,128)S(1)}, f32[2048,1024]{1,0:T(8,128)S(1)}) custom-call(s32[8,64]{1,0:T(8,128)S(1)} %copy-done.3, s32[8,1024]{1,0:T(8,128)S(1)} %copy-done.4, bf16[16,320,128]{2,1,0:T(8,128)(2,1)S(1)} %all_to_all.20.own_ref, ...), custom_call_target="tpu_custom_call" | custom-call | tf_op jit(solution)/shard_map/pallas_call | solution.py:472
  39.6 2.2 %collective-permute-start.1 = (f32[8,1024]{1,0:T(8,128)S(1)}, f32[8,1024]{1,0:T(8,128)S(1)}, u32[]{:S(2)}, u32[]{:S(2)}) collective-permute-start(f32[8,1024]{1,0:T(8,128)S(1)} %get-tuple-element.41.own_stats), channel_id=1, source_target_pairs={{0,128},{128,0},{256,384},{384,256},{1,129},{129,1},{257,385},{385... | collective-permute-start | bytes 98312 | tf_op jit(solution)/shard_map/ppermute | solution.py:507
  41.8 3.6 %collective-permute-done.1.other_stats = f32[8,1024]{1,0:T(8,128)S(1)} collective-permute-done((f32[8,1024]{1,0:T(8,128)S(1)}, f32[8,1024]{1,0:T(8,128)S(1)}, u32[]{:S(2)}, u32[]{:S(2)}) %collective-permute-start.1) | collective-permute-done | bytes 32800 | tf_op jit(solution)/shard_map/ppermute | solution.py:507
  45.4 5.0 %shard_map.96 = (bf16[16,256,128]{2,1,0:T(8,128)(2,1)S(1)}, bf16[16,160,128]{2,1,0:T(8,128)(2,1)S(1)}) custom-call(s32[8,64]{1,0:T(8,128)S(1)} %copy-done.3, bf16[2048,256]{1,0:T(8,128)(2,1)S(1)} %get-tuple-element.38.keys, bf16[1024,256]{1,0:T(8,128)(2,1)S(1)} %get-tuple-element.35.queries, bf16[1024,128]{1,0:T(8,128)(2,1)S(1)} %get-tuple-element.36.grads, ...), custom_call_target="tpu_custom_call" | custom-call | tf_op jit(solution)/shard_map/pallas_call | solution.py:487
  50.4 1.9 %collective-permute-start.2 = (bf16[16,160,128]{2,1,0:T(8,128)(2,1)S(1)}, bf16[16,160,128]{2,1,0:T(8,128)(2,1)S(1)}, u32[]{:S(2)}, u32[]{:S(2)}) collective-permute-start(bf16[16,160,128]{2,1,0:T(8,128)(2,1)S(1)} %get-tuple-element.43), channel_id=1, source_target_pairs={{0,16},{16,0},{1,17},{17,1},{2,18},{18,2},{3,19},{19,3},{4,20},{20... | collective-permute-start | bytes 1966088 | tf_op jit(solution)/shard_map/ppermute | solution.py:507
  52.3 2.1 %collective-permute-done.2 = bf16[16,160,128]{2,1,0:T(8,128)(2,1)S(1)} collective-permute-done((bf16[16,160,128]{2,1,0:T(8,128)(2,1)S(1)}, bf16[16,160,128]{2,1,0:T(8,128)(2,1)S(1)}, u32[]{:S(2)}, u32[]{:S(2)}) %collective-permute-start.2) | collective-permute-done | bytes 655392 | tf_op jit(solution)/shard_map/ppermute | solution.py:507
  54.4 0.3 add_dynamic-update-slice_fusion
  54.7 0.0 copy-start
  54.7 0.0 copy-start.1
  54.7 0.0 copy-start.2
  54.7 21.5 %all_to_all.21.slots_ref = bf16[16,256,128]{2,1,0:T(8,128)(2,1)S(1)} all-to-all(bf16[16,256,128]{2,1,0:T(8,128)(2,1)S(1)} %add_dynamic-update-slice_fusion), channel_id=1, replica_groups=mesh['y'=4,'x'=4,'core'=2,'head'=16] {'y','x'}, dimensions={0} | all-to-all | bytes 2097152 | tf_op jit(solution)/shard_map/all_to_all | solution.py:503
  76.3 0.0 copy-done
  76.3 0.0 copy-done.1
  76.3 0.0 copy-done.2
  76.3 1.5 %shard_map.97 = (bf16[128,640]{1,0:T(8,128)(2,1)}, bf16[128,768]{1,0:T(8,128)(2,1)}, bf16[4,4,16,1024]{3,2,1,0:T(8,128)(2,1)S(1)}, bf16[4,4,16,1024]{3,2,1,0:T(8,128)(2,1)S(1)}) custom-call(bf16[16,256,128]{2,1,0:T(8,128)(2,1)S(1)} %all_to_all.21.slots_ref, bf16[512,512]{1,0:T(8,128)(2,1)S(1)} %copy-done, bf16[512,512]{1,0:T(8,128)(2,1)S(1)} %copy-done.1, ...), custom_call_target="tpu_custom_call" | custom-call | tf_op jit(solution)/shard_map/pallas_call | solution.py:527
  77.7 1.9 %collective-permute-start.3 = (bf16[4,4,16,1024]{3,2,1,0:T(8,128)(2,1)S(1)}, bf16[4,4,16,1024]{3,2,1,0:T(8,128)(2,1)S(1)}, u32[]{:S(2)}, u32[]{:S(2)}) collective-permute-start(bf16[4,4,16,1024]{3,2,1,0:T(8,128)(2,1)S(1)} %get-tuple-element.47), channel_id=1, source_target_pairs={{0,16},{16,0},{1,17},{17,1},{2,18},{18,2},{3,19},{19,3},{4,20},{20... | collective-permute-start | bytes 1572872 | tf_op jit(solution)/shard_map/ppermute | solution.py:507
  79.7 15.2 %all-to-all-start.2 = ((bf16[16,8,640]{2,1,0:T(8,128)(2,1)}), bf16[16,8,640]{2,1,0:T(8,128)(2,1)S(1)}, u32[]{:S(2)}, u32[]{:S(2)}) async-start(bf16[16,8,640]{2,1,0:T(8,128)(2,1)} %bitcast.2), calls=%async_computation.2 | async-start | bytes 327680 | tf_op jit(solution)/shard_map/all_to_all | solution.py:541
  94.9 0.0 collective-permute-done.3
  94.9 0.2 add.33
  95.1 2.5 %collective-permute-start.4 = (bf16[4,16,1024]{2,1,0:T(8,128)(2,1)S(1)}, bf16[4,16,1024]{2,1,0:T(8,128)(2,1)S(1)}, u32[]{:S(2)}, u32[]{:S(2)}) collective-permute-start(bf16[4,16,1024]{2,1,0:T(8,128)(2,1)S(1)} %get-tuple-element.48), channel_id=1, source_target_pairs={{0,32},{32,0},{64,96},{96,64},{1,33},{33,1},{65,97},{97,65},{2,34}... | collective-permute-start | bytes 393224 | tf_op jit(solution)/shard_map/ppermute | solution.py:507
  97.6 3.3 %collective-permute-start.5 = (bf16[4,16,1024]{2,1,0:T(8,128)(2,1)S(1)}, bf16[4,16,1024]{2,1,0:T(8,128)(2,1)S(1)}, u32[]{:S(2)}, u32[]{:S(2)}) collective-permute-start(bf16[4,16,1024]{2,1,0:T(8,128)(2,1)S(1)} %get-tuple-element.50), channel_id=1, source_target_pairs={{0,64},{32,96},{64,0},{96,32},{1,65},{33,97},{65,1},{97,33},{2,66}... | collective-permute-start | bytes 393224 | tf_op jit(solution)/shard_map/ppermute | solution.py:507
  100.9 4.6 %collective-permute-start.6 = (bf16[4,16,1024]{2,1,0:T(8,128)(2,1)S(1)}, bf16[4,16,1024]{2,1,0:T(8,128)(2,1)S(1)}, u32[]{:S(2)}, u32[]{:S(2)}) collective-permute-start(bf16[4,16,1024]{2,1,0:T(8,128)(2,1)S(1)} %get-tuple-element.49), channel_id=1, source_target_pairs={{0,96},{32,64},{64,32},{96,0},{1,97},{33,65},{65,33},{97,1},{2,98}... | collective-permute-start | bytes 393224 | tf_op jit(solution)/shard_map/ppermute | solution.py:507
  105.6 0.1 constant_dynamic-slice_fusion
  105.7 0.1 copy.12.kv_ref
  105.8 4.5 %all-to-all-done.2.slots_ref = bf16[16,8,640]{2,1,0:T(8,128)(2,1)S(1)} async-done(((bf16[16,8,640]{2,1,0:T(8,128)(2,1)}), bf16[16,8,640]{2,1,0:T(8,128)(2,1)S(1)}, u32[]{:S(2)}, u32[]{:S(2)}) %all-to-all-start.2) | async-done | bytes 163872 | tf_op jit(solution)/shard_map/all_to_all | solution.py:541
  110.3 0.8 shard_map.98
  111.1 7.6 %all-to-all-start.3 = ((bf16[16,8,640]{2,1,0:T(8,128)(2,1)}), bf16[16,8,640]{2,1,0:T(8,128)(2,1)S(1)}, u32[]{:S(2)}, u32[]{:S(2)}) async-start(bf16[16,8,640]{2,1,0:T(8,128)(2,1)} %shard_map.98), calls=%async_computation.3 | async-start | bytes 327680 | tf_op jit(solution)/shard_map/all_to_all | solution.py:545
  118.7 0.0 collective-permute-done.4
  118.7 0.0 collective-permute-done.5
  118.7 0.0 collective-permute-done.6
  118.7 0.1 fusion.2
  118.8 1.9 %collective-permute-start.7 = (bf16[16,1024]{1,0:T(8,128)(2,1)S(1)}, bf16[16,1024]{1,0:T(8,128)(2,1)S(1)}, u32[]{:S(2)}, u32[]{:S(2)}) collective-permute-start(bf16[16,1024]{1,0:T(8,128)(2,1)S(1)} %get-tuple-element.51), channel_id=1, source_target_pairs={{0,128},{128,0},{256,384},{384,256},{1,129},{129,1},{257,385},{385... | collective-permute-start | bytes 98312 | tf_op jit(solution)/shard_map/ppermute | solution.py:507
  120.7 4.2 %collective-permute-start.8 = (bf16[16,1024]{1,0:T(8,128)(2,1)S(1)}, bf16[16,1024]{1,0:T(8,128)(2,1)S(1)}, u32[]{:S(2)}, u32[]{:S(2)}) collective-permute-start(bf16[16,1024]{1,0:T(8,128)(2,1)S(1)} %get-tuple-element.53), channel_id=1, source_target_pairs={{0,256},{128,384},{256,0},{384,128},{1,257},{129,385},{257,1},{385... | collective-permute-start | bytes 98312 | tf_op jit(solution)/shard_map/ppermute | solution.py:507
  125.0 4.3 %collective-permute-start.9 = (bf16[16,1024]{1,0:T(8,128)(2,1)S(1)}, bf16[16,1024]{1,0:T(8,128)(2,1)S(1)}, u32[]{:S(2)}, u32[]{:S(2)}) collective-permute-start(bf16[16,1024]{1,0:T(8,128)(2,1)S(1)} %get-tuple-element.52), channel_id=1, source_target_pairs={{0,384},{128,256},{256,128},{384,0},{1,385},{129,257},{257,129},{3... | collective-permute-start | bytes 98312 | tf_op jit(solution)/shard_map/ppermute | solution.py:507
  129.3 0.0 collective-permute-done.7
  129.3 0.0 collective-permute-done.8
  129.3 2.7 %collective-permute-done.9 = bf16[16,1024]{1,0:T(8,128)(2,1)S(1)} collective-permute-done((bf16[16,1024]{1,0:T(8,128)(2,1)S(1)}, bf16[16,1024]{1,0:T(8,128)(2,1)S(1)}, u32[]{:S(2)}, u32[]{:S(2)}) %collective-permute-start.9) | collective-permute-done | bytes 32800 | tf_op jit(solution)/shard_map/ppermute | solution.py:507
  132.0 0.6 fusion.5
  132.6 0.6 all-to-all-done.3
  133.2 0.1 copy.13
  133.4 0.7 convert_element_type.36
  (4 shorter events, 0.1 us)
Async XLA Ops:
  31.7 2.0 %copy-start.3 = (s32[8,64]{1,0:T(8,128)S(1)}, s32[8,64]{1,0:T(8,128)}, u32[]{:S(2)}) copy-start(s32[8,64]{1,0:T(8,128)} %get-tuple-element.32.meta) | copy-start | bytes 6148
  31.7 2.0 %copy-start.5 = (s32[64]{0:T(128)S(1)}, s32[64]{0:T(128)}, u32[]{:S(2)}) copy-start(s32[64]{0:T(128)} %block_start.1) | copy-start | bytes 772
  31.7 4.0 %copy-start.4 = (s32[8,1024]{1,0:T(8,128)S(1)}, s32[8,1024]{1,0:T(8,128)}, u32[]{:S(2)}) copy-start(s32[8,1024]{1,0:T(8,128)} %get-tuple-element.33.q_pos) | copy-start | bytes 98308
  31.8 4.0 %collective-permute-start = (bf16[16,160,128]{2,1,0:T(8,128)(2,1)S(1)}, bf16[16,160,128]{2,1,0:T(8,128)(2,1)S(1)}, u32[]{:S(2)}, u32[]{:S(2)}) collective-permute-start(bf16[16,160,128]{2,1,0:T(8,128)(2,1)S(1)} %slice.73), channel_id=1, source_target_pairs={{0,16},{16,0},{1,17},{17,1},{2,18},{18,2},{3,19},{19,3},{4,20},{20... | collective-permute-start | bytes 1966088 | tf_op jit(solution)/shard_map/ppermute | solution.py:507
  39.6 5.8 %collective-permute-start.1 = (f32[8,1024]{1,0:T(8,128)S(1)}, f32[8,1024]{1,0:T(8,128)S(1)}, u32[]{:S(2)}, u32[]{:S(2)}) collective-permute-start(f32[8,1024]{1,0:T(8,128)S(1)} %get-tuple-element.41.own_stats), channel_id=1, source_target_pairs={{0,128},{128,0},{256,384},{384,256},{1,129},{129,1},{257,385},{385... | collective-permute-start | bytes 98312 | tf_op jit(solution)/shard_map/ppermute | solution.py:507
  50.4 4.0 %collective-permute-start.2 = (bf16[16,160,128]{2,1,0:T(8,128)(2,1)S(1)}, bf16[16,160,128]{2,1,0:T(8,128)(2,1)S(1)}, u32[]{:S(2)}, u32[]{:S(2)}) collective-permute-start(bf16[16,160,128]{2,1,0:T(8,128)(2,1)S(1)} %get-tuple-element.43), channel_id=1, source_target_pairs={{0,16},{16,0},{1,17},{17,1},{2,18},{18,2},{3,19},{19,3},{4,20},{20... | collective-permute-start | bytes 1966088 | tf_op jit(solution)/shard_map/ppermute | solution.py:507
  54.7 21.6 %copy-start = (bf16[512,512]{1,0:T(8,128)(2,1)S(1)}, bf16[512,512]{1,0:T(8,128)(2,1)}, u32[]{:S(2)}) copy-start(bf16[512,512]{1,0:T(8,128)(2,1)} %wk_ref.1) | copy-start | bytes 1572868
  54.7 21.6 %copy-start.1 = (bf16[512,512]{1,0:T(8,128)(2,1)S(1)}, bf16[512,512]{1,0:T(8,128)(2,1)}, u32[]{:S(2)}) copy-start(bf16[512,512]{1,0:T(8,128)(2,1)} %wv_ref.1) | copy-start | bytes 1572868
  54.7 21.5 %copy-start.2 = (bf16[128,576]{0,1:T(8,128)(2,1)S(1)}, bf16[128,576]{0,1:T(8,128)(2,1)}, u32[]{:S(2)}) copy-start(bf16[128,576]{0,1:T(8,128)(2,1)} %param.9) | copy-start | bytes 442372
  77.7 17.1 %collective-permute-start.3 = (bf16[4,4,16,1024]{3,2,1,0:T(8,128)(2,1)S(1)}, bf16[4,4,16,1024]{3,2,1,0:T(8,128)(2,1)S(1)}, u32[]{:S(2)}, u32[]{:S(2)}) collective-permute-start(bf16[4,4,16,1024]{3,2,1,0:T(8,128)(2,1)S(1)} %get-tuple-element.47), channel_id=1, source_target_pairs={{0,16},{16,0},{1,17},{17,1},{2,18},{18,2},{3,19},{19,3},{4,20},{20... | collective-permute-start | bytes 1572872 | tf_op jit(solution)/shard_map/ppermute | solution.py:507
  79.7 30.6 %all-to-all-start.2 = ((bf16[16,8,640]{2,1,0:T(8,128)(2,1)}), bf16[16,8,640]{2,1,0:T(8,128)(2,1)S(1)}, u32[]{:S(2)}, u32[]{:S(2)}) async-start(bf16[16,8,640]{2,1,0:T(8,128)(2,1)} %bitcast.2), calls=%async_computation.2 | async-start | bytes 327680 | tf_op jit(solution)/shard_map/all_to_all | solution.py:541
  95.1 23.6 %collective-permute-start.4 = (bf16[4,16,1024]{2,1,0:T(8,128)(2,1)S(1)}, bf16[4,16,1024]{2,1,0:T(8,128)(2,1)S(1)}, u32[]{:S(2)}, u32[]{:S(2)}) collective-permute-start(bf16[4,16,1024]{2,1,0:T(8,128)(2,1)S(1)} %get-tuple-element.48), channel_id=1, source_target_pairs={{0,32},{32,0},{64,96},{96,64},{1,33},{33,1},{65,97},{97,65},{2,34}... | collective-permute-start | bytes 393224 | tf_op jit(solution)/shard_map/ppermute | solution.py:507
  97.6 21.1 %collective-permute-start.5 = (bf16[4,16,1024]{2,1,0:T(8,128)(2,1)S(1)}, bf16[4,16,1024]{2,1,0:T(8,128)(2,1)S(1)}, u32[]{:S(2)}, u32[]{:S(2)}) collective-permute-start(bf16[4,16,1024]{2,1,0:T(8,128)(2,1)S(1)} %get-tuple-element.50), channel_id=1, source_target_pairs={{0,64},{32,96},{64,0},{96,32},{1,65},{33,97},{65,1},{97,33},{2,66}... | collective-permute-start | bytes 393224 | tf_op jit(solution)/shard_map/ppermute | solution.py:507
  100.9 17.8 %collective-permute-start.6 = (bf16[4,16,1024]{2,1,0:T(8,128)(2,1)S(1)}, bf16[4,16,1024]{2,1,0:T(8,128)(2,1)S(1)}, u32[]{:S(2)}, u32[]{:S(2)}) collective-permute-start(bf16[4,16,1024]{2,1,0:T(8,128)(2,1)S(1)} %get-tuple-element.49), channel_id=1, source_target_pairs={{0,96},{32,64},{64,32},{96,0},{1,97},{33,65},{65,33},{97,1},{2,98}... | collective-permute-start | bytes 393224 | tf_op jit(solution)/shard_map/ppermute | solution.py:507
  111.1 22.1 %all-to-all-start.3 = ((bf16[16,8,640]{2,1,0:T(8,128)(2,1)}), bf16[16,8,640]{2,1,0:T(8,128)(2,1)S(1)}, u32[]{:S(2)}, u32[]{:S(2)}) async-start(bf16[16,8,640]{2,1,0:T(8,128)(2,1)} %shard_map.98), calls=%async_computation.3 | async-start | bytes 327680 | tf_op jit(solution)/shard_map/all_to_all | solution.py:545
  118.8 10.4 %collective-permute-start.7 = (bf16[16,1024]{1,0:T(8,128)(2,1)S(1)}, bf16[16,1024]{1,0:T(8,128)(2,1)S(1)}, u32[]{:S(2)}, u32[]{:S(2)}) collective-permute-start(bf16[16,1024]{1,0:T(8,128)(2,1)S(1)} %get-tuple-element.51), channel_id=1, source_target_pairs={{0,128},{128,0},{256,384},{384,256},{1,129},{129,1},{257,385},{385... | collective-permute-start | bytes 98312 | tf_op jit(solution)/shard_map/ppermute | solution.py:507
  120.7 8.5 %collective-permute-start.8 = (bf16[16,1024]{1,0:T(8,128)(2,1)S(1)}, bf16[16,1024]{1,0:T(8,128)(2,1)S(1)}, u32[]{:S(2)}, u32[]{:S(2)}) collective-permute-start(bf16[16,1024]{1,0:T(8,128)(2,1)S(1)} %get-tuple-element.53), channel_id=1, source_target_pairs={{0,256},{128,384},{256,0},{384,128},{1,257},{129,385},{257,1},{385... | collective-permute-start | bytes 98312 | tf_op jit(solution)/shard_map/ppermute | solution.py:507
  125.0 7.0 %collective-permute-start.9 = (bf16[16,1024]{1,0:T(8,128)(2,1)S(1)}, bf16[16,1024]{1,0:T(8,128)(2,1)S(1)}, u32[]{:S(2)}, u32[]{:S(2)}) collective-permute-start(bf16[16,1024]{1,0:T(8,128)(2,1)S(1)} %get-tuple-element.52), channel_id=1, source_target_pairs={{0,384},{128,256},{256,128},{384,0},{1,385},{129,257},{257,129},{3... | collective-permute-start | bytes 98312 | tf_op jit(solution)/shard_map/ppermute | solution.py:507

commit v6 on v5

--- a/solution.py
+++ b/solution.py
@@ -534,7 +534,7 @@
     terms = own_terms + swap(other_terms, "core", 1)
     for axis in ("x", "y"):
         total = terms[0].astype(f32)
-        for bit in range(1, SIDE):
+        for bit in (3, 2, 1):
             total = total + swap(terms[bit], axis, bit).astype(f32)
         terms = total.astype(bf16)
 

time: 135 us -> 134 us (level)
  starting transfers between devices: 51.6 us -> 50 us
    all_to_all x1, waiting for transfers between devices: 0.6 us -> 2.04 us  [local(): all_rows = lax.all_to_all(rows, 'head', 0, 0).reshape(ROWS, Z_WIDTH)]
  transfers between devices with their start and end apart: 12 -> 12, of which waited for: 6 -> 7; matrix products, arithmetic and copies ran while one was open for 1% -> 1% of each run, Pallas kernels for 1% -> 1%
where the time goes in v6:
time: 134 us; the launch traced here: 133 us
  starting transfers between devices  50 us (37%)
  blocking collectives  47.8 us (36%)
  Pallas kernels  16.1 us (12%)
  waiting for transfers between devices  15.8 us (12%)
    all_to_all x2, blocking collectives, over_chips(): return lax.all_to_all(slots, ('y', 'x'), 0, 0)  47.8 us
    ppermute x10, starting transfers between devices, swap(): lax.ppermute(array, axis, [(i, i ^ bit) for i in range(lax.axis_size(axis...  27.8 us
    all_to_all x1, starting transfers between devices, local(): lax.all_to_all(z_part.reshape(z_size, z_rows, Z_WIDTH), 'head', 0, 0)  15.2 us
    ppermute x10, waiting for transfers between devices, swap(): lax.ppermute(array, axis, [(i, i ^ bit) for i in range(lax.axis_size(axis...  8.64 us
    all_to_all x1, starting transfers between devices, local(): all_rows = lax.all_to_all(rows, 'head', 0, 0).reshape(ROWS, Z_WIDTH)  6.95 us
    all_to_all x1, waiting for transfers between devices, local(): lax.all_to_all(z_part.reshape(z_size, z_rows, Z_WIDTH), 'head', 0, 0)  5.11 us
    pallas_call x1, Pallas kernels, run_gradient(): call(gradient_kernel, [((CHIPS, OUT_ROWS, NOPE), bf16), ((CHIPS, KEY_ROWS...  4.99 us
    pallas_call x1, Pallas kernels, run_pack(): call(pack_kernel, [((CHIPS, IN_ROWS, NOPE), bf16), ((8, BLOCKS), jnp.int3...  4.07 us
  transfers between devices with their start and end apart: 12, of which 7 were waited for; matrix products, arithmetic and copies ran while one was open for 1% of the time, Pallas kernels for 1%

profile of v6, /device:TPU:32, one launch (start us, length us, event | category | flops | bytes accessed | tf_op | source)
XLA Modules:
  0.0 133.0 jit_solution(8625953869124162493)
XLA Ops:
  0.6 4.1 %shard_map.93 = (bf16[16,320,128]{2,1,0:T(8,128)(2,1)}, s32[8,64]{1,0:T(8,128)}, s32[8,1024]{1,0:T(8,128)}) custom-call(s32[1,64]{1,0:T(1,128)} %bitcast.29, bf16[576,128]{1,0:T(8,128)(2,1)} %bitcast.27, bf16[512,512]{1,0:T(8,128)(2,1)} %wk_ref.1, bf16[512,512]{1,0:T(8,128)(2,1)} %wv_ref.1, bf16[128,768]{1,0:T(8,128)(2,1)} %q_any.1, bf16[128,512]{1,0:T(8,128)(2,1)} %g_any.1), custom_call_target="tpu_custom_call" | custom-call | tf_op jit(solution)/shard_map/pallas_call | solution.py:437
  4.7 27.0 %all_to_all.20.own_ref = bf16[16,320,128]{2,1,0:T(8,128)(2,1)S(1)} all-to-all(bf16[16,320,128]{2,1,0:T(8,128)(2,1)} %get-tuple-element.34), channel_id=1, replica_groups=mesh['y'=4,'x'=4,'core'=2,'head'=16] {'y','x'}, dimensions={0} | all-to-all | bytes 2621440 | tf_op jit(solution)/shard_map/all_to_all | solution.py:503
  31.7 0.0 copy-start.3
  31.7 0.0 copy-start.5
  31.7 0.0 copy-start.4
  31.8 1.9 %collective-permute-start = (bf16[16,160,128]{2,1,0:T(8,128)(2,1)S(1)}, bf16[16,160,128]{2,1,0:T(8,128)(2,1)S(1)}, u32[]{:S(2)}, u32[]{:S(2)}) collective-permute-start(bf16[16,160,128]{2,1,0:T(8,128)(2,1)S(1)} %slice.73), channel_id=1, source_target_pairs={{0,16},{16,0},{1,17},{17,1},{2,18},{18,2},{3,19},{19,3},{4,20},{20... | collective-permute-start | bytes 1966088 | tf_op jit(solution)/shard_map/ppermute | solution.py:507
  33.7 0.0 copy-done.3
  33.7 0.0 copy-done.5
  33.7 0.9 shard_map.94
  34.7 1.1 collective-permute-done.other_ref
  35.8 0.0 copy-done.4
  35.8 3.8 %shard_map.95 = (bf16[2048,256]{1,0:T(8,128)(2,1)S(1)}, f32[8,1024]{1,0:T(8,128)S(1)}, f32[2048,1024]{1,0:T(8,128)S(1)}, f32[2048,1024]{1,0:T(8,128)S(1)}) custom-call(s32[8,64]{1,0:T(8,128)S(1)} %copy-done.3, s32[8,1024]{1,0:T(8,128)S(1)} %copy-done.4, bf16[16,320,128]{2,1,0:T(8,128)(2,1)S(1)} %all_to_all.20.own_ref, ...), custom_call_target="tpu_custom_call" | custom-call | tf_op jit(solution)/shard_map/pallas_call | solution.py:472
  39.6 1.9 %collective-permute-start.1 = (f32[8,1024]{1,0:T(8,128)S(1)}, f32[8,1024]{1,0:T(8,128)S(1)}, u32[]{:S(2)}, u32[]{:S(2)}) collective-permute-start(f32[8,1024]{1,0:T(8,128)S(1)} %get-tuple-element.41.own_stats), channel_id=1, source_target_pairs={{0,128},{128,0},{256,384},{384,256},{1,129},{129,1},{257,385},{385... | collective-permute-start | bytes 98312 | tf_op jit(solution)/shard_map/ppermute | solution.py:507
  41.5 4.0 %collective-permute-done.1.other_stats = f32[8,1024]{1,0:T(8,128)S(1)} collective-permute-done((f32[8,1024]{1,0:T(8,128)S(1)}, f32[8,1024]{1,0:T(8,128)S(1)}, u32[]{:S(2)}, u32[]{:S(2)}) %collective-permute-start.1) | collective-permute-done | bytes 32800 | tf_op jit(solution)/shard_map/ppermute | solution.py:507
  45.5 5.0 %shard_map.96 = (bf16[16,256,128]{2,1,0:T(8,128)(2,1)S(1)}, bf16[16,160,128]{2,1,0:T(8,128)(2,1)S(1)}) custom-call(s32[8,64]{1,0:T(8,128)S(1)} %copy-done.3, bf16[2048,256]{1,0:T(8,128)(2,1)S(1)} %get-tuple-element.38.keys, bf16[1024,256]{1,0:T(8,128)(2,1)S(1)} %get-tuple-element.35.queries, bf16[1024,128]{1,0:T(8,128)(2,1)S(1)} %get-tuple-element.36.grads, ...), custom_call_target="tpu_custom_call" | custom-call | tf_op jit(solution)/shard_map/pallas_call | solution.py:487
  50.5 2.4 %collective-permute-start.2 = (bf16[16,160,128]{2,1,0:T(8,128)(2,1)S(1)}, bf16[16,160,128]{2,1,0:T(8,128)(2,1)S(1)}, u32[]{:S(2)}, u32[]{:S(2)}) collective-permute-start(bf16[16,160,128]{2,1,0:T(8,128)(2,1)S(1)} %get-tuple-element.43), channel_id=1, source_target_pairs={{0,16},{16,0},{1,17},{17,1},{2,18},{18,2},{3,19},{19,3},{4,20},{20... | collective-permute-start | bytes 1966088 | tf_op jit(solution)/shard_map/ppermute | solution.py:507
  52.9 1.7 %collective-permute-done.2 = bf16[16,160,128]{2,1,0:T(8,128)(2,1)S(1)} collective-permute-done((bf16[16,160,128]{2,1,0:T(8,128)(2,1)S(1)}, bf16[16,160,128]{2,1,0:T(8,128)(2,1)S(1)}, u32[]{:S(2)}, u32[]{:S(2)}) %collective-permute-start.2) | collective-permute-done | bytes 655392 | tf_op jit(solution)/shard_map/ppermute | solution.py:507
  54.6 0.3 add_dynamic-update-slice_fusion
  54.9 0.0 copy-start
  54.9 0.0 copy-start.1
  54.9 0.0 copy-start.2
  54.9 20.8 %all_to_all.21.slots_ref = bf16[16,256,128]{2,1,0:T(8,128)(2,1)S(1)} all-to-all(bf16[16,256,128]{2,1,0:T(8,128)(2,1)S(1)} %add_dynamic-update-slice_fusion), channel_id=1, replica_groups=mesh['y'=4,'x'=4,'core'=2,'head'=16] {'y','x'}, dimensions={0} | all-to-all | bytes 2097152 | tf_op jit(solution)/shard_map/all_to_all | solution.py:503
  75.7 0.0 copy-done
  75.7 0.0 copy-done.1
  75.7 0.0 copy-done.2
  75.7 1.5 %shard_map.97 = (bf16[128,640]{1,0:T(8,128)(2,1)}, bf16[128,768]{1,0:T(8,128)(2,1)}, bf16[4,4,16,1024]{3,2,1,0:T(8,128)(2,1)S(1)}, bf16[4,4,16,1024]{3,2,1,0:T(8,128)(2,1)S(1)}) custom-call(bf16[16,256,128]{2,1,0:T(8,128)(2,1)S(1)} %all_to_all.21.slots_ref, bf16[512,512]{1,0:T(8,128)(2,1)S(1)} %copy-done, bf16[512,512]{1,0:T(8,128)(2,1)S(1)} %copy-done.1, ...), custom_call_target="tpu_custom_call" | custom-call | tf_op jit(solution)/shard_map/pallas_call | solution.py:527
  77.2 1.9 %collective-permute-start.3 = (bf16[4,4,16,1024]{3,2,1,0:T(8,128)(2,1)S(1)}, bf16[4,4,16,1024]{3,2,1,0:T(8,128)(2,1)S(1)}, u32[]{:S(2)}, u32[]{:S(2)}) collective-permute-start(bf16[4,4,16,1024]{3,2,1,0:T(8,128)(2,1)S(1)} %get-tuple-element.47), channel_id=1, source_target_pairs={{0,16},{16,0},{1,17},{17,1},{2,18},{18,2},{3,19},{19,3},{4,20},{20... | collective-permute-start | bytes 1572872 | tf_op jit(solution)/shard_map/ppermute | solution.py:507
  79.1 15.2 %all-to-all-start.2 = ((bf16[16,8,640]{2,1,0:T(8,128)(2,1)}), bf16[16,8,640]{2,1,0:T(8,128)(2,1)S(1)}, u32[]{:S(2)}, u32[]{:S(2)}) async-start(bf16[16,8,640]{2,1,0:T(8,128)(2,1)} %bitcast.2), calls=%async_computation.2 | async-start | bytes 327680 | tf_op jit(solution)/shard_map/all_to_all | solution.py:541
  94.3 0.0 collective-permute-done.3
  94.3 0.2 add.33
  94.6 2.4 %collective-permute-start.4 = (bf16[4,16,1024]{2,1,0:T(8,128)(2,1)S(1)}, bf16[4,16,1024]{2,1,0:T(8,128)(2,1)S(1)}, u32[]{:S(2)}, u32[]{:S(2)}) collective-permute-start(bf16[4,16,1024]{2,1,0:T(8,128)(2,1)S(1)} %get-tuple-element.48), channel_id=1, source_target_pairs={{0,96},{32,64},{64,32},{96,0},{1,97},{33,65},{65,33},{97,1},{2,98}... | collective-permute-start | bytes 393224 | tf_op jit(solution)/shard_map/ppermute | solution.py:507
  96.9 4.1 %collective-permute-start.5 = (bf16[4,16,1024]{2,1,0:T(8,128)(2,1)S(1)}, bf16[4,16,1024]{2,1,0:T(8,128)(2,1)S(1)}, u32[]{:S(2)}, u32[]{:S(2)}) collective-permute-start(bf16[4,16,1024]{2,1,0:T(8,128)(2,1)S(1)} %get-tuple-element.50), channel_id=1, source_target_pairs={{0,64},{32,96},{64,0},{96,32},{1,65},{33,97},{65,1},{97,33},{2,66}... | collective-permute-start | bytes 393224 | tf_op jit(solution)/shard_map/ppermute | solution.py:507
  101.0 3.4 %collective-permute-start.6 = (bf16[4,16,1024]{2,1,0:T(8,128)(2,1)S(1)}, bf16[4,16,1024]{2,1,0:T(8,128)(2,1)S(1)}, u32[]{:S(2)}, u32[]{:S(2)}) collective-permute-start(bf16[4,16,1024]{2,1,0:T(8,128)(2,1)S(1)} %get-tuple-element.49), channel_id=1, source_target_pairs={{0,32},{32,0},{64,96},{96,64},{1,33},{33,1},{65,97},{97,65},{2,34}... | collective-permute-start | bytes 393224 | tf_op jit(solution)/shard_map/ppermute | solution.py:507
  104.4 0.1 constant_dynamic-slice_fusion
  104.5 0.1 copy.12.kv_ref
  104.6 5.1 %all-to-all-done.2.slots_ref = bf16[16,8,640]{2,1,0:T(8,128)(2,1)S(1)} async-done(((bf16[16,8,640]{2,1,0:T(8,128)(2,1)}), bf16[16,8,640]{2,1,0:T(8,128)(2,1)S(1)}, u32[]{:S(2)}, u32[]{:S(2)}) %all-to-all-start.2) | async-done | bytes 163872 | tf_op jit(solution)/shard_map/all_to_all | solution.py:541
  109.7 0.8 shard_map.98
  110.6 7.0 %all-to-all-start.3 = ((bf16[16,8,640]{2,1,0:T(8,128)(2,1)}), bf16[16,8,640]{2,1,0:T(8,128)(2,1)S(1)}, u32[]{:S(2)}, u32[]{:S(2)}) async-start(bf16[16,8,640]{2,1,0:T(8,128)(2,1)} %shard_map.98), calls=%async_computation.3 | async-start | bytes 327680 | tf_op jit(solution)/shard_map/all_to_all | solution.py:545
  117.5 0.0 collective-permute-done.4
  117.5 0.0 collective-permute-done.5
  117.5 0.0 collective-permute-done.6
  117.6 0.1 fusion.2
  117.6 2.8 %collective-permute-start.7 = (bf16[16,1024]{1,0:T(8,128)(2,1)S(1)}, bf16[16,1024]{1,0:T(8,128)(2,1)S(1)}, u32[]{:S(2)}, u32[]{:S(2)}) collective-permute-start(bf16[16,1024]{1,0:T(8,128)(2,1)S(1)} %get-tuple-element.51), channel_id=1, source_target_pairs={{0,384},{128,256},{256,128},{384,0},{1,385},{129,257},{257,129},{3... | collective-permute-start | bytes 98312 | tf_op jit(solution)/shard_map/ppermute | solution.py:507
  120.4 2.5 %collective-permute-start.8 = (bf16[16,1024]{1,0:T(8,128)(2,1)S(1)}, bf16[16,1024]{1,0:T(8,128)(2,1)S(1)}, u32[]{:S(2)}, u32[]{:S(2)}) collective-permute-start(bf16[16,1024]{1,0:T(8,128)(2,1)S(1)} %get-tuple-element.53), channel_id=1, source_target_pairs={{0,256},{128,384},{256,0},{384,128},{1,257},{129,385},{257,1},{385... | collective-permute-start | bytes 98312 | tf_op jit(solution)/shard_map/ppermute | solution.py:507
  122.9 4.6 %collective-permute-start.9 = (bf16[16,1024]{1,0:T(8,128)(2,1)S(1)}, bf16[16,1024]{1,0:T(8,128)(2,1)S(1)}, u32[]{:S(2)}, u32[]{:S(2)}) collective-permute-start(bf16[16,1024]{1,0:T(8,128)(2,1)S(1)} %get-tuple-element.52), channel_id=1, source_target_pairs={{0,128},{128,0},{256,384},{384,256},{1,129},{129,1},{257,385},{385... | collective-permute-start | bytes 98312 | tf_op jit(solution)/shard_map/ppermute | solution.py:507
  127.5 0.0 collective-permute-done.7
  127.5 0.2 collective-permute-done.8
  127.7 1.6 %collective-permute-done.9 = bf16[16,1024]{1,0:T(8,128)(2,1)S(1)} collective-permute-done((bf16[16,1024]{1,0:T(8,128)(2,1)S(1)}, bf16[16,1024]{1,0:T(8,128)(2,1)S(1)}, u32[]{:S(2)}, u32[]{:S(2)}) %collective-permute-start.9) | collective-permute-done | bytes 32800 | tf_op jit(solution)/shard_map/ppermute | solution.py:507
  129.4 0.6 fusion.5
  130.0 2.0 %all-to-all-done.3 = bf16[16,8,640]{2,1,0:T(8,128)(2,1)S(1)} async-done(((bf16[16,8,640]{2,1,0:T(8,128)(2,1)}), bf16[16,8,640]{2,1,0:T(8,128)(2,1)S(1)}, u32[]{:S(2)}, u32[]{:S(2)}) %all-to-all-start.3) | async-done | bytes 163872 | tf_op jit(solution)/shard_map/all_to_all | solution.py:545
  132.1 0.1 copy.13
  132.2 0.7 convert_element_type.36
  (4 shorter events, 0.1 us)
Async XLA Ops:
  31.7 2.0 %copy-start.3 = (s32[8,64]{1,0:T(8,128)S(1)}, s32[8,64]{1,0:T(8,128)}, u32[]{:S(2)}) copy-start(s32[8,64]{1,0:T(8,128)} %get-tuple-element.32.meta) | copy-start | bytes 6148
  31.7 2.0 %copy-start.5 = (s32[64]{0:T(128)S(1)}, s32[64]{0:T(128)}, u32[]{:S(2)}) copy-start(s32[64]{0:T(128)} %block_start.1) | copy-start | bytes 772
  31.7 4.0 %copy-start.4 = (s32[8,1024]{1,0:T(8,128)S(1)}, s32[8,1024]{1,0:T(8,128)}, u32[]{:S(2)}) copy-start(s32[8,1024]{1,0:T(8,128)} %get-tuple-element.33.q_pos) | copy-start | bytes 98308
  31.8 4.0 %collective-permute-start = (bf16[16,160,128]{2,1,0:T(8,128)(2,1)S(1)}, bf16[16,160,128]{2,1,0:T(8,128)(2,1)S(1)}, u32[]{:S(2)}, u32[]{:S(2)}) collective-permute-start(bf16[16,160,128]{2,1,0:T(8,128)(2,1)S(1)} %slice.73), channel_id=1, source_target_pairs={{0,16},{16,0},{1,17},{17,1},{2,18},{18,2},{3,19},{19,3},{4,20},{20... | collective-permute-start | bytes 1966088 | tf_op jit(solution)/shard_map/ppermute | solution.py:507
  39.6 5.9 %collective-permute-start.1 = (f32[8,1024]{1,0:T(8,128)S(1)}, f32[8,1024]{1,0:T(8,128)S(1)}, u32[]{:S(2)}, u32[]{:S(2)}) collective-permute-start(f32[8,1024]{1,0:T(8,128)S(1)} %get-tuple-element.41.own_stats), channel_id=1, source_target_pairs={{0,128},{128,0},{256,384},{384,256},{1,129},{129,1},{257,385},{385... | collective-permute-start | bytes 98312 | tf_op jit(solution)/shard_map/ppermute | solution.py:507
  50.5 4.1 %collective-permute-start.2 = (bf16[16,160,128]{2,1,0:T(8,128)(2,1)S(1)}, bf16[16,160,128]{2,1,0:T(8,128)(2,1)S(1)}, u32[]{:S(2)}, u32[]{:S(2)}) collective-permute-start(bf16[16,160,128]{2,1,0:T(8,128)(2,1)S(1)} %get-tuple-element.43), channel_id=1, source_target_pairs={{0,16},{16,0},{1,17},{17,1},{2,18},{18,2},{3,19},{19,3},{4,20},{20... | collective-permute-start | bytes 1966088 | tf_op jit(solution)/shard_map/ppermute | solution.py:507
  54.9 20.8 %copy-start = (bf16[512,512]{1,0:T(8,128)(2,1)S(1)}, bf16[512,512]{1,0:T(8,128)(2,1)}, u32[]{:S(2)}) copy-start(bf16[512,512]{1,0:T(8,128)(2,1)} %wk_ref.1) | copy-start | bytes 1572868
  54.9 20.8 %copy-start.1 = (bf16[512,512]{1,0:T(8,128)(2,1)S(1)}, bf16[512,512]{1,0:T(8,128)(2,1)}, u32[]{:S(2)}) copy-start(bf16[512,512]{1,0:T(8,128)(2,1)} %wv_ref.1) | copy-start | bytes 1572868
  54.9 20.8 %copy-start.2 = (bf16[128,576]{0,1:T(8,128)(2,1)S(1)}, bf16[128,576]{0,1:T(8,128)(2,1)}, u32[]{:S(2)}) copy-start(bf16[128,576]{0,1:T(8,128)(2,1)} %param.9) | copy-start | bytes 442372
  77.2 17.1 %collective-permute-start.3 = (bf16[4,4,16,1024]{3,2,1,0:T(8,128)(2,1)S(1)}, bf16[4,4,16,1024]{3,2,1,0:T(8,128)(2,1)S(1)}, u32[]{:S(2)}, u32[]{:S(2)}) collective-permute-start(bf16[4,4,16,1024]{3,2,1,0:T(8,128)(2,1)S(1)} %get-tuple-element.47), channel_id=1, source_target_pairs={{0,16},{16,0},{1,17},{17,1},{2,18},{18,2},{3,19},{19,3},{4,20},{20... | collective-permute-start | bytes 1572872 | tf_op jit(solution)/shard_map/ppermute | solution.py:507
  79.1 30.6 %all-to-all-start.2 = ((bf16[16,8,640]{2,1,0:T(8,128)(2,1)}), bf16[16,8,640]{2,1,0:T(8,128)(2,1)S(1)}, u32[]{:S(2)}, u32[]{:S(2)}) async-start(bf16[16,8,640]{2,1,0:T(8,128)(2,1)} %bitcast.2), calls=%async_computation.2 | async-start | bytes 327680 | tf_op jit(solution)/shard_map/all_to_all | solution.py:541
  94.6 23.0 %collective-permute-start.4 = (bf16[4,16,1024]{2,1,0:T(8,128)(2,1)S(1)}, bf16[4,16,1024]{2,1,0:T(8,128)(2,1)S(1)}, u32[]{:S(2)}, u32[]{:S(2)}) collective-permute-start(bf16[4,16,1024]{2,1,0:T(8,128)(2,1)S(1)} %get-tuple-element.48), channel_id=1, source_target_pairs={{0,96},{32,64},{64,32},{96,0},{1,97},{33,65},{65,33},{97,1},{2,98}... | collective-permute-start | bytes 393224 | tf_op jit(solution)/shard_map/ppermute | solution.py:507
  96.9 20.6 %collective-permute-start.5 = (bf16[4,16,1024]{2,1,0:T(8,128)(2,1)S(1)}, bf16[4,16,1024]{2,1,0:T(8,128)(2,1)S(1)}, u32[]{:S(2)}, u32[]{:S(2)}) collective-permute-start(bf16[4,16,1024]{2,1,0:T(8,128)(2,1)S(1)} %get-tuple-element.50), channel_id=1, source_target_pairs={{0,64},{32,96},{64,0},{96,32},{1,65},{33,97},{65,1},{97,33},{2,66}... | collective-permute-start | bytes 393224 | tf_op jit(solution)/shard_map/ppermute | solution.py:507
  101.0 16.5 %collective-permute-start.6 = (bf16[4,16,1024]{2,1,0:T(8,128)(2,1)S(1)}, bf16[4,16,1024]{2,1,0:T(8,128)(2,1)S(1)}, u32[]{:S(2)}, u32[]{:S(2)}) collective-permute-start(bf16[4,16,1024]{2,1,0:T(8,128)(2,1)S(1)} %get-tuple-element.49), channel_id=1, source_target_pairs={{0,32},{32,0},{64,96},{96,64},{1,33},{33,1},{65,97},{97,65},{2,34}... | collective-permute-start | bytes 393224 | tf_op jit(solution)/shard_map/ppermute | solution.py:507
  110.6 21.5 %all-to-all-start.3 = ((bf16[16,8,640]{2,1,0:T(8,128)(2,1)}), bf16[16,8,640]{2,1,0:T(8,128)(2,1)S(1)}, u32[]{:S(2)}, u32[]{:S(2)}) async-start(bf16[16,8,640]{2,1,0:T(8,128)(2,1)} %shard_map.98), calls=%async_computation.3 | async-start | bytes 327680 | tf_op jit(solution)/shard_map/all_to_all | solution.py:545
  117.6 9.8 %collective-permute-start.7 = (bf16[16,1024]{1,0:T(8,128)(2,1)S(1)}, bf16[16,1024]{1,0:T(8,128)(2,1)S(1)}, u32[]{:S(2)}, u32[]{:S(2)}) collective-permute-start(bf16[16,1024]{1,0:T(8,128)(2,1)S(1)} %get-tuple-element.51), channel_id=1, source_target_pairs={{0,384},{128,256},{256,128},{384,0},{1,385},{129,257},{257,129},{3... | collective-permute-start | bytes 98312 | tf_op jit(solution)/shard_map/ppermute | solution.py:507
  120.4 7.3 %collective-permute-start.8 = (bf16[16,1024]{1,0:T(8,128)(2,1)S(1)}, bf16[16,1024]{1,0:T(8,128)(2,1)S(1)}, u32[]{:S(2)}, u32[]{:S(2)}) collective-permute-start(bf16[16,1024]{1,0:T(8,128)(2,1)S(1)} %get-tuple-element.53), channel_id=1, source_target_pairs={{0,256},{128,384},{256,0},{384,128},{1,257},{129,385},{257,1},{385... | collective-permute-start | bytes 98312 | tf_op jit(solution)/shard_map/ppermute | solution.py:507
  122.9 6.5 %collective-permute-start.9 = (bf16[16,1024]{1,0:T(8,128)(2,1)S(1)}, bf16[16,1024]{1,0:T(8,128)(2,1)S(1)}, u32[]{:S(2)}, u32[]{:S(2)}) collective-permute-start(bf16[16,1024]{1,0:T(8,128)(2,1)S(1)} %get-tuple-element.52), channel_id=1, source_target_pairs={{0,128},{128,0},{256,384},{384,256},{1,129},{129,1},{257,385},{385... | collective-permute-start | bytes 98312 | tf_op jit(solution)/shard_map/ppermute | solution.py:507

commit v7 on v6

--- a/solution.py
+++ b/solution.py
@@ -297,7 +297,7 @@
     other_fade = jnp.exp2(other_top - top)
     weight_sum = own_stats[1:2, :] * own_fade + other_stats[1:2, :] * other_fade
     weighted = own_stats[2:3, :] * own_fade + other_stats[2:3, :] * other_fade
-    log_total = top + jnp.log2(weight_sum)
+    log_scaled = top + jnp.log2(weight_sum) - math.log2(SCALE)
     average = weighted / weight_sum
     query_grads[...] = jnp.zeros_like(query_grads)
 
@@ -314,15 +314,14 @@
                 def _(lanes=lanes, rows=rows, step=step):
                     part = slice(step * rows, (step + 1) * rows)
                     at = pl.ds(pl.multiple_of(index * CHUNK + step * rows, rows), rows)
-                    probs = jnp.exp2(scores[at, lanes] - log_total[:, lanes])
-                    slope = (slopes[at, lanes] - average[:, lanes]) * SCALE
-                    score_grad = (probs * slope).astype(bf16)
+                    probs = jnp.exp2(scores[at, lanes] - log_scaled[:, lanes])
+                    score_grad = (probs * (slopes[at, lanes] - average[:, lanes])).astype(bf16)
                     value_sum[part, :] += dot(probs.astype(bf16), grads[lanes, :])
                     key_sum[part, :] += dot(score_grad, queries[lanes, :])
                     query_grads[lanes, :] += dot(score_grad, keys[at, :], 0, 0)
 
         key_grads[at, :] = key_sum[...].astype(bf16)
-        value_grads[at, :] = value_sum[...].astype(bf16)
+        value_grads[at, :] = (value_sum[...] * (1.0 / SCALE)).astype(bf16)
         return carry
 
     lax.fori_loop(0, N_CHUNKS, gradients, 0)

time: 134 us -> 134 us (level)
  no operation moved by 1% of the time
where the time goes in v7:
time: 134 us
  starting transfers between devices  49.5 us (37%)
  blocking collectives  47.5 us (35%)
  Pallas kernels  17.3 us (13%)
  waiting for transfers between devices  16.1 us (12%)
    all_to_all x2, blocking collectives, over_chips(): return lax.all_to_all(slots, ('y', 'x'), 0, 0)  47.5 us
    ppermute x10, starting transfers between devices, swap(): lax.ppermute(array, axis, [(i, i ^ bit) for i in range(lax.axis_size(axis...  27.3 us
    all_to_all x1, starting transfers between devices, local(): lax.all_to_all(z_part.reshape(z_size, z_rows, Z_WIDTH), 'head', 0, 0)  15.2 us
    ppermute x10, waiting for transfers between devices, swap(): lax.ppermute(array, axis, [(i, i ^ bit) for i in range(lax.axis_size(axis...  8.93 us
    all_to_all x1, starting transfers between devices, local(): all_rows = lax.all_to_all(rows, 'head', 0, 0).reshape(ROWS, Z_WIDTH)  6.95 us
    pallas_call x1, Pallas kernels, run_gradient(): call(gradient_kernel, [((CHIPS, OUT_ROWS, NOPE), bf16), ((CHIPS, KEY_ROWS...  5.6 us
    all_to_all x1, waiting for transfers between devices, local(): lax.all_to_all(z_part.reshape(z_size, z_rows, Z_WIDTH), 'head', 0, 0)  5.11 us
    pallas_call x1, Pallas kernels, run_stats(): call(stats_kernel, [((KEYS, 2 * NOPE), bf16), ((8, QUERIES), f32), ((KEYS...  4.4 us
  transfers between devices with their start and end apart: 12, of which 7 were waited for; matrix products, arithmetic and copies ran while one was open for 1% of the time, Pallas kernels for 1%

profile of v7, /device:TPU:32, one launch (start us, length us, event | category | flops | bytes accessed | tf_op | source)
XLA Modules:
  0.0 133.7 jit_solution(165639069566996888)
XLA Ops:
  0.6 4.1 %shard_map.93 = (bf16[16,320,128]{2,1,0:T(8,128)(2,1)}, s32[8,64]{1,0:T(8,128)}, s32[8,1024]{1,0:T(8,128)}) custom-call(s32[1,64]{1,0:T(1,128)} %bitcast.29, bf16[576,128]{1,0:T(8,128)(2,1)} %bitcast.27, bf16[512,512]{1,0:T(8,128)(2,1)} %wk_ref.1, bf16[512,512]{1,0:T(8,128)(2,1)} %wv_ref.1, bf16[128,768]{1,0:T(8,128)(2,1)} %q_any.1, bf16[128,512]{1,0:T(8,128)(2,1)} %g_any.1), custom_call_target="tpu_custom_call" | custom-call | tf_op jit(solution)/shard_map/pallas_call | solution.py:436
  4.7 27.0 %all_to_all.20.own_ref = bf16[16,320,128]{2,1,0:T(8,128)(2,1)S(1)} all-to-all(bf16[16,320,128]{2,1,0:T(8,128)(2,1)} %get-tuple-element.34), channel_id=1, replica_groups=mesh['y'=4,'x'=4,'core'=2,'head'=16] {'y','x'}, dimensions={0} | all-to-all | bytes 2621440 | tf_op jit(solution)/shard_map/all_to_all | solution.py:502
  31.7 0.0 copy-start.3
  31.7 0.0 copy-start.5
  31.7 0.0 copy-start.4
  31.8 1.9 %collective-permute-start = (bf16[16,160,128]{2,1,0:T(8,128)(2,1)S(1)}, bf16[16,160,128]{2,1,0:T(8,128)(2,1)S(1)}, u32[]{:S(2)}, u32[]{:S(2)}) collective-permute-start(bf16[16,160,128]{2,1,0:T(8,128)(2,1)S(1)} %slice.73), channel_id=1, source_target_pairs={{0,16},{16,0},{1,17},{17,1},{2,18},{18,2},{3,19},{19,3},{4,20},{20... | collective-permute-start | bytes 1966088 | tf_op jit(solution)/shard_map/ppermute | solution.py:506
  33.7 0.0 copy-done.3
  33.7 0.0 copy-done.5
  33.7 0.9 shard_map.94
  34.7 1.1 collective-permute-done.other_ref
  35.8 0.0 copy-done.4
  35.8 4.4 %shard_map.95 = (bf16[2048,256]{1,0:T(8,128)(2,1)S(1)}, f32[8,1024]{1,0:T(8,128)S(1)}, f32[2048,1024]{1,0:T(8,128)S(1)}, f32[2048,1024]{1,0:T(8,128)S(1)}) custom-call(s32[8,64]{1,0:T(8,128)S(1)} %copy-done.3, s32[8,1024]{1,0:T(8,128)S(1)} %copy-done.4, bf16[16,320,128]{2,1,0:T(8,128)(2,1)S(1)} %all_to_all.20.own_ref, ...), custom_call_target="tpu_custom_call" | custom-call | tf_op jit(solution)/shard_map/pallas_call | solution.py:471
  40.2 1.9 %collective-permute-start.1 = (f32[8,1024]{1,0:T(8,128)S(1)}, f32[8,1024]{1,0:T(8,128)S(1)}, u32[]{:S(2)}, u32[]{:S(2)}) collective-permute-start(f32[8,1024]{1,0:T(8,128)S(1)} %get-tuple-element.41.own_stats), channel_id=1, source_target_pairs={{0,128},{128,0},{256,384},{384,256},{1,129},{129,1},{257,385},{385... | collective-permute-start | bytes 98312 | tf_op jit(solution)/shard_map/ppermute | solution.py:506
  42.1 3.9 %collective-permute-done.1.other_stats = f32[8,1024]{1,0:T(8,128)S(1)} collective-permute-done((f32[8,1024]{1,0:T(8,128)S(1)}, f32[8,1024]{1,0:T(8,128)S(1)}, u32[]{:S(2)}, u32[]{:S(2)}) %collective-permute-start.1) | collective-permute-done | bytes 32800 | tf_op jit(solution)/shard_map/ppermute | solution.py:506
  46.0 5.6 %shard_map.96 = (bf16[16,256,128]{2,1,0:T(8,128)(2,1)S(1)}, bf16[16,160,128]{2,1,0:T(8,128)(2,1)S(1)}) custom-call(s32[8,64]{1,0:T(8,128)S(1)} %copy-done.3, bf16[2048,256]{1,0:T(8,128)(2,1)S(1)} %get-tuple-element.38.keys, bf16[1024,256]{1,0:T(8,128)(2,1)S(1)} %get-tuple-element.35.queries, bf16[1024,128]{1,0:T(8,128)(2,1)S(1)} %get-tuple-element.36.grads, ...), custom_call_target="tpu_custom_call" | custom-call | tf_op jit(solution)/shard_map/pallas_call | solution.py:486
  51.6 1.9 %collective-permute-start.2 = (bf16[16,160,128]{2,1,0:T(8,128)(2,1)S(1)}, bf16[16,160,128]{2,1,0:T(8,128)(2,1)S(1)}, u32[]{:S(2)}, u32[]{:S(2)}) collective-permute-start(bf16[16,160,128]{2,1,0:T(8,128)(2,1)S(1)} %get-tuple-element.43), channel_id=1, source_target_pairs={{0,16},{16,0},{1,17},{17,1},{2,18},{18,2},{3,19},{19,3},{4,20},{20... | collective-permute-start | bytes 1966088 | tf_op jit(solution)/shard_map/ppermute | solution.py:506
  53.5 2.1 %collective-permute-done.2 = bf16[16,160,128]{2,1,0:T(8,128)(2,1)S(1)} collective-permute-done((bf16[16,160,128]{2,1,0:T(8,128)(2,1)S(1)}, bf16[16,160,128]{2,1,0:T(8,128)(2,1)S(1)}, u32[]{:S(2)}, u32[]{:S(2)}) %collective-permute-start.2) | collective-permute-done | bytes 655392 | tf_op jit(solution)/shard_map/ppermute | solution.py:506
  55.6 0.3 add_dynamic-update-slice_fusion
  55.9 0.0 copy-start
  55.9 0.0 copy-start.1
  55.9 0.0 copy-start.2
  55.9 20.5 %all_to_all.21.slots_ref = bf16[16,256,128]{2,1,0:T(8,128)(2,1)S(1)} all-to-all(bf16[16,256,128]{2,1,0:T(8,128)(2,1)S(1)} %add_dynamic-update-slice_fusion), channel_id=1, replica_groups=mesh['y'=4,'x'=4,'core'=2,'head'=16] {'y','x'}, dimensions={0} | all-to-all | bytes 2097152 | tf_op jit(solution)/shard_map/all_to_all | solution.py:502
  76.4 0.0 copy-done
  76.4 0.0 copy-done.1
  76.4 0.0 copy-done.2
  76.4 1.5 %shard_map.97 = (bf16[128,640]{1,0:T(8,128)(2,1)}, bf16[128,768]{1,0:T(8,128)(2,1)}, bf16[4,4,16,1024]{3,2,1,0:T(8,128)(2,1)S(1)}, bf16[4,4,16,1024]{3,2,1,0:T(8,128)(2,1)S(1)}) custom-call(bf16[16,256,128]{2,1,0:T(8,128)(2,1)S(1)} %all_to_all.21.slots_ref, bf16[512,512]{1,0:T(8,128)(2,1)S(1)} %copy-done, bf16[512,512]{1,0:T(8,128)(2,1)S(1)} %copy-done.1, ...), custom_call_target="tpu_custom_call" | custom-call | tf_op jit(solution)/shard_map/pallas_call | solution.py:526
  77.9 1.9 %collective-permute-start.3 = (bf16[4,4,16,1024]{3,2,1,0:T(8,128)(2,1)S(1)}, bf16[4,4,16,1024]{3,2,1,0:T(8,128)(2,1)S(1)}, u32[]{:S(2)}, u32[]{:S(2)}) collective-permute-start(bf16[4,4,16,1024]{3,2,1,0:T(8,128)(2,1)S(1)} %get-tuple-element.47), channel_id=1, source_target_pairs={{0,16},{16,0},{1,17},{17,1},{2,18},{18,2},{3,19},{19,3},{4,20},{20... | collective-permute-start | bytes 1572872 | tf_op jit(solution)/shard_map/ppermute | solution.py:506
  79.8 15.2 %all-to-all-start.2 = ((bf16[16,8,640]{2,1,0:T(8,128)(2,1)}), bf16[16,8,640]{2,1,0:T(8,128)(2,1)S(1)}, u32[]{:S(2)}, u32[]{:S(2)}) async-start(bf16[16,8,640]{2,1,0:T(8,128)(2,1)} %bitcast.2), calls=%async_computation.2 | async-start | bytes 327680 | tf_op jit(solution)/shard_map/all_to_all | solution.py:540
  95.0 0.0 collective-permute-done.3
  95.0 0.2 add.33
  95.3 2.4 %collective-permute-start.4 = (bf16[4,16,1024]{2,1,0:T(8,128)(2,1)S(1)}, bf16[4,16,1024]{2,1,0:T(8,128)(2,1)S(1)}, u32[]{:S(2)}, u32[]{:S(2)}) collective-permute-start(bf16[4,16,1024]{2,1,0:T(8,128)(2,1)S(1)} %get-tuple-element.48), channel_id=1, source_target_pairs={{0,96},{32,64},{64,32},{96,0},{1,97},{33,65},{65,33},{97,1},{2,98}... | collective-permute-start | bytes 393224 | tf_op jit(solution)/shard_map/ppermute | solution.py:506
  97.7 4.0 %collective-permute-start.5 = (bf16[4,16,1024]{2,1,0:T(8,128)(2,1)S(1)}, bf16[4,16,1024]{2,1,0:T(8,128)(2,1)S(1)}, u32[]{:S(2)}, u32[]{:S(2)}) collective-permute-start(bf16[4,16,1024]{2,1,0:T(8,128)(2,1)S(1)} %get-tuple-element.50), channel_id=1, source_target_pairs={{0,64},{32,96},{64,0},{96,32},{1,65},{33,97},{65,1},{97,33},{2,66}... | collective-permute-start | bytes 393224 | tf_op jit(solution)/shard_map/ppermute | solution.py:506
  101.7 3.4 %collective-permute-start.6 = (bf16[4,16,1024]{2,1,0:T(8,128)(2,1)S(1)}, bf16[4,16,1024]{2,1,0:T(8,128)(2,1)S(1)}, u32[]{:S(2)}, u32[]{:S(2)}) collective-permute-start(bf16[4,16,1024]{2,1,0:T(8,128)(2,1)S(1)} %get-tuple-element.49), channel_id=1, source_target_pairs={{0,32},{32,0},{64,96},{96,64},{1,33},{33,1},{65,97},{97,65},{2,34}... | collective-permute-start | bytes 393224 | tf_op jit(solution)/shard_map/ppermute | solution.py:506
  105.1 0.1 constant_dynamic-slice_fusion
  105.2 0.1 copy.12.kv_ref
  105.3 5.1 %all-to-all-done.2.slots_ref = bf16[16,8,640]{2,1,0:T(8,128)(2,1)S(1)} async-done(((bf16[16,8,640]{2,1,0:T(8,128)(2,1)}), bf16[16,8,640]{2,1,0:T(8,128)(2,1)S(1)}, u32[]{:S(2)}, u32[]{:S(2)}) %all-to-all-start.2) | async-done | bytes 163872 | tf_op jit(solution)/shard_map/all_to_all | solution.py:540
  110.4 0.8 shard_map.98
  111.3 7.0 %all-to-all-start.3 = ((bf16[16,8,640]{2,1,0:T(8,128)(2,1)}), bf16[16,8,640]{2,1,0:T(8,128)(2,1)S(1)}, u32[]{:S(2)}, u32[]{:S(2)}) async-start(bf16[16,8,640]{2,1,0:T(8,128)(2,1)} %shard_map.98), calls=%async_computation.3 | async-start | bytes 327680 | tf_op jit(solution)/shard_map/all_to_all | solution.py:544
  118.2 0.0 collective-permute-done.4
  118.2 0.0 collective-permute-done.5
  118.2 0.0 collective-permute-done.6
  118.3 0.1 fusion.2
  118.3 2.8 %collective-permute-start.7 = (bf16[16,1024]{1,0:T(8,128)(2,1)S(1)}, bf16[16,1024]{1,0:T(8,128)(2,1)S(1)}, u32[]{:S(2)}, u32[]{:S(2)}) collective-permute-start(bf16[16,1024]{1,0:T(8,128)(2,1)S(1)} %get-tuple-element.51), channel_id=1, source_target_pairs={{0,384},{128,256},{256,128},{384,0},{1,385},{129,257},{257,129},{3... | collective-permute-start | bytes 98312 | tf_op jit(solution)/shard_map/ppermute | solution.py:506
  121.1 2.5 %collective-permute-start.8 = (bf16[16,1024]{1,0:T(8,128)(2,1)S(1)}, bf16[16,1024]{1,0:T(8,128)(2,1)S(1)}, u32[]{:S(2)}, u32[]{:S(2)}) collective-permute-start(bf16[16,1024]{1,0:T(8,128)(2,1)S(1)} %get-tuple-element.53), channel_id=1, source_target_pairs={{0,256},{128,384},{256,0},{384,128},{1,257},{129,385},{257,1},{385... | collective-permute-start | bytes 98312 | tf_op jit(solution)/shard_map/ppermute | solution.py:506
  123.6 4.6 %collective-permute-start.9 = (bf16[16,1024]{1,0:T(8,128)(2,1)S(1)}, bf16[16,1024]{1,0:T(8,128)(2,1)S(1)}, u32[]{:S(2)}, u32[]{:S(2)}) collective-permute-start(bf16[16,1024]{1,0:T(8,128)(2,1)S(1)} %get-tuple-element.52), channel_id=1, source_target_pairs={{0,128},{128,0},{256,384},{384,256},{1,129},{129,1},{257,385},{385... | collective-permute-start | bytes 98312 | tf_op jit(solution)/shard_map/ppermute | solution.py:506
  128.2 0.0 collective-permute-done.7
  128.2 0.2 collective-permute-done.8
  128.4 1.6 %collective-permute-done.9 = bf16[16,1024]{1,0:T(8,128)(2,1)S(1)} collective-permute-done((bf16[16,1024]{1,0:T(8,128)(2,1)S(1)}, bf16[16,1024]{1,0:T(8,128)(2,1)S(1)}, u32[]{:S(2)}, u32[]{:S(2)}) %collective-permute-start.9) | collective-permute-done | bytes 32800 | tf_op jit(solution)/shard_map/ppermute | solution.py:506
  130.1 0.6 fusion.5
  130.7 2.0 %all-to-all-done.3 = bf16[16,8,640]{2,1,0:T(8,128)(2,1)S(1)} async-done(((bf16[16,8,640]{2,1,0:T(8,128)(2,1)}), bf16[16,8,640]{2,1,0:T(8,128)(2,1)S(1)}, u32[]{:S(2)}, u32[]{:S(2)}) %all-to-all-start.3) | async-done | bytes 163872 | tf_op jit(solution)/shard_map/all_to_all | solution.py:544
  132.8 0.1 copy.13
  132.9 0.7 convert_element_type.36
  (4 shorter events, 0.1 us)
Async XLA Ops:
  31.7 2.0 %copy-start.3 = (s32[8,64]{1,0:T(8,128)S(1)}, s32[8,64]{1,0:T(8,128)}, u32[]{:S(2)}) copy-start(s32[8,64]{1,0:T(8,128)} %get-tuple-element.32.meta) | copy-start | bytes 6148
  31.7 2.0 %copy-start.5 = (s32[64]{0:T(128)S(1)}, s32[64]{0:T(128)}, u32[]{:S(2)}) copy-start(s32[64]{0:T(128)} %block_start.1) | copy-start | bytes 772
  31.7 4.0 %copy-start.4 = (s32[8,1024]{1,0:T(8,128)S(1)}, s32[8,1024]{1,0:T(8,128)}, u32[]{:S(2)}) copy-start(s32[8,1024]{1,0:T(8,128)} %get-tuple-element.33.q_pos) | copy-start | bytes 98308
  31.8 4.0 %collective-permute-start = (bf16[16,160,128]{2,1,0:T(8,128)(2,1)S(1)}, bf16[16,160,128]{2,1,0:T(8,128)(2,1)S(1)}, u32[]{:S(2)}, u32[]{:S(2)}) collective-permute-start(bf16[16,160,128]{2,1,0:T(8,128)(2,1)S(1)} %slice.73), channel_id=1, source_target_pairs={{0,16},{16,0},{1,17},{17,1},{2,18},{18,2},{3,19},{19,3},{4,20},{20... | collective-permute-start | bytes 1966088 | tf_op jit(solution)/shard_map/ppermute | solution.py:506
  40.2 5.8 %collective-permute-start.1 = (f32[8,1024]{1,0:T(8,128)S(1)}, f32[8,1024]{1,0:T(8,128)S(1)}, u32[]{:S(2)}, u32[]{:S(2)}) collective-permute-start(f32[8,1024]{1,0:T(8,128)S(1)} %get-tuple-element.41.own_stats), channel_id=1, source_target_pairs={{0,128},{128,0},{256,384},{384,256},{1,129},{129,1},{257,385},{385... | collective-permute-start | bytes 98312 | tf_op jit(solution)/shard_map/ppermute | solution.py:506
  51.6 4.0 %collective-permute-start.2 = (bf16[16,160,128]{2,1,0:T(8,128)(2,1)S(1)}, bf16[16,160,128]{2,1,0:T(8,128)(2,1)S(1)}, u32[]{:S(2)}, u32[]{:S(2)}) collective-permute-start(bf16[16,160,128]{2,1,0:T(8,128)(2,1)S(1)} %get-tuple-element.43), channel_id=1, source_target_pairs={{0,16},{16,0},{1,17},{17,1},{2,18},{18,2},{3,19},{19,3},{4,20},{20... | collective-permute-start | bytes 1966088 | tf_op jit(solution)/shard_map/ppermute | solution.py:506
  55.9 20.5 %copy-start = (bf16[512,512]{1,0:T(8,128)(2,1)S(1)}, bf16[512,512]{1,0:T(8,128)(2,1)}, u32[]{:S(2)}) copy-start(bf16[512,512]{1,0:T(8,128)(2,1)} %wk_ref.1) | copy-start | bytes 1572868
  55.9 20.5 %copy-start.1 = (bf16[512,512]{1,0:T(8,128)(2,1)S(1)}, bf16[512,512]{1,0:T(8,128)(2,1)}, u32[]{:S(2)}) copy-start(bf16[512,512]{1,0:T(8,128)(2,1)} %wv_ref.1) | copy-start | bytes 1572868
  55.9 20.5 %copy-start.2 = (bf16[128,576]{0,1:T(8,128)(2,1)S(1)}, bf16[128,576]{0,1:T(8,128)(2,1)}, u32[]{:S(2)}) copy-start(bf16[128,576]{0,1:T(8,128)(2,1)} %param.9) | copy-start | bytes 442372
  77.9 17.1 %collective-permute-start.3 = (bf16[4,4,16,1024]{3,2,1,0:T(8,128)(2,1)S(1)}, bf16[4,4,16,1024]{3,2,1,0:T(8,128)(2,1)S(1)}, u32[]{:S(2)}, u32[]{:S(2)}) collective-permute-start(bf16[4,4,16,1024]{3,2,1,0:T(8,128)(2,1)S(1)} %get-tuple-element.47), channel_id=1, source_target_pairs={{0,16},{16,0},{1,17},{17,1},{2,18},{18,2},{3,19},{19,3},{4,20},{20... | collective-permute-start | bytes 1572872 | tf_op jit(solution)/shard_map/ppermute | solution.py:506
  79.8 30.6 %all-to-all-start.2 = ((bf16[16,8,640]{2,1,0:T(8,128)(2,1)}), bf16[16,8,640]{2,1,0:T(8,128)(2,1)S(1)}, u32[]{:S(2)}, u32[]{:S(2)}) async-start(bf16[16,8,640]{2,1,0:T(8,128)(2,1)} %bitcast.2), calls=%async_computation.2 | async-start | bytes 327680 | tf_op jit(solution)/shard_map/all_to_all | solution.py:540
  95.3 23.0 %collective-permute-start.4 = (bf16[4,16,1024]{2,1,0:T(8,128)(2,1)S(1)}, bf16[4,16,1024]{2,1,0:T(8,128)(2,1)S(1)}, u32[]{:S(2)}, u32[]{:S(2)}) collective-permute-start(bf16[4,16,1024]{2,1,0:T(8,128)(2,1)S(1)} %get-tuple-element.48), channel_id=1, source_target_pairs={{0,96},{32,64},{64,32},{96,0},{1,97},{33,65},{65,33},{97,1},{2,98}... | collective-permute-start | bytes 393224 | tf_op jit(solution)/shard_map/ppermute | solution.py:506
  97.7 20.6 %collective-permute-start.5 = (bf16[4,16,1024]{2,1,0:T(8,128)(2,1)S(1)}, bf16[4,16,1024]{2,1,0:T(8,128)(2,1)S(1)}, u32[]{:S(2)}, u32[]{:S(2)}) collective-permute-start(bf16[4,16,1024]{2,1,0:T(8,128)(2,1)S(1)} %get-tuple-element.50), channel_id=1, source_target_pairs={{0,64},{32,96},{64,0},{96,32},{1,65},{33,97},{65,1},{97,33},{2,66}... | collective-permute-start | bytes 393224 | tf_op jit(solution)/shard_map/ppermute | solution.py:506
  101.7 16.5 %collective-permute-start.6 = (bf16[4,16,1024]{2,1,0:T(8,128)(2,1)S(1)}, bf16[4,16,1024]{2,1,0:T(8,128)(2,1)S(1)}, u32[]{:S(2)}, u32[]{:S(2)}) collective-permute-start(bf16[4,16,1024]{2,1,0:T(8,128)(2,1)S(1)} %get-tuple-element.49), channel_id=1, source_target_pairs={{0,32},{32,0},{64,96},{96,64},{1,33},{33,1},{65,97},{97,65},{2,34}... | collective-permute-start | bytes 393224 | tf_op jit(solution)/shard_map/ppermute | solution.py:506
  111.3 21.5 %all-to-all-start.3 = ((bf16[16,8,640]{2,1,0:T(8,128)(2,1)}), bf16[16,8,640]{2,1,0:T(8,128)(2,1)S(1)}, u32[]{:S(2)}, u32[]{:S(2)}) async-start(bf16[16,8,640]{2,1,0:T(8,128)(2,1)} %shard_map.98), calls=%async_computation.3 | async-start | bytes 327680 | tf_op jit(solution)/shard_map/all_to_all | solution.py:544
  118.3 9.8 %collective-permute-start.7 = (bf16[16,1024]{1,0:T(8,128)(2,1)S(1)}, bf16[16,1024]{1,0:T(8,128)(2,1)S(1)}, u32[]{:S(2)}, u32[]{:S(2)}) collective-permute-start(bf16[16,1024]{1,0:T(8,128)(2,1)S(1)} %get-tuple-element.51), channel_id=1, source_target_pairs={{0,384},{128,256},{256,128},{384,0},{1,385},{129,257},{257,129},{3... | collective-permute-start | bytes 98312 | tf_op jit(solution)/shard_map/ppermute | solution.py:506
  121.1 7.3 %collective-permute-start.8 = (bf16[16,1024]{1,0:T(8,128)(2,1)S(1)}, bf16[16,1024]{1,0:T(8,128)(2,1)S(1)}, u32[]{:S(2)}, u32[]{:S(2)}) collective-permute-start(bf16[16,1024]{1,0:T(8,128)(2,1)S(1)} %get-tuple-element.53), channel_id=1, source_target_pairs={{0,256},{128,384},{256,0},{384,128},{1,257},{129,385},{257,1},{385... | collective-permute-start | bytes 98312 | tf_op jit(solution)/shard_map/ppermute | solution.py:506
  123.6 6.5 %collective-permute-start.9 = (bf16[16,1024]{1,0:T(8,128)(2,1)S(1)}, bf16[16,1024]{1,0:T(8,128)(2,1)S(1)}, u32[]{:S(2)}, u32[]{:S(2)}) collective-permute-start(bf16[16,1024]{1,0:T(8,128)(2,1)S(1)} %get-tuple-element.52), channel_id=1, source_target_pairs={{0,128},{128,0},{256,384},{384,256},{1,129},{129,1},{257,385},{385... | collective-permute-start | bytes 98312 | tf_op jit(solution)/shard_map/ppermute | solution.py:506

commit v8 on v7

--- a/solution.py
+++ b/solution.py
@@ -113,7 +113,7 @@
         pltpu.make_async_copy(source, target, sems.at[index])
         for index, (source, target) in enumerate(pairs)
     ]
-    for copy in copies:
+    for copy in reversed(copies):
         copy.start()
     list_blocks(block_start, meta, q_pos)
     copies[0].wait()

time: 134 us -> 134 us (level)
  no operation moved by 1% of the time
where the time goes in v8:
time: 134 us; the launch traced here: 133 us
  starting transfers between devices  49.5 us (37%)
  blocking collectives  47.8 us (36%)
  Pallas kernels  16.4 us (12%)
  waiting for transfers between devices  16.1 us (12%)
    all_to_all x2, blocking collectives, over_chips(): return lax.all_to_all(slots, ('y', 'x'), 0, 0)  47.8 us
    ppermute x10, starting transfers between devices, swap(): lax.ppermute(array, axis, [(i, i ^ bit) for i in range(lax.axis_size(axis...  27.3 us
    all_to_all x1, starting transfers between devices, local(): lax.all_to_all(z_part.reshape(z_size, z_rows, Z_WIDTH), 'head', 0, 0)  15.2 us
    ppermute x10, waiting for transfers between devices, swap(): lax.ppermute(array, axis, [(i, i ^ bit) for i in range(lax.axis_size(axis...  8.93 us
    all_to_all x1, starting transfers between devices, local(): all_rows = lax.all_to_all(rows, 'head', 0, 0).reshape(ROWS, Z_WIDTH)  6.95 us
    all_to_all x1, waiting for transfers between devices, local(): lax.all_to_all(z_part.reshape(z_size, z_rows, Z_WIDTH), 'head', 0, 0)  5.11 us
    pallas_call x1, Pallas kernels, run_gradient(): call(gradient_kernel, [((CHIPS, OUT_ROWS, NOPE), bf16), ((CHIPS, KEY_ROWS...  4.96 us
    pallas_call x1, Pallas kernels, run_pack(): call(pack_kernel, [((CHIPS, IN_ROWS, NOPE), bf16), ((8, BLOCKS), jnp.int3...  4.4 us
  transfers between devices with their start and end apart: 12, of which 7 were waited for; matrix products, arithmetic and copies ran while one was open for 1% of the time, Pallas kernels for 1%

profile of v8, /device:TPU:32, one launch (start us, length us, event | category | flops | bytes accessed | tf_op | source)
XLA Modules:
  0.0 133.1 jit_solution(5072120631769782654)
XLA Ops:
  0.6 4.4 %shard_map.93 = (bf16[16,320,128]{2,1,0:T(8,128)(2,1)}, s32[8,64]{1,0:T(8,128)}, s32[8,1024]{1,0:T(8,128)}) custom-call(s32[1,64]{1,0:T(1,128)} %bitcast.29, bf16[576,128]{1,0:T(8,128)(2,1)} %bitcast.27, bf16[512,512]{1,0:T(8,128)(2,1)} %wk_ref.1, bf16[512,512]{1,0:T(8,128)(2,1)} %wv_ref.1, bf16[128,768]{1,0:T(8,128)(2,1)} %q_any.1, bf16[128,512]{1,0:T(8,128)(2,1)} %g_any.1), custom_call_target="tpu_custom_call" | custom-call | tf_op jit(solution)/shard_map/pallas_call | solution.py:436
  5.0 27.0 %all_to_all.20.own_ref = bf16[16,320,128]{2,1,0:T(8,128)(2,1)S(1)} all-to-all(bf16[16,320,128]{2,1,0:T(8,128)(2,1)} %get-tuple-element.34), channel_id=1, replica_groups=mesh['y'=4,'x'=4,'core'=2,'head'=16] {'y','x'}, dimensions={0} | all-to-all | bytes 2621440 | tf_op jit(solution)/shard_map/all_to_all | solution.py:502
  32.0 0.0 copy-start.3
  32.0 0.0 copy-start.5
  32.0 0.0 copy-start.4
  32.1 1.9 %collective-permute-start = (bf16[16,160,128]{2,1,0:T(8,128)(2,1)S(1)}, bf16[16,160,128]{2,1,0:T(8,128)(2,1)S(1)}, u32[]{:S(2)}, u32[]{:S(2)}) collective-permute-start(bf16[16,160,128]{2,1,0:T(8,128)(2,1)S(1)} %slice.73), channel_id=1, source_target_pairs={{0,16},{16,0},{1,17},{17,1},{2,18},{18,2},{3,19},{19,3},{4,20},{20... | collective-permute-start | bytes 1966088 | tf_op jit(solution)/shard_map/ppermute | solution.py:506
  34.0 0.0 copy-done.3
  34.0 0.0 copy-done.5
  34.0 0.9 shard_map.94
  35.0 1.1 collective-permute-done.other_ref
  36.1 0.0 copy-done.4
  36.1 3.8 %shard_map.95 = (bf16[2048,256]{1,0:T(8,128)(2,1)S(1)}, f32[8,1024]{1,0:T(8,128)S(1)}, f32[2048,1024]{1,0:T(8,128)S(1)}, f32[2048,1024]{1,0:T(8,128)S(1)}) custom-call(s32[8,64]{1,0:T(8,128)S(1)} %copy-done.3, s32[8,1024]{1,0:T(8,128)S(1)} %copy-done.4, bf16[16,320,128]{2,1,0:T(8,128)(2,1)S(1)} %all_to_all.20.own_ref, ...), custom_call_target="tpu_custom_call" | custom-call | tf_op jit(solution)/shard_map/pallas_call | solution.py:471
  39.9 1.9 %collective-permute-start.1 = (f32[8,1024]{1,0:T(8,128)S(1)}, f32[8,1024]{1,0:T(8,128)S(1)}, u32[]{:S(2)}, u32[]{:S(2)}) collective-permute-start(f32[8,1024]{1,0:T(8,128)S(1)} %get-tuple-element.41.own_stats), channel_id=1, source_target_pairs={{0,128},{128,0},{256,384},{384,256},{1,129},{129,1},{257,385},{385... | collective-permute-start | bytes 98312 | tf_op jit(solution)/shard_map/ppermute | solution.py:506
  41.9 3.9 %collective-permute-done.1.other_stats = f32[8,1024]{1,0:T(8,128)S(1)} collective-permute-done((f32[8,1024]{1,0:T(8,128)S(1)}, f32[8,1024]{1,0:T(8,128)S(1)}, u32[]{:S(2)}, u32[]{:S(2)}) %collective-permute-start.1) | collective-permute-done | bytes 32800 | tf_op jit(solution)/shard_map/ppermute | solution.py:506
  45.7 5.0 %shard_map.96 = (bf16[16,256,128]{2,1,0:T(8,128)(2,1)S(1)}, bf16[16,160,128]{2,1,0:T(8,128)(2,1)S(1)}) custom-call(s32[8,64]{1,0:T(8,128)S(1)} %copy-done.3, bf16[2048,256]{1,0:T(8,128)(2,1)S(1)} %get-tuple-element.38.keys, bf16[1024,256]{1,0:T(8,128)(2,1)S(1)} %get-tuple-element.35.queries, bf16[1024,128]{1,0:T(8,128)(2,1)S(1)} %get-tuple-element.36.grads, ...), custom_call_target="tpu_custom_call" | custom-call | tf_op jit(solution)/shard_map/pallas_call | solution.py:486
  50.7 1.9 %collective-permute-start.2 = (bf16[16,160,128]{2,1,0:T(8,128)(2,1)S(1)}, bf16[16,160,128]{2,1,0:T(8,128)(2,1)S(1)}, u32[]{:S(2)}, u32[]{:S(2)}) collective-permute-start(bf16[16,160,128]{2,1,0:T(8,128)(2,1)S(1)} %get-tuple-element.43), channel_id=1, source_target_pairs={{0,16},{16,0},{1,17},{17,1},{2,18},{18,2},{3,19},{19,3},{4,20},{20... | collective-permute-start | bytes 1966088 | tf_op jit(solution)/shard_map/ppermute | solution.py:506
  52.6 2.1 %collective-permute-done.2 = bf16[16,160,128]{2,1,0:T(8,128)(2,1)S(1)} collective-permute-done((bf16[16,160,128]{2,1,0:T(8,128)(2,1)S(1)}, bf16[16,160,128]{2,1,0:T(8,128)(2,1)S(1)}, u32[]{:S(2)}, u32[]{:S(2)}) %collective-permute-start.2) | collective-permute-done | bytes 655392 | tf_op jit(solution)/shard_map/ppermute | solution.py:506
  54.7 0.3 add_dynamic-update-slice_fusion
  55.0 0.0 copy-start
  55.0 0.0 copy-start.1
  55.0 0.0 copy-start.2
  55.0 20.8 %all_to_all.21.slots_ref = bf16[16,256,128]{2,1,0:T(8,128)(2,1)S(1)} all-to-all(bf16[16,256,128]{2,1,0:T(8,128)(2,1)S(1)} %add_dynamic-update-slice_fusion), channel_id=1, replica_groups=mesh['y'=4,'x'=4,'core'=2,'head'=16] {'y','x'}, dimensions={0} | all-to-all | bytes 2097152 | tf_op jit(solution)/shard_map/all_to_all | solution.py:502
  75.8 0.0 copy-done
  75.8 0.0 copy-done.1
  75.8 0.0 copy-done.2
  75.8 1.5 %shard_map.97 = (bf16[128,640]{1,0:T(8,128)(2,1)}, bf16[128,768]{1,0:T(8,128)(2,1)}, bf16[4,4,16,1024]{3,2,1,0:T(8,128)(2,1)S(1)}, bf16[4,4,16,1024]{3,2,1,0:T(8,128)(2,1)S(1)}) custom-call(bf16[16,256,128]{2,1,0:T(8,128)(2,1)S(1)} %all_to_all.21.slots_ref, bf16[512,512]{1,0:T(8,128)(2,1)S(1)} %copy-done, bf16[512,512]{1,0:T(8,128)(2,1)S(1)} %copy-done.1, ...), custom_call_target="tpu_custom_call" | custom-call | tf_op jit(solution)/shard_map/pallas_call | solution.py:526
  77.3 1.9 %collective-permute-start.3 = (bf16[4,4,16,1024]{3,2,1,0:T(8,128)(2,1)S(1)}, bf16[4,4,16,1024]{3,2,1,0:T(8,128)(2,1)S(1)}, u32[]{:S(2)}, u32[]{:S(2)}) collective-permute-start(bf16[4,4,16,1024]{3,2,1,0:T(8,128)(2,1)S(1)} %get-tuple-element.47), channel_id=1, source_target_pairs={{0,16},{16,0},{1,17},{17,1},{2,18},{18,2},{3,19},{19,3},{4,20},{20... | collective-permute-start | bytes 1572872 | tf_op jit(solution)/shard_map/ppermute | solution.py:506
  79.2 15.2 %all-to-all-start.2 = ((bf16[16,8,640]{2,1,0:T(8,128)(2,1)}), bf16[16,8,640]{2,1,0:T(8,128)(2,1)S(1)}, u32[]{:S(2)}, u32[]{:S(2)}) async-start(bf16[16,8,640]{2,1,0:T(8,128)(2,1)} %bitcast.2), calls=%async_computation.2 | async-start | bytes 327680 | tf_op jit(solution)/shard_map/all_to_all | solution.py:540
  94.4 0.0 collective-permute-done.3
  94.4 0.2 add.33
  94.7 2.4 %collective-permute-start.4 = (bf16[4,16,1024]{2,1,0:T(8,128)(2,1)S(1)}, bf16[4,16,1024]{2,1,0:T(8,128)(2,1)S(1)}, u32[]{:S(2)}, u32[]{:S(2)}) collective-permute-start(bf16[4,16,1024]{2,1,0:T(8,128)(2,1)S(1)} %get-tuple-element.48), channel_id=1, source_target_pairs={{0,96},{32,64},{64,32},{96,0},{1,97},{33,65},{65,33},{97,1},{2,98}... | collective-permute-start | bytes 393224 | tf_op jit(solution)/shard_map/ppermute | solution.py:506
  97.0 4.1 %collective-permute-start.5 = (bf16[4,16,1024]{2,1,0:T(8,128)(2,1)S(1)}, bf16[4,16,1024]{2,1,0:T(8,128)(2,1)S(1)}, u32[]{:S(2)}, u32[]{:S(2)}) collective-permute-start(bf16[4,16,1024]{2,1,0:T(8,128)(2,1)S(1)} %get-tuple-element.50), channel_id=1, source_target_pairs={{0,64},{32,96},{64,0},{96,32},{1,65},{33,97},{65,1},{97,33},{2,66}... | collective-permute-start | bytes 393224 | tf_op jit(solution)/shard_map/ppermute | solution.py:506
  101.1 3.4 %collective-permute-start.6 = (bf16[4,16,1024]{2,1,0:T(8,128)(2,1)S(1)}, bf16[4,16,1024]{2,1,0:T(8,128)(2,1)S(1)}, u32[]{:S(2)}, u32[]{:S(2)}) collective-permute-start(bf16[4,16,1024]{2,1,0:T(8,128)(2,1)S(1)} %get-tuple-element.49), channel_id=1, source_target_pairs={{0,32},{32,0},{64,96},{96,64},{1,33},{33,1},{65,97},{97,65},{2,34}... | collective-permute-start | bytes 393224 | tf_op jit(solution)/shard_map/ppermute | solution.py:506
  104.5 0.1 constant_dynamic-slice_fusion
  104.6 0.1 copy.12.kv_ref
  104.7 5.1 %all-to-all-done.2.slots_ref = bf16[16,8,640]{2,1,0:T(8,128)(2,1)S(1)} async-done(((bf16[16,8,640]{2,1,0:T(8,128)(2,1)}), bf16[16,8,640]{2,1,0:T(8,128)(2,1)S(1)}, u32[]{:S(2)}, u32[]{:S(2)}) %all-to-all-start.2) | async-done | bytes 163872 | tf_op jit(solution)/shard_map/all_to_all | solution.py:540
  109.8 0.8 shard_map.98
  110.7 7.0 %all-to-all-start.3 = ((bf16[16,8,640]{2,1,0:T(8,128)(2,1)}), bf16[16,8,640]{2,1,0:T(8,128)(2,1)S(1)}, u32[]{:S(2)}, u32[]{:S(2)}) async-start(bf16[16,8,640]{2,1,0:T(8,128)(2,1)} %shard_map.98), calls=%async_computation.3 | async-start | bytes 327680 | tf_op jit(solution)/shard_map/all_to_all | solution.py:544
  117.6 0.0 collective-permute-done.4
  117.6 0.0 collective-permute-done.5
  117.6 0.0 collective-permute-done.6
  117.7 0.1 fusion.2
  117.7 2.8 %collective-permute-start.7 = (bf16[16,1024]{1,0:T(8,128)(2,1)S(1)}, bf16[16,1024]{1,0:T(8,128)(2,1)S(1)}, u32[]{:S(2)}, u32[]{:S(2)}) collective-permute-start(bf16[16,1024]{1,0:T(8,128)(2,1)S(1)} %get-tuple-element.51), channel_id=1, source_target_pairs={{0,384},{128,256},{256,128},{384,0},{1,385},{129,257},{257,129},{3... | collective-permute-start | bytes 98312 | tf_op jit(solution)/shard_map/ppermute | solution.py:506
  120.5 2.5 %collective-permute-start.8 = (bf16[16,1024]{1,0:T(8,128)(2,1)S(1)}, bf16[16,1024]{1,0:T(8,128)(2,1)S(1)}, u32[]{:S(2)}, u32[]{:S(2)}) collective-permute-start(bf16[16,1024]{1,0:T(8,128)(2,1)S(1)} %get-tuple-element.53), channel_id=1, source_target_pairs={{0,256},{128,384},{256,0},{384,128},{1,257},{129,385},{257,1},{385... | collective-permute-start | bytes 98312 | tf_op jit(solution)/shard_map/ppermute | solution.py:506
  123.0 4.6 %collective-permute-start.9 = (bf16[16,1024]{1,0:T(8,128)(2,1)S(1)}, bf16[16,1024]{1,0:T(8,128)(2,1)S(1)}, u32[]{:S(2)}, u32[]{:S(2)}) collective-permute-start(bf16[16,1024]{1,0:T(8,128)(2,1)S(1)} %get-tuple-element.52), channel_id=1, source_target_pairs={{0,128},{128,0},{256,384},{384,256},{1,129},{129,1},{257,385},{385... | collective-permute-start | bytes 98312 | tf_op jit(solution)/shard_map/ppermute | solution.py:506
  127.6 0.0 collective-permute-done.7
  127.6 0.2 collective-permute-done.8
  127.8 1.6 %collective-permute-done.9 = bf16[16,1024]{1,0:T(8,128)(2,1)S(1)} collective-permute-done((bf16[16,1024]{1,0:T(8,128)(2,1)S(1)}, bf16[16,1024]{1,0:T(8,128)(2,1)S(1)}, u32[]{:S(2)}, u32[]{:S(2)}) %collective-permute-start.9) | collective-permute-done | bytes 32800 | tf_op jit(solution)/shard_map/ppermute | solution.py:506
  129.5 0.6 fusion.5
  130.1 2.0 %all-to-all-done.3 = bf16[16,8,640]{2,1,0:T(8,128)(2,1)S(1)} async-done(((bf16[16,8,640]{2,1,0:T(8,128)(2,1)}), bf16[16,8,640]{2,1,0:T(8,128)(2,1)S(1)}, u32[]{:S(2)}, u32[]{:S(2)}) %all-to-all-start.3) | async-done | bytes 163872 | tf_op jit(solution)/shard_map/all_to_all | solution.py:544
  132.2 0.1 copy.13
  132.3 0.7 convert_element_type.36
  (4 shorter events, 0.1 us)
Async XLA Ops:
  32.0 2.0 %copy-start.3 = (s32[8,64]{1,0:T(8,128)S(1)}, s32[8,64]{1,0:T(8,128)}, u32[]{:S(2)}) copy-start(s32[8,64]{1,0:T(8,128)} %get-tuple-element.32.meta) | copy-start | bytes 6148
  32.0 2.0 %copy-start.5 = (s32[64]{0:T(128)S(1)}, s32[64]{0:T(128)}, u32[]{:S(2)}) copy-start(s32[64]{0:T(128)} %block_start.1) | copy-start | bytes 772
  32.0 4.0 %copy-start.4 = (s32[8,1024]{1,0:T(8,128)S(1)}, s32[8,1024]{1,0:T(8,128)}, u32[]{:S(2)}) copy-start(s32[8,1024]{1,0:T(8,128)} %get-tuple-element.33.q_pos) | copy-start | bytes 98308
  32.1 4.0 %collective-permute-start = (bf16[16,160,128]{2,1,0:T(8,128)(2,1)S(1)}, bf16[16,160,128]{2,1,0:T(8,128)(2,1)S(1)}, u32[]{:S(2)}, u32[]{:S(2)}) collective-permute-start(bf16[16,160,128]{2,1,0:T(8,128)(2,1)S(1)} %slice.73), channel_id=1, source_target_pairs={{0,16},{16,0},{1,17},{17,1},{2,18},{18,2},{3,19},{19,3},{4,20},{20... | collective-permute-start | bytes 1966088 | tf_op jit(solution)/shard_map/ppermute | solution.py:506
  39.9 5.8 %collective-permute-start.1 = (f32[8,1024]{1,0:T(8,128)S(1)}, f32[8,1024]{1,0:T(8,128)S(1)}, u32[]{:S(2)}, u32[]{:S(2)}) collective-permute-start(f32[8,1024]{1,0:T(8,128)S(1)} %get-tuple-element.41.own_stats), channel_id=1, source_target_pairs={{0,128},{128,0},{256,384},{384,256},{1,129},{129,1},{257,385},{385... | collective-permute-start | bytes 98312 | tf_op jit(solution)/shard_map/ppermute | solution.py:506
  50.7 4.0 %collective-permute-start.2 = (bf16[16,160,128]{2,1,0:T(8,128)(2,1)S(1)}, bf16[16,160,128]{2,1,0:T(8,128)(2,1)S(1)}, u32[]{:S(2)}, u32[]{:S(2)}) collective-permute-start(bf16[16,160,128]{2,1,0:T(8,128)(2,1)S(1)} %get-tuple-element.43), channel_id=1, source_target_pairs={{0,16},{16,0},{1,17},{17,1},{2,18},{18,2},{3,19},{19,3},{4,20},{20... | collective-permute-start | bytes 1966088 | tf_op jit(solution)/shard_map/ppermute | solution.py:506
  55.0 20.8 %copy-start = (bf16[512,512]{1,0:T(8,128)(2,1)S(1)}, bf16[512,512]{1,0:T(8,128)(2,1)}, u32[]{:S(2)}) copy-start(bf16[512,512]{1,0:T(8,128)(2,1)} %wk_ref.1) | copy-start | bytes 1572868
  55.0 20.8 %copy-start.1 = (bf16[512,512]{1,0:T(8,128)(2,1)S(1)}, bf16[512,512]{1,0:T(8,128)(2,1)}, u32[]{:S(2)}) copy-start(bf16[512,512]{1,0:T(8,128)(2,1)} %wv_ref.1) | copy-start | bytes 1572868
  55.0 20.8 %copy-start.2 = (bf16[128,576]{0,1:T(8,128)(2,1)S(1)}, bf16[128,576]{0,1:T(8,128)(2,1)}, u32[]{:S(2)}) copy-start(bf16[128,576]{0,1:T(8,128)(2,1)} %param.9) | copy-start | bytes 442372
  77.3 17.1 %collective-permute-start.3 = (bf16[4,4,16,1024]{3,2,1,0:T(8,128)(2,1)S(1)}, bf16[4,4,16,1024]{3,2,1,0:T(8,128)(2,1)S(1)}, u32[]{:S(2)}, u32[]{:S(2)}) collective-permute-start(bf16[4,4,16,1024]{3,2,1,0:T(8,128)(2,1)S(1)} %get-tuple-element.47), channel_id=1, source_target_pairs={{0,16},{16,0},{1,17},{17,1},{2,18},{18,2},{3,19},{19,3},{4,20},{20... | collective-permute-start | bytes 1572872 | tf_op jit(solution)/shard_map/ppermute | solution.py:506
  79.2 30.6 %all-to-all-start.2 = ((bf16[16,8,640]{2,1,0:T(8,128)(2,1)}), bf16[16,8,640]{2,1,0:T(8,128)(2,1)S(1)}, u32[]{:S(2)}, u32[]{:S(2)}) async-start(bf16[16,8,640]{2,1,0:T(8,128)(2,1)} %bitcast.2), calls=%async_computation.2 | async-start | bytes 327680 | tf_op jit(solution)/shard_map/all_to_all | solution.py:540
  94.7 23.0 %collective-permute-start.4 = (bf16[4,16,1024]{2,1,0:T(8,128)(2,1)S(1)}, bf16[4,16,1024]{2,1,0:T(8,128)(2,1)S(1)}, u32[]{:S(2)}, u32[]{:S(2)}) collective-permute-start(bf16[4,16,1024]{2,1,0:T(8,128)(2,1)S(1)} %get-tuple-element.48), channel_id=1, source_target_pairs={{0,96},{32,64},{64,32},{96,0},{1,97},{33,65},{65,33},{97,1},{2,98}... | collective-permute-start | bytes 393224 | tf_op jit(solution)/shard_map/ppermute | solution.py:506
  97.0 20.6 %collective-permute-start.5 = (bf16[4,16,1024]{2,1,0:T(8,128)(2,1)S(1)}, bf16[4,16,1024]{2,1,0:T(8,128)(2,1)S(1)}, u32[]{:S(2)}, u32[]{:S(2)}) collective-permute-start(bf16[4,16,1024]{2,1,0:T(8,128)(2,1)S(1)} %get-tuple-element.50), channel_id=1, source_target_pairs={{0,64},{32,96},{64,0},{96,32},{1,65},{33,97},{65,1},{97,33},{2,66}... | collective-permute-start | bytes 393224 | tf_op jit(solution)/shard_map/ppermute | solution.py:506
  101.1 16.5 %collective-permute-start.6 = (bf16[4,16,1024]{2,1,0:T(8,128)(2,1)S(1)}, bf16[4,16,1024]{2,1,0:T(8,128)(2,1)S(1)}, u32[]{:S(2)}, u32[]{:S(2)}) collective-permute-start(bf16[4,16,1024]{2,1,0:T(8,128)(2,1)S(1)} %get-tuple-element.49), channel_id=1, source_target_pairs={{0,32},{32,0},{64,96},{96,64},{1,33},{33,1},{65,97},{97,65},{2,34}... | collective-permute-start | bytes 393224 | tf_op jit(solution)/shard_map/ppermute | solution.py:506
  110.7 21.5 %all-to-all-start.3 = ((bf16[16,8,640]{2,1,0:T(8,128)(2,1)}), bf16[16,8,640]{2,1,0:T(8,128)(2,1)S(1)}, u32[]{:S(2)}, u32[]{:S(2)}) async-start(bf16[16,8,640]{2,1,0:T(8,128)(2,1)} %shard_map.98), calls=%async_computation.3 | async-start | bytes 327680 | tf_op jit(solution)/shard_map/all_to_all | solution.py:544
  117.7 9.8 %collective-permute-start.7 = (bf16[16,1024]{1,0:T(8,128)(2,1)S(1)}, bf16[16,1024]{1,0:T(8,128)(2,1)S(1)}, u32[]{:S(2)}, u32[]{:S(2)}) collective-permute-start(bf16[16,1024]{1,0:T(8,128)(2,1)S(1)} %get-tuple-element.51), channel_id=1, source_target_pairs={{0,384},{128,256},{256,128},{384,0},{1,385},{129,257},{257,129},{3... | collective-permute-start | bytes 98312 | tf_op jit(solution)/shard_map/ppermute | solution.py:506
  120.5 7.3 %collective-permute-start.8 = (bf16[16,1024]{1,0:T(8,128)(2,1)S(1)}, bf16[16,1024]{1,0:T(8,128)(2,1)S(1)}, u32[]{:S(2)}, u32[]{:S(2)}) collective-permute-start(bf16[16,1024]{1,0:T(8,128)(2,1)S(1)} %get-tuple-element.53), channel_id=1, source_target_pairs={{0,256},{128,384},{256,0},{384,128},{1,257},{129,385},{257,1},{385... | collective-permute-start | bytes 98312 | tf_op jit(solution)/shard_map/ppermute | solution.py:506
  123.0 6.5 %collective-permute-start.9 = (bf16[16,1024]{1,0:T(8,128)(2,1)S(1)}, bf16[16,1024]{1,0:T(8,128)(2,1)S(1)}, u32[]{:S(2)}, u32[]{:S(2)}) collective-permute-start(bf16[16,1024]{1,0:T(8,128)(2,1)S(1)} %get-tuple-element.52), channel_id=1, source_target_pairs={{0,128},{128,0},{256,384},{384,256},{1,129},{129,1},{257,385},{385... | collective-permute-start | bytes 98312 | tf_op jit(solution)/shard_map/ppermute | solution.py:506
